TPU v7x, 32 devices: a whole 2x2x4 slice. The times are simulated.
32 devices in a mesh: dp: 4 (over y, x), expert: 8 (over z, core).
Axes of the slice: x: 2, y: 2, z: 4, core: 2. Of those that a mesh axis runs over, the one named last changes fastest.
Arguments:
- tokens: bfloat16 [4096, 2048], P(('dp', 'expert')), may hold values from -6 to 6
- routes: int32 [4096, 2], P(('dp', 'expert')), may hold values from 0 to 7, all different within a row; in each aligned block of 128 rows (0 to 127, 128 to 255, ...) at most 36 rows name the same one
- gates: int32 [4096, 2], P(('dp', 'expert')), may hold values from 1 to 1023
- cotangent: bfloat16 [4096, 2048], P(('dp', 'expert')), may hold values from -6 to 6
- w_gate: bfloat16 [2048, 8192], P(None, 'expert'), may hold values from -0.125 to 0.125
- w_up: bfloat16 [2048, 8192], P(None, 'expert'), may hold values from -0.125 to 0.125
- w_down: bfloat16 [8192, 2048], P('expert'), may hold values from -0.1875 to 0.1875
Outputs:
- mixed: bfloat16 [4096, 2048], P(('dp', 'expert'))
- input_grad: bfloat16 [4096, 2048], P(('dp', 'expert'))
- grad_gate: float32 [2048, 8192], P('dp', 'expert')
- grad_up: float32 [2048, 8192], P('dp', 'expert')
- grad_down: float32 [8192, 2048], P('expert', 'dp')
Inputs may be any that keep to these rules, and one draw needn't show every extreme that they name: `routes`: the two experts of a token differ. In the rows of one device no expert is named by more than 36 pairs, a bound that some block reaches.
All inputs are finite; a program needn't handle non-finite values.
Results may differ from a plain program's by a relative error of at most 0.0064.
Values may be sent and summed in bfloat16 or wider, within the bound.
No kernel may reach another device: no remote copies, remote signals or barrier semaphores. Data moves between devices by JAX's collectives and lax.ppermute only.
A program may use at most 128 MiB of HBM per device.

v0:
```python
import jax
import jax.numpy as jnp
from jax import lax
from jax.sharding import PartitionSpec as P

EXPERTS = 8
CAP = 36


def slot_table(pairs):
    count = pairs.shape[0]
    onehot = (pairs[:, None] == jnp.arange(EXPERTS, dtype=jnp.int32)[None, :]).astype(jnp.int32)
    before = jnp.cumsum(onehot, axis=0) - onehot
    position = jnp.sum(before * onehot, axis=1)
    table = jnp.full((EXPERTS * CAP,), count, jnp.int32)
    table = table.at[pairs * CAP + position].set(jnp.arange(count, dtype=jnp.int32))
    return (position, table)


def contract_rows(left, right):
    return lax.dot_general(
        left, right, (((0,), (0,)), ((), ())), preferred_element_type=jnp.float32
    )


def contract_cols(left, right):
    return lax.dot_general(
        left, right, (((1,), (1,)), ((), ())), preferred_element_type=jnp.float32
    )


def per_device(tokens, routes, gates, cotangent, w_gate, w_up, w_down):
    tok_dev, width = tokens.shape
    devices = lax.axis_size("expert")
    tiles = devices // EXPERTS
    slots = devices * CAP
    hidden = w_gate.shape[1]
    pairs = routes.reshape(-1)
    position, table = slot_table(pairs)
    send_index = jnp.broadcast_to(table.reshape(EXPERTS, 1, CAP), (EXPERTS, tiles, CAP)).reshape(-1)
    zero_row = jnp.zeros((1, width), jnp.bfloat16)
    factor = gates.reshape(-1).astype(jnp.float32) / 1024.0
    factor_pad = jnp.concatenate([factor, jnp.zeros((1,), jnp.float32)])
    padded_x = jnp.concatenate([tokens, zero_row])
    padded_dy = jnp.concatenate([cotangent, zero_row])
    x_send = jnp.take(padded_x, send_index // 2, axis=0).reshape(devices, CAP, width)
    slot_factor = jnp.take(factor_pad, send_index, axis=0)
    dy_rows = jnp.take(padded_dy, send_index // 2, axis=0)
    dz_send = (
        (slot_factor[:, None] * dy_rows.astype(jnp.float32))
        .astype(jnp.bfloat16)
        .reshape(devices, CAP, width)
    )
    w_both = jnp.concatenate([w_gate, w_up], axis=1)
    x_recv = lax.all_to_all(x_send, "expert", split_axis=0, concat_axis=0, tiled=True)
    forward_xrows = x_recv.reshape(slots, width)
    joined = jnp.dot(forward_xrows, w_both, preferred_element_type=jnp.float32)
    a = joined[:, :hidden]
    b = joined[:, hidden:]
    sig = jax.nn.sigmoid(a)
    act = a * sig
    forward_h = (act * b).astype(jnp.bfloat16)
    z = jnp.dot(forward_h, w_down, preferred_element_type=jnp.float32).astype(jnp.bfloat16)
    xrows, a, b, sig, act, h, z = (
        forward_xrows,
        a,
        b,
        sig,
        act,
        forward_h,
        z.reshape(devices, CAP, width),
    )
    z_back = lax.all_to_all(z, "expert", split_axis=0, concat_axis=0, tiled=True)
    dz_recv = lax.all_to_all(dz_send, "expert", split_axis=0, concat_axis=0, tiled=True)
    backward_dz = dz_recv.reshape(slots, width)
    dh = contract_cols(backward_dz, w_down)
    dsilu = sig * (1.0 + a * (1.0 - sig))
    d_gate = (dh * b * dsilu).astype(jnp.bfloat16)
    d_up = (dh * act).astype(jnp.bfloat16)
    backward_both_grads = jnp.concatenate([d_gate, d_up], axis=1)
    dx = contract_cols(backward_both_grads, w_both).astype(jnp.bfloat16)
    dz, both_grads, dx = (backward_dz, backward_both_grads, dx.reshape(devices, CAP, width))
    dx_back = lax.all_to_all(dx, "expert", split_axis=0, concat_axis=0, tiled=True)
    pair_slot = pairs * CAP + position

    def combine(back):
        summed = jnp.sum(back.reshape(EXPERTS, tiles, CAP, width).astype(jnp.float32), axis=1)
        return jnp.take(summed.reshape(EXPERTS * CAP, width), pair_slot, axis=0)

    mixed = jnp.sum((factor[:, None] * combine(z_back)).reshape(tok_dev, 2, width), axis=1).astype(
        jnp.bfloat16
    )
    input_grad = jnp.sum(combine(dx_back).reshape(tok_dev, 2, width), axis=1).astype(jnp.bfloat16)
    summed = lax.psum_scatter(
        jnp.concatenate([contract_rows(xrows, both_grads), contract_rows(dz, h)], axis=1),
        "dp",
        scatter_dimension=0,
        tiled=True,
    )
    grad_gate = summed[:, :hidden]
    grad_up = summed[:, hidden : 2 * hidden]
    grad_down = summed[:, 2 * hidden :].T
    return (mixed, input_grad, grad_gate, grad_up, grad_down)


def solution(mesh):
    in_specs = (
        P(("dp", "expert"), None),
        P(("dp", "expert"), None),
        P(("dp", "expert"), None),
        P(("dp", "expert"), None),
        P(None, "expert"),
        P(None, "expert"),
        P("expert", None),
    )
    out_specs = (
        P(("dp", "expert"), None),
        P(("dp", "expert"), None),
        P("dp", "expert"),
        P("dp", "expert"),
        P("expert", "dp"),
    )
    return jax.shard_map(
        per_device, mesh=mesh, in_specs=in_specs, out_specs=out_specs, check_vma=False
    )
```

profile of v0, /device:TPU:0, one launch (start us, length us, event | category | flops | bytes accessed | tf_op | source)
XLA Modules:
  0.0 355.6 jit_solution(15242284238534842646)
XLA Ops:
  12.7 2.4 gather_fusion.1
  16.5 6.3 %all-to-all-start = ((bf16[8,36,2048]{2,1,0:T(8,128)(2,1)}), bf16[8,36,2048]{2,1,0:T(8,128)(2,1)S(1)}, u32[]{:S(2)}, u32[]{:S(2)}) async-start(bf16[8,36,2048]{2,1,0:T(8,128)(2,1)} %reshape.130), calls=%async_computation | async-start | bytes 2621440 | tf_op jit(solution)/shard_map/all_to_all | solution.py:55
  23.2 3.0 gather_fusion.3
  26.2 2.4 gather_fusion
  28.6 1.6 multiply_convert_fusion
  31.4 23.6 %all-to-all-done = bf16[8,36,2048]{2,1,0:T(8,128)(2,1)S(1)} async-done(((bf16[8,36,2048]{2,1,0:T(8,128)(2,1)}), bf16[8,36,2048]{2,1,0:T(8,128)(2,1)S(1)}, u32[]{:S(2)}, u32[]{:S(2)}) %all-to-all-start) | async-done | bytes 1179680 | tf_op jit(solution)/shard_map/all_to_all | solution.py:55
  55.1 4.3 %all-to-all-start.2 = ((bf16[8,36,2048]{2,1,0:T(8,128)(2,1)}), bf16[8,36,2048]{2,1,0:T(8,128)(2,1)}, u32[]{:S(2)}, u32[]{:S(2)}) async-start(bf16[8,36,2048]{2,1,0:T(8,128)(2,1)} %reshape.136), calls=%async_computation.2 | async-start | bytes 2621440 | tf_op jit(solution)/shard_map/all_to_all | solution.py:74
  59.6 4.8 %constant_dynamic-update-slice_fusion.1 = bf16[2048,2048]{1,0:T(8,128)(2,1)} fusion(bf16[2048,1024]{1,0:T(8,128)(2,1)} %param.15), kind=kLoop, calls=%fused_computation.34 | loop fusion | bytes 8388608
  64.4 2.5 constant_dynamic-update-slice_fusion
  67.2 7.4 %fusion.11 = f32[288,2048]{1,0:T(8,128)} fusion(bf16[288,2048]{1,0:T(8,128)(2,1)S(1)} %reshape.131, bf16[2048,2048]{1,0:T(8,128)(2,1)} %constant_dynamic-update-slice_fusion), kind=kOutput, calls=%fused_computation.54 | convolution fusion | flops 2415919104 | bytes 11927552 | tf_op jit(solution)/shard_map/dot_general | solution.py:57
  74.6 17.0 %all-to-all-done.2 = bf16[8,36,2048]{2,1,0:T(8,128)(2,1)} async-done(((bf16[8,36,2048]{2,1,0:T(8,128)(2,1)}), bf16[8,36,2048]{2,1,0:T(8,128)(2,1)}, u32[]{:S(2)}, u32[]{:S(2)}) %all-to-all-start.2) | async-done | bytes 1179680 | tf_op jit(solution)/shard_map/all_to_all | solution.py:74
  93.0 4.6 %multiply_convert_fusion.2 = (bf16[288,1024]{1,0:T(8,128)(2,1)S(1)}, bf16[288,1024]{1,0:T(8,128)(2,1)S(1)}, bf16[288,1024]{1,0:T(8,128)(2,1)S(1)}) fusion(f32[288,2048]{1,0:T(8,128)} %fusion.11, bf16[288,2048]{1,0:T(8,128)(2,1)S(1)} %reshape.137, bf16[1024,2048]{1,0:T(8,128)(2,1)} %param.17), kind=kOutput, calls=%fused_computation.14 | convolution fusion | flops 1212383232 | bytes 9502720 | tf_op jit(solution)/shard_map/dot_general | solution.py:27
  97.6 2.4 fusion.12
  100.1 4.6 %fusion.1 = f32[2048,2048]{0,1:T(8,128)S(1)} fusion(bf16[288,2048]{1,0:T(8,128)(2,1)S(1)} %reshape.131, bf16[288,1024]{1,0:T(8,128)(2,1)S(1)} %get-tuple-element.25, bf16[288,1024]{1,0:T(8,128)(2,1)S(1)} %get-tuple-element.24), kind=kOutput, calls=%fused_computation.20 | convolution fusion | flops 2418278400 | bytes 19136512 | tf_op jit(solution)/shard_map/dot_general | solution.py:21
  104.7 12.8 %pad_maximum_fusion = f32[2048,3072]{0,1:T(8,128)} fusion(f32[2048,1024]{0,1:T(8,128)S(1)} %fusion.12, f32[2048,2048]{0,1:T(8,128)S(1)} %fusion.1), kind=kLoop, calls=%fused_computation.6 | loop fusion | flops 6291456 | bytes 50331648 | tf_op jit(solution)/shard_map/concatenate | solution.py:95
  118.8 6.0 %convolution_convert_fusion = bf16[288,2048]{1,0:T(8,128)(2,1)S(1)} fusion(bf16[2048,2048]{1,0:T(8,128)(2,1)} %constant_dynamic-update-slice_fusion, bf16[288,1024]{1,0:T(8,128)(2,1)S(1)} %copy-done.6, bf16[288,1024]{1,0:T(8,128)(2,1)S(1)} %copy-done.4), kind=kOutput, calls=%fused_computation.7 | convolution fusion | flops 2418868224 | bytes 10747904 | tf_op jit(solution)/shard_map/dot_general | solution.py:27
  126.0 3.6 %all-to-all-start.3 = ((bf16[8,36,2048]{2,1,0:T(8,128)(2,1)}), bf16[8,36,2048]{2,1,0:T(8,128)(2,1)S(1)}, u32[]{:S(2)}, u32[]{:S(2)}) async-start(bf16[8,36,2048]{2,1,0:T(8,128)(2,1)} %reshape.138), calls=%async_computation.3 | async-start | bytes 2621440 | tf_op jit(solution)/shard_map/all_to_all | solution.py:83
  129.6 3.9 %convolution_convert_fusion.1 = bf16[288,2048]{1,0:T(8,128)(2,1)S(1)} fusion(bf16[288,1024]{1,0:T(8,128)(2,1)S(1)} %get-tuple-element.26, bf16[1024,2048]{1,0:T(8,128)(2,1)} %param.17), kind=kOutput, calls=%fused_computation.8 | convolution fusion | flops 1208549376 | bytes 5963776 | tf_op jit(solution)/shard_map/dot_general | solution.py:63
  134.7 27.1 %all-to-all-done.3 = bf16[8,36,2048]{2,1,0:T(8,128)(2,1)S(1)} async-done(((bf16[8,36,2048]{2,1,0:T(8,128)(2,1)}), bf16[8,36,2048]{2,1,0:T(8,128)(2,1)S(1)}, u32[]{:S(2)}, u32[]{:S(2)}) %all-to-all-start.3) | async-done | bytes 1179680 | tf_op jit(solution)/shard_map/all_to_all | solution.py:83
  161.7 4.3 %all-to-all-start.1 = ((bf16[8,36,2048]{2,1,0:T(8,128)(2,1)}), bf16[8,36,2048]{2,1,0:T(8,128)(2,1)}, u32[]{:S(2)}, u32[]{:S(2)}) async-start(bf16[8,36,2048]{2,1,0:T(8,128)(2,1)} %reshape.132), calls=%async_computation.1 | async-start | bytes 2621440 | tf_op jit(solution)/shard_map/all_to_all | solution.py:73
  167.5 2.7 gather_fusion.4
  170.1 28.1 %all-to-all-done.1 = bf16[8,36,2048]{2,1,0:T(8,128)(2,1)} async-done(((bf16[8,36,2048]{2,1,0:T(8,128)(2,1)}), bf16[8,36,2048]{2,1,0:T(8,128)(2,1)}, u32[]{:S(2)}, u32[]{:S(2)}) %all-to-all-start.1) | async-done | bytes 1179680 | tf_op jit(solution)/shard_map/all_to_all | solution.py:73
  199.8 2.7 gather_fusion.2
  202.5 4.3 %broadcast_select_fusion.1 = (f32[256,2048]{1,0:T(8,128)}, f32[256,2048]{1,0:T(8,128)S(1)}) fusion(f32[256,2048]{1,0:T(8,128)} %gather_fusion.4, pred[256]{0:T(512)(128)(4,1)S(1)} %get-tuple-element.17, f32[256,2048]{1,0:T(8,128)} %gather_fusion.2, f32[256]{0:T(256)S(1)} %div.25), kind=kLoop, calls=%fused_computation.19 | loop fusion | flops 1572864 | bytes 8389888 | tf_op jit(solution)/shard_map/jit(_take)/select_n | solution.py:88
  206.8 3.6 %reshape.141 = f32[128,2,2048]{2,1,0:T(2,128)} reshape(f32[256,2048]{1,0:T(8,128)} %get-tuple-element.27) | data formatting | bytes 4194304 | tf_op jit(solution)/shard_map/reshape | solution.py:93
  210.4 2.2 reshape.135
  212.6 5.1 %reduce_sum.40 = bf16[128,2048]{1,0:T(8,128)(2,1)} reduce(f32[128,2,2048]{2,1,0:T(2,128)} %reshape.141, f32[]{:T(128)} %constant.69.clone.1), dimensions={1}, to_apply=%region_5.8 | reduce | flops 262144 | bytes 2621444 | tf_op jit(solution)/shard_map/reduce_sum | solution.py:93
  217.7 3.8 %reduce_sum.34 = bf16[128,2048]{1,0:T(8,128)(2,1)} reduce(f32[128,2,2048]{2,1,0:T(2,128)S(1)} %copy-done, f32[]{:T(128)} %constant.69.clone.1), dimensions={1}, to_apply=%region_4.7 | reduce | flops 262144 | bytes 2621444 | tf_op jit(solution)/shard_map/reduce_sum | solution.py:90
  221.5 117.0 %reduce-scatter.2.cloned.1.call-done = f32[512,3072]{0,1:T(8,128)} async-done(((f32[2048,3072]{0,1:T(8,128)}), f32[512,3072]{0,1:T(8,128)}) %reduce-scatter.2.cloned.1.call-update) | async-done | bytes 6291472 | tf_op jit(solution)/shard_map/reduce_scatter | solution.py:94
  338.5 5.6 %slice_bitcast_fusion = (f32[1024,512]{1,0:T(8,128)}, f32[512,1024]{0,1:T(8,128)}, f32[512,1024]{0,1:T(8,128)S(1)}) fusion(f32[512,3072]{0,1:T(8,128)} %reduce-scatter.2.cloned.1.call-done), kind=kLoop, calls=%fused_computation.10 | loop fusion | bytes 12582912 | tf_op jit(solution)/shard_map/transpose | solution.py:102
  344.1 2.9 copy.19
  346.9 1.8 copy.18
  (56 shorter events, 16.9 us)
Async XLA Ops:
  15.3 7.5 %copy-start.8 = (s32[128,2]{0,1:T(2,128)S(1)}, s32[128,2]{0,1:T(2,128)}, u32[]{:S(2)}) copy-start(s32[128,2]{0,1:T(2,128)} %param.13) | copy-start | bytes 3076
  15.3 7.8 %copy-start.7 = (bf16[128,2048]{1,0:T(8,128)(2,1)S(1)}, bf16[128,2048]{1,0:T(8,128)(2,1)}, u32[]{:S(2)}) copy-start(bf16[128,2048]{1,0:T(8,128)(2,1)} %param.14) | copy-start | bytes 1572868
  16.5 38.5 %all-to-all-start = ((bf16[8,36,2048]{2,1,0:T(8,128)(2,1)}), bf16[8,36,2048]{2,1,0:T(8,128)(2,1)S(1)}, u32[]{:S(2)}, u32[]{:S(2)}) async-start(bf16[8,36,2048]{2,1,0:T(8,128)(2,1)} %reshape.130), calls=%async_computation | async-start | bytes 2621440 | tf_op jit(solution)/shard_map/all_to_all | solution.py:55
  55.1 36.5 %all-to-all-start.2 = ((bf16[8,36,2048]{2,1,0:T(8,128)(2,1)}), bf16[8,36,2048]{2,1,0:T(8,128)(2,1)}, u32[]{:S(2)}, u32[]{:S(2)}) async-start(bf16[8,36,2048]{2,1,0:T(8,128)(2,1)} %reshape.136), calls=%async_computation.2 | async-start | bytes 2621440 | tf_op jit(solution)/shard_map/all_to_all | solution.py:74
  59.3 279.1 %reduce-scatter.2.cloned.1.call-start = ((), (), s32[]{:S(2)}) async-start(), calls=%async_computation.5 | async-start | bytes 31457280 | tf_op jit(solution)/shard_map/reduce_scatter | solution.py:94
  59.6 4.9 %copy-start.2 = (bf16[2048,1024]{1,0:T(8,128)(2,1)S(1)}, bf16[2048,1024]{1,0:T(8,128)(2,1)}, u32[]{:S(2)}) copy-start(bf16[2048,1024]{1,0:T(8,128)(2,1)} %param.16) | copy-start | bytes 12582916
  97.6 2.5 copy-start.3
  97.6 2.4 copy-start.5
  117.6 1.1 copy-start.4
  117.6 1.3 copy-start.6
  126.0 35.7 %all-to-all-start.3 = ((bf16[8,36,2048]{2,1,0:T(8,128)(2,1)}), bf16[8,36,2048]{2,1,0:T(8,128)(2,1)S(1)}, u32[]{:S(2)}, u32[]{:S(2)}) async-start(bf16[8,36,2048]{2,1,0:T(8,128)(2,1)} %reshape.138), calls=%async_computation.3 | async-start | bytes 2621440 | tf_op jit(solution)/shard_map/all_to_all | solution.py:83
  161.7 4.3 %copy-start.1 = (bf16[8,36,2048]{2,1,0:T(8,128)(2,1)}, bf16[8,36,2048]{2,1,0:T(8,128)(2,1)S(1)}, u32[]{:S(2)}) copy-start(bf16[8,36,2048]{2,1,0:T(8,128)(2,1)S(1)} %all-to-all-done.3) | copy-start | bytes 3538948
  161.7 36.5 %all-to-all-start.1 = ((bf16[8,36,2048]{2,1,0:T(8,128)(2,1)}), bf16[8,36,2048]{2,1,0:T(8,128)(2,1)}, u32[]{:S(2)}, u32[]{:S(2)}) async-start(bf16[8,36,2048]{2,1,0:T(8,128)(2,1)} %reshape.132), calls=%async_computation.1 | async-start | bytes 2621440 | tf_op jit(solution)/shard_map/all_to_all | solution.py:73
  212.6 5.1 %copy-start = (f32[128,2,2048]{2,1,0:T(2,128)S(1)}, f32[128,2,2048]{2,1,0:T(2,128)}, u32[]{:S(2)}) copy-start(f32[128,2,2048]{2,1,0:T(2,128)} %reshape.135) | copy-start | bytes 6291460
Sparse Core Ops, SparseCore 0:
  117.7 220.7 reduce-scatter.1
where the time goes:
time: 356 us
  waiting for transfers between devices  213 us (60%)
  local copies, waits for them, and re-layouts  51.6 us (14%)
  other arithmetic  29.3 us (8%)
  matrix products  29 us (8%)
  starting transfers between devices  18.6 us (5%)
  between operations  14.3 us (4%)
    reduce_scatter x1, waiting for transfers between devices, per_device(): lax.psum_scatter(jnp.concatenate([contract_rows(xrows, both_grads), contr...  117 us
    all_to_all x1, waiting for transfers between devices, per_device(): lax.all_to_all(z, 'expert', split_axis=0, concat_axis=0, tiled=True)  28.1 us
    all_to_all x1, waiting for transfers between devices, per_device(): lax.all_to_all(dx, 'expert', split_axis=0, concat_axis=0, tiled=True)  27.1 us
    all_to_all x1, waiting for transfers between devices, per_device(): lax.all_to_all(x_send, 'expert', split_axis=0, concat_axis=0, tiled=True)  23.6 us
    all_to_all x1, waiting for transfers between devices, per_device(): lax.all_to_all(dz_send, 'expert', split_axis=0, concat_axis=0, tiled=True)  17 us
    concatenate x1, other arithmetic, per_device(): jnp.concatenate([contract_rows(xrows, both_grads), contract_rows(dz, h)],...  12.8 us
    unnamed x22, local copies, waits for them, and re-layouts  11.6 us
    dot_general x2, matrix products, contract_cols(): lax.dot_general(left, right, (((1,), (1,)), ((), ())), preferred_element_...  10.6 us
  transfers between devices with their start and end apart: 5, of which 5 were waited for; matrix products, arithmetic and copies ran while one was open for 18% of the time, Pallas kernels for 0%

commit v1 on v0

v1 whole, which is shorter than its diff:
```python
import functools

import jax
import jax.numpy as jnp
from jax import lax
from jax.experimental import pallas as pl
from jax.experimental.pallas import tpu as pltpu
from jax.sharding import PartitionSpec as P

EXPERTS = 8
CAP = 36
PIECE = 2 * CAP
MIB = 1 << 20
VMEM = pl.BlockSpec(memory_space=pltpu.VMEM)


def dot(left, right, dims=((1,), (0,))):
    return lax.dot_general(left, right, (dims, ((), ())), preferred_element_type=jnp.float32)


def params(mib):
    return pltpu.CompilerParams(vmem_limit_bytes=mib * MIB)


def cost(flops, moved):
    return pl.CostEstimate(flops=int(flops), bytes_accessed=int(moved), transcendentals=0)


def partner_expert(k, tiles):
    d = lax.axis_index("expert")
    return (2 * (lax.shift_right_logical(d, 1) ^ k) + (d & 1)) // tiles


def slot_rows(routing, chips, tiles):
    tok = routing.shape[1] // 2
    r0, r1, g0, g1 = (routing[i : i + 1, :] for i in range(4))
    before = (
        lax.broadcasted_iota(jnp.int32, (tok, tok), 0) < lax.broadcasted_iota(jnp.int32, (tok, tok), 1)
    ).astype(jnp.bfloat16)
    lane = lax.broadcasted_iota(jnp.int32, (1, 2 * tok), 1)
    base = jnp.where(lane >= tok, CAP, 0)
    result = []
    for k in range(chips):
        expert = partner_expert(k, tiles)
        first, second = r0 == expert, r1 == expert
        named = (first | second).astype(jnp.float32)
        flags = jnp.broadcast_to(named, (8, 2 * tok)).astype(jnp.bfloat16)
        position = jnp.concatenate(
            [dot(flags[:, :tok], before), dot(flags[:, tok:], before)], axis=1
        )[0:1]
        row = position.astype(jnp.int32) + base + k * PIECE
        gate = jnp.where(first, g0, g1)
        result.append((jnp.where(named > 0, row, -1), gate))
    return result


def dispatch_kernel(chips, tiles, scaled, routing_ref, other_routing_ref, own_ref, other_ref, *out_refs):
    tok, width = own_ref.shape
    routing = jnp.concatenate([routing_ref[...], other_routing_ref[...]], axis=1)
    slots = chips * PIECE
    row_id = lax.broadcasted_iota(jnp.int32, (slots, 2 * tok), 0)
    chosen = jnp.zeros((slots, 2 * tok), jnp.float32)
    factor = jnp.zeros((slots, 2 * tok), jnp.float32)
    for row, gate in slot_rows(routing, chips, tiles):
        hit = row_id == row
        chosen = jnp.where(hit, 1.0, chosen)
        if scaled:
            factor = jnp.where(hit, gate.astype(jnp.float32), factor)
    pick = chosen.astype(jnp.bfloat16)
    if scaled:
        scale = jnp.sum(factor, axis=1, keepdims=True) / 1024.0
    step = min(512, width)
    for col in range(0, width, step):
        rows = jnp.concatenate([own_ref[:, col : col + step], other_ref[:, col : col + step]], axis=0)
        moved = dot(pick, rows)
        if scaled:
            moved = scale * moved
        for k in range(chips):
            out_refs[k][:, col : col + step] = moved[k * PIECE : (k + 1) * PIECE].astype(jnp.bfloat16)


def dispatch(routing, other_routing, own, other, chips, tiles, scaled):
    width = own.shape[1]
    slots = chips * PIECE
    return pl.pallas_call(
        functools.partial(dispatch_kernel, chips, tiles, scaled),
        out_shape=[jax.ShapeDtypeStruct((PIECE, width), jnp.bfloat16)] * chips,
        in_specs=[VMEM] * 4,
        out_specs=[VMEM] * chips,
        compiler_params=params(24),
        cost_estimate=cost(4 * slots * own.shape[0] * width, 4 * (own.size + slots * width)),
        name="dispatch_dz" if scaled else "dispatch_x",
    )(routing, other_routing, own, other)


def combine_kernel(chips, tiles, scaled, routing_ref, other_routing_ref, *refs):
    backs, own_ref, other_ref = refs[:chips], refs[chips], refs[chips + 1]
    tok, width = own_ref.shape
    routing = jnp.concatenate([routing_ref[...], other_routing_ref[...]], axis=1)
    slots = chips * PIECE
    row_id = lax.broadcasted_iota(jnp.int32, (slots, 2 * tok), 0)
    high = jnp.zeros((slots, 2 * tok), jnp.float32)
    low = jnp.zeros((slots, 2 * tok), jnp.float32)
    for row, gate in slot_rows(routing, chips, tiles):
        hit = row_id == row
        if scaled:
            rest = gate & 3
            high = jnp.where(hit, (gate - rest).astype(jnp.float32), high)
            low = jnp.where(hit, rest.astype(jnp.float32), low)
        else:
            high = jnp.where(hit, 1.0, high)
    high = high.astype(jnp.bfloat16)
    low = low.astype(jnp.bfloat16)
    step = min(512, width)
    for col in range(0, width, step):
        rows = jnp.concatenate([back[:, col : col + step] for back in backs], axis=0)
        summed = dot(high, rows, ((0,), (0,)))
        if scaled:
            summed = (summed + dot(low, rows, ((0,), (0,)))) / 1024.0
        own_ref[:, col : col + step] = summed[:tok]
        other_ref[:, col : col + step] = summed[tok:]


def combine(routing, other_routing, backs, tiles, scaled):
    chips = len(backs)
    tok, width = routing.shape[1], backs[0].shape[1]
    return pl.pallas_call(
        functools.partial(combine_kernel, chips, tiles, scaled),
        out_shape=[jax.ShapeDtypeStruct((tok, width), jnp.float32)] * 2,
        in_specs=[VMEM] * (2 + chips),
        out_specs=[VMEM] * 2,
        compiler_params=params(24),
        cost_estimate=cost(4 * chips * PIECE * tok * width, 2 * chips * PIECE * width + 8 * tok * width),
        name="combine_mixed" if scaled else "combine_grad",
    )(routing, other_routing, *backs)


def forward_kernel(n, groups, *refs):
    pieces, (wg, wu, wd) = refs[:n], refs[n : n + 3]
    zs, a_ref, b_ref = refs[n + 3 : 2 * n + 3], refs[2 * n + 3], refs[2 * n + 4]
    sends = refs[2 * n + 5 : 2 * n + 5 + groups]
    x, total = refs[2 * n + 5 + groups :]
    step, last = pl.program_id(0), pl.num_programs(0) - 1
    share = x.shape[1] // groups
    tile = wg.shape[1]

    @pl.when(step == 0)
    def _():
        x[...] = jnp.concatenate([piece[...] for piece in pieces], axis=0)
        me = lax.axis_index("dp")
        for k in range(groups):
            start = pl.multiple_of((me ^ k) * share, share)
            sends[k][:, :share] = x[:, pl.ds(start, share)]

    a = dot(x[...], wg[...])
    b = dot(x[...], wu[...])
    h = (a * jax.nn.sigmoid(a) * b).astype(jnp.bfloat16)
    a_ref[...] = a
    b_ref[...] = b
    column = pl.multiple_of(share + step * tile, 128)
    for k in range(groups):
        sends[k][:, pl.ds(column, tile)] = h
    part = dot(h, wd[...])

    @pl.when(step == 0)
    def _():
        total[...] = part

    @pl.when(step > 0)
    def _():
        total[...] += part

    @pl.when(step == last)
    def _():
        for i in range(n):
            zs[i][...] = total[i * PIECE : (i + 1) * PIECE].astype(jnp.bfloat16)


def backward_kernel(n, groups, *refs):
    pieces, (a_ref, b_ref, wg, wu, wd) = refs[:n], refs[n : n + 5]
    dxs = refs[n + 5 : 2 * n + 5]
    sends = refs[2 * n + 5 : 2 * n + 5 + groups]
    dz, total = refs[2 * n + 5 + groups :]
    step, last = pl.program_id(0), pl.num_programs(0) - 1
    share = dz.shape[1] // groups
    tile = wg.shape[1]
    hidden = (sends[0].shape[1] - share) // 2

    @pl.when(step == 0)
    def _():
        dz[...] = jnp.concatenate([piece[...] for piece in pieces], axis=0)
        me = lax.axis_index("dp")
        for k in range(groups):
            start = pl.multiple_of((me ^ k) * share, share)
            sends[k][:, :share] = dz[:, pl.ds(start, share)]

    dh = dot(dz[...], wd[...], ((1,), (1,)))
    a, b = a_ref[...], b_ref[...]
    sig = jax.nn.sigmoid(a)
    d_gate = (dh * b * (sig * (1.0 + a * (1.0 - sig)))).astype(jnp.bfloat16)
    d_up = (dh * (a * sig)).astype(jnp.bfloat16)
    column = pl.multiple_of(share + step * tile, 128)
    for k in range(groups):
        sends[k][:, pl.ds(column, tile)] = d_gate
        sends[k][:, pl.ds(column + hidden, tile)] = d_up
    part = dot(d_gate, wg[...], ((1,), (1,))) + dot(d_up, wu[...], ((1,), (1,)))

    @pl.when(step == 0)
    def _():
        total[...] = part

    @pl.when(step > 0)
    def _():
        total[...] += part

    @pl.when(step == last)
    def _():
        for i in range(n):
            dxs[i][...] = total[i * PIECE : (i + 1) * PIECE].astype(jnp.bfloat16)


def whole(shape):
    return pl.BlockSpec(shape, lambda i: (0, 0))


def hidden_tile(hidden):
    return 256 if hidden % 256 == 0 else hidden


def forward(pieces, wg, wu, wd, groups):
    n = len(pieces)
    rows, width, hidden = n * PIECE, wg.shape[0], wg.shape[1]
    tile = hidden_tile(hidden)
    share = width // groups
    results = pl.pallas_call(
        functools.partial(forward_kernel, n, groups),
        grid=(hidden // tile,),
        out_shape=[jax.ShapeDtypeStruct((PIECE, width), jnp.bfloat16)] * n
        + [jax.ShapeDtypeStruct((rows, hidden), jnp.float32)] * 2
        + [jax.ShapeDtypeStruct((rows, share + hidden), jnp.bfloat16)] * groups,
        in_specs=[whole((PIECE, width))] * n
        + [pl.BlockSpec((width, tile), lambda i: (0, i))] * 2
        + [pl.BlockSpec((tile, width), lambda i: (i, 0))],
        out_specs=[whole((PIECE, width))] * n
        + [pl.BlockSpec((rows, tile), lambda i: (0, i))] * 2
        + [whole((rows, share + hidden))] * groups,
        scratch_shapes=[pltpu.VMEM((rows, width), jnp.bfloat16), pltpu.VMEM((rows, width), jnp.float32)],
        compiler_params=params(40),
        cost_estimate=cost(6 * rows * width * hidden, 6 * width * hidden + 8 * rows * width),
        name="experts_forward",
    )(*pieces, wg, wu, wd)
    return results[:n], results[n], results[n + 1], results[n + 2 :]


def backward(pieces, a, b, wg, wu, wd, groups):
    n = len(pieces)
    rows, width, hidden = n * PIECE, wg.shape[0], wg.shape[1]
    tile = hidden_tile(hidden)
    share = width // groups
    results = pl.pallas_call(
        functools.partial(backward_kernel, n, groups),
        grid=(hidden // tile,),
        out_shape=[jax.ShapeDtypeStruct((PIECE, width), jnp.bfloat16)] * n
        + [jax.ShapeDtypeStruct((rows, share + 2 * hidden), jnp.bfloat16)] * groups,
        in_specs=[whole((PIECE, width))] * n
        + [pl.BlockSpec((rows, tile), lambda i: (0, i))] * 2
        + [pl.BlockSpec((width, tile), lambda i: (0, i))] * 2
        + [pl.BlockSpec((tile, width), lambda i: (i, 0))],
        out_specs=[whole((PIECE, width))] * n + [whole((rows, share + 2 * hidden))] * groups,
        scratch_shapes=[pltpu.VMEM((rows, width), jnp.bfloat16), pltpu.VMEM((rows, width), jnp.float32)],
        compiler_params=params(40),
        cost_estimate=cost(6 * rows * width * hidden, 6 * width * hidden + 8 * rows * width),
        name="experts_backward",
    )(*pieces, a, b, wg, wu, wd)
    return results[:n], results[n:]


def weight_kernel(count, *refs):
    fwd, bwd = refs[:count], refs[count : 2 * count]
    gate_ref, up_ref, down_ref = refs[2 * count : 2 * count + 3]
    share, hidden = gate_ref.shape
    tile = min(256, hidden)
    x = jnp.concatenate([ref[:, :share] for ref in fwd], axis=0)
    dz = jnp.concatenate([ref[:, :share] for ref in bwd], axis=0)
    for col in range(0, hidden, tile):
        lo = share + col
        h = jnp.concatenate([ref[:, lo : lo + tile] for ref in fwd], axis=0)
        d_gate = jnp.concatenate([ref[:, lo : lo + tile] for ref in bwd], axis=0)
        d_up = jnp.concatenate([ref[:, lo + hidden : lo + hidden + tile] for ref in bwd], axis=0)
        gate_ref[:, col : col + tile] = dot(x, d_gate, ((0,), (0,)))
        up_ref[:, col : col + tile] = dot(x, d_up, ((0,), (0,)))
        down_ref[col : col + tile, :] = dot(h, dz, ((0,), (0,)))


def weight_grads(fwd, bwd, share, hidden):
    count = len(fwd)
    rows = sum(f.shape[0] for f in fwd)
    return pl.pallas_call(
        functools.partial(weight_kernel, count),
        out_shape=[jax.ShapeDtypeStruct((share, hidden), jnp.float32)] * 2
        + [jax.ShapeDtypeStruct((hidden, share), jnp.float32)],
        in_specs=[VMEM] * (2 * count),
        out_specs=[VMEM] * 3,
        compiler_params=params(56),
        cost_estimate=cost(6 * rows * share * hidden, 12 * share * hidden + 2 * rows * (2 * share + 3 * hidden)),
        name="weight_grads",
    )(*fwd, *bwd)


def per_device(tokens, routes, gates, cotangent, w_gate, w_up, w_down):
    devices, groups = lax.axis_size("expert"), lax.axis_size("dp")
    chips, tiles = devices // 2, devices // EXPERTS
    width, hidden = w_gate.shape
    share = width // groups

    def swap(v):
        return lax.ppermute(v, "expert", [(i, i ^ 1) for i in range(devices)])

    def over_z(v, k):
        return lax.ppermute(v, "expert", [(i, i ^ (2 * k)) for i in range(devices)]) if k else v

    def over_dp(v, k):
        return lax.ppermute(v, "dp", [(i, i ^ k) for i in range(groups)]) if k else v

    routing = jnp.concatenate([routes.T, gates.T], axis=0)
    other_routing = swap(routing)
    other_tokens = swap(tokens)
    other_cotangent = swap(cotangent)
    x_out = dispatch(routing, other_routing, tokens, other_tokens, chips, tiles, False)
    dz_out = dispatch(routing, other_routing, cotangent, other_cotangent, chips, tiles, True)
    half = chips // 2
    chunks = [list(range(half)), list(range(half, chips))]
    x_in, dz_in = {}, {}
    for k in reversed(range(chips)):
        x_in[k] = over_z(x_out[k], k)
    for k in reversed(range(chips)):
        dz_in[k] = over_z(dz_out[k], k)
    z_back, dx_back, fwd, bwd = {}, {}, [], []
    saved = []
    for chunk in chunks:
        zs, a, b, sends = forward([x_in[k] for k in chunk], w_gate, w_up, w_down, groups)
        saved.append((a, b))
        for k, z in zip(chunk, zs):
            z_back[k] = over_z(z, k)
        fwd += [over_dp(v, k) for k, v in enumerate(sends)]
    for chunk, (a, b) in zip(chunks, saved):
        dxs, sends = backward([dz_in[k] for k in chunk], a, b, w_gate, w_up, w_down, groups)
        for k, dx in zip(chunk, dxs):
            dx_back[k] = over_z(dx, k)
        bwd += [over_dp(v, k) for k, v in enumerate(sends)]

    def finish(back, scaled):
        mine, theirs = combine(routing, other_routing, [back[k] for k in range(chips)], tiles, scaled)
        return (mine + swap(theirs)).astype(jnp.bfloat16)

    mixed = finish(z_back, True)
    input_grad = finish(dx_back, False)
    grad_gate, grad_up, grad_down = weight_grads(fwd, bwd, share, hidden)
    return (mixed, input_grad, grad_gate, grad_up, grad_down)


def solution(mesh):
    rows = P(("dp", "expert"), None)
    in_specs = (rows, rows, rows, rows, P(None, "expert"), P(None, "expert"), P("expert", None))
    out_specs = (rows, rows, P("dp", "expert"), P("dp", "expert"), P("expert", "dp"))
    return jax.shard_map(
        per_device, mesh=mesh, in_specs=in_specs, out_specs=out_specs, check_vma=False
    )
```

time: 356 us -> 212 us (0.60)
  the two profiles are of different devices: /device:TPU:0 before, /device:TPU:16 now
where the time goes in v1:
time: 212 us; the launch traced here: 211 us
  waiting for transfers between devices  117 us (55%)
  Pallas kernels  46.7 us (22%)
  starting transfers between devices  31.7 us (15%)
  local copies, waits for them, and re-layouts  12.5 us (6%)
  other arithmetic  2.53 us (1%)
    ppermute x12, waiting for transfers between devices, over_dp(): lax.ppermute(v, 'dp', [(i, i ^ k) for i in range(groups)])  72.6 us
    ppermute x12, waiting for transfers between devices, over_z(): lax.ppermute(v, 'expert', [(i, i ^ 2 * k) for i in range(devices)])  43.3 us
    pallas_call x2, Pallas kernels, backward(): pl.pallas_call(functools.partial(backward_kernel, n, groups), grid=(hidde...  19.2 us
    ppermute x12, starting transfers between devices, over_dp(): lax.ppermute(v, 'dp', [(i, i ^ k) for i in range(groups)])  16.9 us
    ppermute x12, starting transfers between devices, over_z(): lax.ppermute(v, 'expert', [(i, i ^ 2 * k) for i in range(devices)])  14.1 us
    pallas_call x2, Pallas kernels, forward(): pl.pallas_call(functools.partial(forward_kernel, n, groups), grid=(hidden...  13.2 us
    unnamed x48, local copies, waits for them, and re-layouts  12.5 us
    pallas_call x1, Pallas kernels, weight_grads(): pl.pallas_call(functools.partial(weight_kernel, count), out_shape=[jax.Sh...  10.3 us
  transfers between devices with their start and end apart: 29, of which 12 were waited for; matrix products, arithmetic and copies ran while one was open for 1% of the time, Pallas kernels for 22%

profile of v1, /device:TPU:16, one launch (start us, length us, event | category | flops | bytes accessed | tf_op | source)
XLA Modules:
  0.0 211.5 jit_solution(16788259045143491984)
XLA Ops:
  2.0 1.4 collective-permute-done.other_routing_ref
  5.1 1.6 collective-permute-start.2
  7.0 1.6 collective-permute-start.5
  10.4 2.5 %collective-permute-start.10 = (bf16[72,2048]{1,0:T(8,128)(2,1)S(1)}, bf16[72,2048]{1,0:T(8,128)(2,1)S(1)}, u32[]{:S(2)}, u32[]{:S(2)}) collective-permute-start(bf16[72,2048]{1,0:T(8,128)(2,1)S(1)} %get-tuple-element.59), channel_id=1, source_target_pairs={{0,2},{1,3},{2,0},{3,1},{4,6},{5,7},{6,4},{7,5},{8,10},{9,11},{10,... | collective-permute-start | bytes 884744 | tf_op jit(solution)/shard_map/ppermute | solution.py:320
  12.9 6.2 %collective-permute-done.2.refs_1_ = bf16[72,2048]{1,0:T(8,128)(2,1)S(1)} collective-permute-done((bf16[72,2048]{1,0:T(8,128)(2,1)S(1)}, bf16[72,2048]{1,0:T(8,128)(2,1)S(1)}, u32[]{:S(2)}, u32[]{:S(2)}) %collective-permute-start.2) | collective-permute-done | bytes 294944 | tf_op jit(solution)/shard_map/ppermute | solution.py:320
  19.1 2.2 %copy-done = bf16[2048,1024]{1,0:T(8,128)(2,1)S(1)} copy-done((bf16[2048,1024]{1,0:T(8,128)(2,1)S(1)}, bf16[2048,1024]{1,0:T(8,128)(2,1)}, u32[]{:S(2)}) %copy-start) | copy-done | bytes 4194328
  21.3 2.2 %copy-done.2 = bf16[2048,1024]{1,0:T(8,128)(2,1)S(1)} copy-done((bf16[2048,1024]{1,0:T(8,128)(2,1)S(1)}, bf16[2048,1024]{1,0:T(8,128)(2,1)}, u32[]{:S(2)}) %copy-start.2) | copy-done | bytes 4194328
  23.5 7.1 %experts_forward.2 = (bf16[72,2048]{1,0:T(8,128)(2,1)S(1)}, bf16[72,2048]{1,0:T(8,128)(2,1)}, f32[144,1024]{1,0:T(8,128)S(1)}, f32[144,1024]{1,0:T(8,128)S(1)}, ...) custom-call(bf16[72,2048]{1,0:T(8,128)(2,1)S(1)} %get-tuple-element., ...), custom_call_target="tpu_custom_call" | custom-call | flops 1811939328 | bytes 14942208 | tf_op jit(solution)/shard_map/experts_forward/pallas_call | solution.py:235
  32.2 3.0 %collective-permute-start.3 = (bf16[72,2048]{1,0:T(8,128)(2,1)}, bf16[72,2048]{1,0:T(8,128)(2,1)S(1)}, u32[]{:S(2)}, u32[]{:S(2)}) collective-permute-start(bf16[72,2048]{1,0:T(8,128)(2,1)} %get-tuple-element.51), channel_id=1, source_target_pairs={{0,2},{1,3},{2,0},{3,1},{4,6},{5,7},{6,4},{7,5},{8,10},{9,11},{10,... | collective-permute-start | bytes 884744 | tf_op jit(solution)/shard_map/ppermute | solution.py:320
  35.2 13.0 %collective-permute-done.5.refs_1_ = bf16[72,2048]{1,0:T(8,128)(2,1)S(1)} collective-permute-done((bf16[72,2048]{1,0:T(8,128)(2,1)S(1)}, bf16[72,2048]{1,0:T(8,128)(2,1)S(1)}, u32[]{:S(2)}, u32[]{:S(2)}) %collective-permute-start.5) | collective-permute-done | bytes 294944 | tf_op jit(solution)/shard_map/ppermute | solution.py:320
  48.1 6.1 %experts_forward.3 = (bf16[72,2048]{1,0:T(8,128)(2,1)S(1)}, bf16[72,2048]{1,0:T(8,128)(2,1)S(1)}, f32[144,1024]{1,0:T(8,128)S(1)}, f32[144,1024]{1,0:T(8,128)S(1...) custom-call(bf16[72,2048]{1,0:T(8,128)(2,1)S(1)} %collective-permute, ...), custom_call_target="tpu_custom_call" | custom-call | flops 1811939328 | bytes 14942208 | tf_op jit(solution)/shard_map/experts_forward/pallas_call | solution.py:235
  55.5 9.5 %experts_backward.2 = (bf16[72,2048]{1,0:T(8,128)(2,1)S(1)}, bf16[72,2048]{1,0:T(8,128)(2,1)S(1)}, bf16[144,2560]{1,0:T(8,128)(2,1)S(1)}, bf16[144,2560]{1,0:T(8...) custom-call(bf16[72,2048]{1,0:T(8,128)(2,1)S(1)} %get-tuple-element.58.refs_0_, ...), custom_call_target="tpu_custom_call" | custom-call | flops 1811939328 | bytes 14942208 | tf_op jit(solution)/shard_map/experts_backward/pallas_call | solution.py:260
  65.9 3.9 %collective-permute-start.11 = (bf16[72,2048]{1,0:T(8,128)(2,1)S(1)}, bf16[72,2048]{1,0:T(8,128)(2,1)S(1)}, u32[]{:S(2)}, u32[]{:S(2)}) collective-permute-start(bf16[72,2048]{1,0:T(8,128)(2,1)S(1)} %get-tuple-element.63), channel_id=1, source_target_pairs={{0,2},{1,3},{2,0},{3,1},{4,6},{5,7},{6,4},{7,5},{8,10},{9,11},{10,... | collective-permute-start | bytes 884744 | tf_op jit(solution)/shard_map/ppermute | solution.py:320
  69.8 3.6 %collective-permute-done.13.refs_1_ = bf16[72,2048]{1,0:T(8,128)(2,1)S(1)} collective-permute-done((bf16[72,2048]{1,0:T(8,128)(2,1)S(1)}, bf16[72,2048]{1,0:T(8,128)(2,1)S(1)}, u32[]{:S(2)}, u32[]{:S(2)}) %collective-permute-start.13) | collective-permute-done | bytes 294944 | tf_op jit(solution)/shard_map/ppermute | solution.py:320
  73.4 1.5 collective-permute-start.17
  74.9 9.7 %experts_backward.3 = (bf16[72,2048]{1,0:T(8,128)(2,1)S(1)}, bf16[72,2048]{1,0:T(8,128)(2,1)S(1)}, bf16[144,2560]{1,0:T(8,128)(2,1)S(1)}, bf16[144,2560]{1,0:T(8...) custom-call(bf16[72,2048]{1,0:T(8,128)(2,1)S(1)} %collective-permute-done.12.refs_0_, ...), custom_call_target="tpu_custom_call" | custom-call | flops 1811939328 | bytes 14942208 | tf_op jit(solution)/shard_map/experts_backward/pallas_call | solution.py:260
  85.2 13.5 %collective-permute-done.7.refs_3_ = bf16[72,2048]{1,0:T(8,128)(2,1)S(1)} collective-permute-done((bf16[72,2048]{1,0:T(8,128)(2,1)S(1)}, bf16[72,2048]{1,0:T(8,128)(2,1)S(1)}, u32[]{:S(2)}, u32[]{:S(2)}) %collective-permute-start.7) | collective-permute-done | bytes 294944 | tf_op jit(solution)/shard_map/ppermute | solution.py:320
  98.7 1.5 collective-permute-start.18
  100.3 1.4 collective-permute-start.19
  103.0 1.6 collective-permute-start.23
  104.5 5.7 %collective-permute-done.15.refs_3_ = bf16[72,2048]{1,0:T(8,128)(2,1)S(1)} collective-permute-done((bf16[72,2048]{1,0:T(8,128)(2,1)S(1)}, bf16[72,2048]{1,0:T(8,128)(2,1)S(1)}, u32[]{:S(2)}, u32[]{:S(2)}) %collective-permute-start.15) | collective-permute-done | bytes 294944 | tf_op jit(solution)/shard_map/ppermute | solution.py:320
  110.3 1.5 collective-permute-start.24
  111.8 1.5 collective-permute-start.20
  114.2 1.4 collective-permute-start.22
  115.6 22.9 %collective-permute-done.20.refs_5_ = bf16[144,1536]{1,0:T(8,128)(2,1)S(1)} collective-permute-done((bf16[144,1536]{1,0:T(8,128)(2,1)S(1)}, bf16[144,1536]{1,0:T(8,128)(2,1)S(1)}, u32[]{:S(2)}, u32[]{:S(2)}) %collective-permute-start.20) | collective-permute-done | bytes 442400 | tf_op jit(solution)/shard_map/ppermute | solution.py:323
  138.5 2.5 %collective-permute-start.25 = (bf16[144,2560]{1,0:T(8,128)(2,1)S(1)}, bf16[144,2560]{1,0:T(8,128)(2,1)S(1)}, u32[]{:S(2)}, u32[]{:S(2)}) collective-permute-start(bf16[144,2560]{1,0:T(8,128)(2,1)S(1)} %get-tuple-element.83), channel_id=1, source_target_pairs={{0,24},{8,16},{16,8},{24,0},{1,25},{9,17},{17,9},{25,1},{2,26},{10... | collective-permute-start | bytes 2211848 | tf_op jit(solution)/shard_map/ppermute | solution.py:323
  141.0 22.6 %collective-permute-done.21.refs_6_ = bf16[144,1536]{1,0:T(8,128)(2,1)S(1)} collective-permute-done((bf16[144,1536]{1,0:T(8,128)(2,1)S(1)}, bf16[144,1536]{1,0:T(8,128)(2,1)S(1)}, u32[]{:S(2)}, u32[]{:S(2)}) %collective-permute-start.21) | collective-permute-done | bytes 442400 | tf_op jit(solution)/shard_map/ppermute | solution.py:323
  163.6 1.5 collective-permute-start.26
  167.1 1.6 combine_mixed.1
  171.5 11.6 %collective-permute-done.26.refs_13_ = bf16[144,2560]{1,0:T(8,128)(2,1)S(1)} collective-permute-done((bf16[144,2560]{1,0:T(8,128)(2,1)S(1)}, bf16[144,2560]{1,0:T(8,128)(2,1)S(1)}, u32[]{:S(2)}, u32[]{:S(2)}) %collective-permute-start.26) | collective-permute-done | bytes 737312 | tf_op jit(solution)/shard_map/ppermute | solution.py:323
  183.0 15.1 %collective-permute-done.27.refs_14_ = bf16[144,2560]{1,0:T(8,128)(2,1)S(1)} collective-permute-done((bf16[144,2560]{1,0:T(8,128)(2,1)S(1)}, bf16[144,2560]{1,0:T(8,128)(2,1)S(1)}, u32[]{:S(2)}, u32[]{:S(2)}) %collective-permute-start.27) | collective-permute-done | bytes 737312 | tf_op jit(solution)/shard_map/ppermute | solution.py:323
  199.3 10.3 %weight_grads.1 = (f32[512,1024]{1,0:T(8,128)}, f32[512,1024]{1,0:T(8,128)}, f32[1024,512]{1,0:T(8,128)}) custom-call(bf16[144,1536]{1,0:T(8,128)(2,1)} %copy-done.8, bf16[144,1536]{1,0:T(8,128)(2,1)} %copy-done.18, bf16[144,1536]{1,0:T(8,128)(2,1)} %copy-done.19, bf16[144,1536]{1,0:T(8,128)(2,1)} %copy-done.20, bf16[144,1536]{1,0:T(8,128)(2,1)} %copy-done.9, ...), custom_call_target="tpu_custom_call" | custom-call | flops 3623878656 | bytes 15728640 | tf_op jit(solution)/shard_map/weight_grads/pallas_call | solution.py:298
  (86 shorter events, 19.3 us)
Async XLA Ops:
  0.6 2.7 %collective-permute-start.1 = (bf16[128,2048]{1,0:T(8,128)(2,1)}, bf16[128,2048]{1,0:T(8,128)(2,1)S(1)}, u32[]{:S(2)}, u32[]{:S(2)}) collective-permute-start(bf16[128,2048]{1,0:T(8,128)(2,1)} %own_ref.2), channel_id=1, source_target_pairs={{0,1},{1,0},{2,3},{3,2},{4,5},{5,4},{6,7},{7,6},{8,9},{9,8},{10,11... | collective-permute-start | bytes 1572872 | tf_op jit(solution)/shard_map/ppermute | solution.py:317
  0.7 7.9 %collective-permute-start.9 = (bf16[128,2048]{1,0:T(8,128)(2,1)}, bf16[128,2048]{1,0:T(8,128)(2,1)S(1)}, u32[]{:S(2)}, u32[]{:S(2)}) collective-permute-start(bf16[128,2048]{1,0:T(8,128)(2,1)} %own_ref.3), channel_id=1, source_target_pairs={{0,1},{1,0},{2,3},{3,2},{4,5},{5,4},{6,7},{7,6},{8,9},{9,8},{10,11... | collective-permute-start | bytes 1572872 | tf_op jit(solution)/shard_map/ppermute | solution.py:317
  1.9 1.4 collective-permute-start
  5.1 14.1 %collective-permute-start.2 = (bf16[72,2048]{1,0:T(8,128)(2,1)S(1)}, bf16[72,2048]{1,0:T(8,128)(2,1)S(1)}, u32[]{:S(2)}, u32[]{:S(2)}) collective-permute-start(bf16[72,2048]{1,0:T(8,128)(2,1)S(1)} %get-tuple-element.49), channel_id=1, source_target_pairs={{0,2},{1,3},{2,0},{3,1},{4,6},{5,7},{6,4},{7,5},{8,10},{9,11},{10,... | collective-permute-start | bytes 884744 | tf_op jit(solution)/shard_map/ppermute | solution.py:320
  6.7 25.5 %collective-permute-start.4 = (bf16[72,2048]{1,0:T(8,128)(2,1)S(1)}, bf16[72,2048]{1,0:T(8,128)(2,1)S(1)}, u32[]{:S(2)}, u32[]{:S(2)}) collective-permute-start(bf16[72,2048]{1,0:T(8,128)(2,1)S(1)} %get-tuple-element.52), channel_id=1, source_target_pairs={{0,4},{1,5},{2,6},{3,7},{4,0},{5,1},{6,2},{7,3},{8,12},{9,13},{10,... | collective-permute-start | bytes 884744 | tf_op jit(solution)/shard_map/ppermute | solution.py:320
  7.0 41.1 %collective-permute-start.5 = (bf16[72,2048]{1,0:T(8,128)(2,1)S(1)}, bf16[72,2048]{1,0:T(8,128)(2,1)S(1)}, u32[]{:S(2)}, u32[]{:S(2)}) collective-permute-start(bf16[72,2048]{1,0:T(8,128)(2,1)S(1)} %get-tuple-element.53), channel_id=1, source_target_pairs={{0,6},{1,7},{2,4},{3,5},{4,2},{5,3},{6,0},{7,1},{8,14},{9,15},{10,... | collective-permute-start | bytes 884744 | tf_op jit(solution)/shard_map/ppermute | solution.py:320
  10.4 44.6 %collective-permute-start.10 = (bf16[72,2048]{1,0:T(8,128)(2,1)S(1)}, bf16[72,2048]{1,0:T(8,128)(2,1)S(1)}, u32[]{:S(2)}, u32[]{:S(2)}) collective-permute-start(bf16[72,2048]{1,0:T(8,128)(2,1)S(1)} %get-tuple-element.59), channel_id=1, source_target_pairs={{0,2},{1,3},{2,0},{3,1},{4,6},{5,7},{6,4},{7,5},{8,10},{9,11},{10,... | collective-permute-start | bytes 884744 | tf_op jit(solution)/shard_map/ppermute | solution.py:320
  12.9 52.9 %collective-permute-start.12 = (bf16[72,2048]{1,0:T(8,128)(2,1)S(1)}, bf16[72,2048]{1,0:T(8,128)(2,1)S(1)}, u32[]{:S(2)}, u32[]{:S(2)}) collective-permute-start(bf16[72,2048]{1,0:T(8,128)(2,1)S(1)} %get-tuple-element.64), channel_id=1, source_target_pairs={{0,4},{1,5},{2,6},{3,7},{4,0},{5,1},{6,2},{7,3},{8,12},{9,13},{10,... | collective-permute-start | bytes 884744 | tf_op jit(solution)/shard_map/ppermute | solution.py:320
  19.1 54.3 %collective-permute-start.13 = (bf16[72,2048]{1,0:T(8,128)(2,1)S(1)}, bf16[72,2048]{1,0:T(8,128)(2,1)S(1)}, u32[]{:S(2)}, u32[]{:S(2)}) collective-permute-start(bf16[72,2048]{1,0:T(8,128)(2,1)S(1)} %get-tuple-element.65), channel_id=1, source_target_pairs={{0,6},{1,7},{2,4},{3,5},{4,2},{5,3},{6,0},{7,1},{8,14},{9,15},{10,... | collective-permute-start | bytes 884744 | tf_op jit(solution)/shard_map/ppermute | solution.py:320
  32.2 52.4 %collective-permute-start.3 = (bf16[72,2048]{1,0:T(8,128)(2,1)}, bf16[72,2048]{1,0:T(8,128)(2,1)S(1)}, u32[]{:S(2)}, u32[]{:S(2)}) collective-permute-start(bf16[72,2048]{1,0:T(8,128)(2,1)} %get-tuple-element.51), channel_id=1, source_target_pairs={{0,2},{1,3},{2,0},{3,1},{4,6},{5,7},{6,4},{7,5},{8,10},{9,11},{10,... | collective-permute-start | bytes 884744 | tf_op jit(solution)/shard_map/ppermute | solution.py:320
  55.0 29.7 %collective-permute-start.6 = (bf16[72,2048]{1,0:T(8,128)(2,1)S(1)}, bf16[72,2048]{1,0:T(8,128)(2,1)S(1)}, u32[]{:S(2)}, u32[]{:S(2)}) collective-permute-start(bf16[72,2048]{1,0:T(8,128)(2,1)S(1)} %get-tuple-element.54), channel_id=1, source_target_pairs={{0,4},{1,5},{2,6},{3,7},{4,0},{5,1},{6,2},{7,3},{8,12},{9,13},{10,... | collective-permute-start | bytes 884744 | tf_op jit(solution)/shard_map/ppermute | solution.py:320
  55.0 43.7 %collective-permute-start.7 = (bf16[72,2048]{1,0:T(8,128)(2,1)S(1)}, bf16[72,2048]{1,0:T(8,128)(2,1)S(1)}, u32[]{:S(2)}, u32[]{:S(2)}) collective-permute-start(bf16[72,2048]{1,0:T(8,128)(2,1)S(1)} %get-tuple-element.55), channel_id=1, source_target_pairs={{0,6},{1,7},{2,4},{3,5},{4,2},{5,3},{6,0},{7,1},{8,14},{9,15},{10,... | collective-permute-start | bytes 884744 | tf_op jit(solution)/shard_map/ppermute | solution.py:320
  65.9 34.4 %collective-permute-start.11 = (bf16[72,2048]{1,0:T(8,128)(2,1)S(1)}, bf16[72,2048]{1,0:T(8,128)(2,1)S(1)}, u32[]{:S(2)}, u32[]{:S(2)}) collective-permute-start(bf16[72,2048]{1,0:T(8,128)(2,1)S(1)} %get-tuple-element.63), channel_id=1, source_target_pairs={{0,2},{1,3},{2,0},{3,1},{4,6},{5,7},{6,4},{7,5},{8,10},{9,11},{10,... | collective-permute-start | bytes 884744 | tf_op jit(solution)/shard_map/ppermute | solution.py:320
  73.4 38.4 %collective-permute-start.17 = (bf16[144,1536]{1,0:T(8,128)(2,1)}, bf16[144,1536]{1,0:T(8,128)(2,1)S(1)}, u32[]{:S(2)}, u32[]{:S(2)}) collective-permute-start(bf16[144,1536]{1,0:T(8,128)(2,1)} %get-tuple-element.73), channel_id=1, source_target_pairs={{0,8},{8,0},{16,24},{24,16},{1,9},{9,1},{17,25},{25,17},{2,10},{10... | collective-permute-start | bytes 1327112 | tf_op jit(solution)/shard_map/ppermute | solution.py:323
  84.6 86.9 %copy-start.5 = (bf16[144,2560]{1,0:T(8,128)(2,1)}, bf16[144,2560]{1,0:T(8,128)(2,1)S(1)}, u32[]{:S(2)}) copy-start(bf16[144,2560]{1,0:T(8,128)(2,1)S(1)} %get-tuple-element.84.refs_12_) | copy-start | bytes 2211844
  84.6 18.4 %collective-permute-start.14 = (bf16[72,2048]{1,0:T(8,128)(2,1)S(1)}, bf16[72,2048]{1,0:T(8,128)(2,1)S(1)}, u32[]{:S(2)}, u32[]{:S(2)}) collective-permute-start(bf16[72,2048]{1,0:T(8,128)(2,1)S(1)} %get-tuple-element.68), channel_id=1, source_target_pairs={{0,4},{1,5},{2,6},{3,7},{4,0},{5,1},{6,2},{7,3},{8,12},{9,13},{10,... | collective-permute-start | bytes 884744 | tf_op jit(solution)/shard_map/ppermute | solution.py:320
  84.7 25.6 %collective-permute-start.15 = (bf16[72,2048]{1,0:T(8,128)(2,1)S(1)}, bf16[72,2048]{1,0:T(8,128)(2,1)S(1)}, u32[]{:S(2)}, u32[]{:S(2)}) collective-permute-start(bf16[72,2048]{1,0:T(8,128)(2,1)S(1)} %get-tuple-element.69), channel_id=1, source_target_pairs={{0,6},{1,7},{2,4},{3,5},{4,2},{5,3},{6,0},{7,1},{8,14},{9,15},{10,... | collective-permute-start | bytes 884744 | tf_op jit(solution)/shard_map/ppermute | solution.py:320
  98.7 14.6 %collective-permute-start.18 = (bf16[144,1536]{1,0:T(8,128)(2,1)S(1)}, bf16[144,1536]{1,0:T(8,128)(2,1)S(1)}, u32[]{:S(2)}, u32[]{:S(2)}) collective-permute-start(bf16[144,1536]{1,0:T(8,128)(2,1)S(1)} %copy-done.11), channel_id=1, source_target_pairs={{0,16},{8,24},{16,0},{24,8},{1,17},{9,25},{17,1},{25,9},{2,18},{10... | collective-permute-start | bytes 1327112 | tf_op jit(solution)/shard_map/ppermute | solution.py:323
  100.3 13.9 %collective-permute-start.19 = (bf16[144,1536]{1,0:T(8,128)(2,1)S(1)}, bf16[144,1536]{1,0:T(8,128)(2,1)S(1)}, u32[]{:S(2)}, u32[]{:S(2)}) collective-permute-start(bf16[144,1536]{1,0:T(8,128)(2,1)S(1)} %get-tuple-element.75), channel_id=1, source_target_pairs={{0,24},{8,16},{16,8},{24,0},{1,25},{9,17},{17,9},{25,1},{2,26},{10... | collective-permute-start | bytes 1327112 | tf_op jit(solution)/shard_map/ppermute | solution.py:323
  103.0 63.2 %collective-permute-start.23 = (bf16[144,2560]{1,0:T(8,128)(2,1)S(1)}, bf16[144,2560]{1,0:T(8,128)(2,1)S(1)}, u32[]{:S(2)}, u32[]{:S(2)}) collective-permute-start(bf16[144,2560]{1,0:T(8,128)(2,1)S(1)} %get-tuple-element.81), channel_id=1, source_target_pairs={{0,8},{8,0},{16,24},{24,16},{1,9},{9,1},{17,25},{25,17},{2,10},{10... | collective-permute-start | bytes 2211848 | tf_op jit(solution)/shard_map/ppermute | solution.py:323
  110.3 58.4 %collective-permute-start.24 = (bf16[144,2560]{1,0:T(8,128)(2,1)S(1)}, bf16[144,2560]{1,0:T(8,128)(2,1)S(1)}, u32[]{:S(2)}, u32[]{:S(2)}) collective-permute-start(bf16[144,2560]{1,0:T(8,128)(2,1)S(1)} %get-tuple-element.82), channel_id=1, source_target_pairs={{0,16},{8,24},{16,0},{24,8},{1,17},{9,25},{17,1},{25,9},{2,18},{10... | collective-permute-start | bytes 2211848 | tf_op jit(solution)/shard_map/ppermute | solution.py:323
  111.8 26.7 %collective-permute-start.20 = (bf16[144,1536]{1,0:T(8,128)(2,1)S(1)}, bf16[144,1536]{1,0:T(8,128)(2,1)S(1)}, u32[]{:S(2)}, u32[]{:S(2)}) collective-permute-start(bf16[144,1536]{1,0:T(8,128)(2,1)S(1)} %get-tuple-element.77), channel_id=1, source_target_pairs={{0,8},{8,0},{16,24},{24,16},{1,9},{9,1},{17,25},{25,17},{2,10},{10... | collective-permute-start | bytes 1327112 | tf_op jit(solution)/shard_map/ppermute | solution.py:323
  113.3 86.0 %copy-start.19 = (bf16[144,1536]{1,0:T(8,128)(2,1)}, bf16[144,1536]{1,0:T(8,128)(2,1)S(1)}, u32[]{:S(2)}) copy-start(bf16[144,1536]{1,0:T(8,128)(2,1)S(1)} %collective-permute-done.18.refs_2_) | copy-start | bytes 1327108
  113.3 50.3 %collective-permute-start.21 = (bf16[144,1536]{1,0:T(8,128)(2,1)S(1)}, bf16[144,1536]{1,0:T(8,128)(2,1)S(1)}, u32[]{:S(2)}, u32[]{:S(2)}) collective-permute-start(bf16[144,1536]{1,0:T(8,128)(2,1)S(1)} %get-tuple-element.78), channel_id=1, source_target_pairs={{0,16},{8,24},{16,0},{24,8},{1,17},{9,25},{17,1},{25,9},{2,18},{10... | collective-permute-start | bytes 1327112 | tf_op jit(solution)/shard_map/ppermute | solution.py:323
  114.2 85.1 %copy-start.20 = (bf16[144,1536]{1,0:T(8,128)(2,1)}, bf16[144,1536]{1,0:T(8,128)(2,1)S(1)}, u32[]{:S(2)}) copy-start(bf16[144,1536]{1,0:T(8,128)(2,1)S(1)} %collective-permute-done.19.refs_3_) | copy-start | bytes 1327108
  114.2 50.9 %collective-permute-start.22 = (bf16[144,1536]{1,0:T(8,128)(2,1)S(1)}, bf16[144,1536]{1,0:T(8,128)(2,1)S(1)}, u32[]{:S(2)}, u32[]{:S(2)}) collective-permute-start(bf16[144,1536]{1,0:T(8,128)(2,1)S(1)} %get-tuple-element.79), channel_id=1, source_target_pairs={{0,24},{8,16},{16,8},{24,0},{1,25},{9,17},{17,9},{25,1},{2,26},{10... | collective-permute-start | bytes 1327112 | tf_op jit(solution)/shard_map/ppermute | solution.py:323
  138.5 32.1 %collective-permute-start.25 = (bf16[144,2560]{1,0:T(8,128)(2,1)S(1)}, bf16[144,2560]{1,0:T(8,128)(2,1)S(1)}, u32[]{:S(2)}, u32[]{:S(2)}) collective-permute-start(bf16[144,2560]{1,0:T(8,128)(2,1)S(1)} %get-tuple-element.83), channel_id=1, source_target_pairs={{0,24},{8,16},{16,8},{24,0},{1,25},{9,17},{17,9},{25,1},{2,26},{10... | collective-permute-start | bytes 2211848 | tf_op jit(solution)/shard_map/ppermute | solution.py:323
  163.6 19.4 %collective-permute-start.26 = (bf16[144,2560]{1,0:T(8,128)(2,1)S(1)}, bf16[144,2560]{1,0:T(8,128)(2,1)S(1)}, u32[]{:S(2)}, u32[]{:S(2)}) collective-permute-start(bf16[144,2560]{1,0:T(8,128)(2,1)S(1)} %get-tuple-element.85), channel_id=1, source_target_pairs={{0,8},{8,0},{16,24},{24,16},{1,9},{9,1},{17,25},{25,17},{2,10},{10... | collective-permute-start | bytes 2211848 | tf_op jit(solution)/shard_map/ppermute | solution.py:323
  165.1 33.0 %collective-permute-start.27 = (bf16[144,2560]{1,0:T(8,128)(2,1)S(1)}, bf16[144,2560]{1,0:T(8,128)(2,1)S(1)}, u32[]{:S(2)}, u32[]{:S(2)}) collective-permute-start(bf16[144,2560]{1,0:T(8,128)(2,1)S(1)} %get-tuple-element.86), channel_id=1, source_target_pairs={{0,16},{8,24},{16,0},{24,8},{1,17},{9,25},{17,1},{25,9},{2,18},{10... | collective-permute-start | bytes 2211848 | tf_op jit(solution)/shard_map/ppermute | solution.py:323
  166.1 32.0 %collective-permute-start.28 = (bf16[144,2560]{1,0:T(8,128)(2,1)S(1)}, bf16[144,2560]{1,0:T(8,128)(2,1)S(1)}, u32[]{:S(2)}, u32[]{:S(2)}) collective-permute-start(bf16[144,2560]{1,0:T(8,128)(2,1)S(1)} %get-tuple-element.87), channel_id=1, source_target_pairs={{0,24},{8,16},{16,8},{24,0},{1,25},{9,17},{17,9},{25,1},{2,26},{10... | collective-permute-start | bytes 2211848 | tf_op jit(solution)/shard_map/ppermute | solution.py:323
  168.7 40.9 %collective-permute-start.8 = (f32[128,2048]{1,0:T(8,128)S(1)}, f32[128,2048]{1,0:T(8,128)S(1)}, u32[]{:S(2)}, u32[]{:S(2)}) collective-permute-start(f32[128,2048]{1,0:T(8,128)S(1)} %get-tuple-element.57), channel_id=1, source_target_pairs={{0,1},{1,0},{2,3},{3,2},{4,5},{5,4},{6,7},{7,6},{8,9},{9,8},{10,11... | collective-permute-start | bytes 3145736 | tf_op jit(solution)/shard_map/ppermute | solution.py:317
  171.4 39.1 %collective-permute-start.16 = (f32[128,2048]{1,0:T(8,128)S(1)}, f32[128,2048]{1,0:T(8,128)S(1)}, u32[]{:S(2)}, u32[]{:S(2)}) collective-permute-start(f32[128,2048]{1,0:T(8,128)S(1)} %get-tuple-element.71), channel_id=1, source_target_pairs={{0,1},{1,0},{2,3},{3,2},{4,5},{5,4},{6,7},{7,6},{8,9},{9,8},{10,11... | collective-permute-start | bytes 3145736 | tf_op jit(solution)/shard_map/ppermute | solution.py:317
  (21 other events, 292.1 us)

commit v2 on v1

v2 whole, which is shorter than its diff:
```python
import functools

import jax
import jax.numpy as jnp
from jax import lax
from jax.experimental import pallas as pl
from jax.experimental.pallas import tpu as pltpu
from jax.sharding import PartitionSpec as P

EXPERTS = 8
CAP = 36
PIECE = 2 * CAP
KINDS = ("x", "dz")
MIB = 1 << 20
VMEM = pl.BlockSpec(memory_space=pltpu.VMEM)


def dot(left, right, dims=((1,), (0,))):
    return lax.dot_general(left, right, (dims, ((), ())), preferred_element_type=jnp.float32)


def params(mib):
    return pltpu.CompilerParams(vmem_limit_bytes=mib * MIB)


def cost(flops, moved):
    return pl.CostEstimate(flops=int(flops), bytes_accessed=int(moved), transcendentals=0)


def send_layout(groups, share, part, kinds):
    if groups != 4:
        return [(k, [(kind, k, 0, share) for kind in kinds] + [("part", 0, 0, part)]) for k in range(1, groups)], 0
    half, cut = part // 2, share // 2
    left, right = ("part", 0, 0, half), ("part", 0, half, half)
    over_x = [(kind, 1, 0, share) for kind in kinds] + [right, left] + [(kind, 3, 0, cut) for kind in kinds]
    over_y = [(kind, 2, 0, share) for kind in kinds] + [left, right] + [(kind, 3, cut, cut) for kind in kinds]
    return [(1, over_x), (2, over_y)], half + cut * len(kinds)


def own_fields(share, part, kinds):
    return [(kind, 0, 0, share) for kind in kinds] + [("part", 0, 0, part)]


def all_layouts(groups, share, part, kinds):
    return [own_fields(share, part, kinds)] + [f for _, f in send_layout(groups, share, part, kinds)[0]]


def fields_width(fields):
    return sum(field[3] for field in fields)


def received(groups, share, part, kinds):
    messages, relayed = send_layout(groups, share, part, kinds)
    result = []
    for index, (sent, fields) in enumerate([(0, own_fields(share, part, kinds))] + messages):
        column, found = 0, {}
        for kind, offset, first, count in fields:
            if kind == "part" or offset == sent:
                found.setdefault(kind, []).append((index, column, first, count))
            column += count
        found["part"].sort(key=lambda f: f[2])
        result.append(found)
    if relayed:
        half, cut = part // 2, share // 2
        found = {"part": [(3, 0, 0, half), (4, 0, half, half)]}
        for i, kind in enumerate(kinds):
            found[kind] = [(3, half + i * cut, 0, cut), (4, half + i * cut, cut, cut)]
        result.append(found)
    return result


def store_rows(outs, layouts, want, source, top, share):
    me = lax.axis_index("dp")
    for out, fields in zip(outs, layouts):
        column = 0
        for kind, offset, first, count in fields:
            if kind == want:
                start = pl.multiple_of((me ^ offset) * share + first, 128)
                out[:, column : column + count] = source[top : top + PIECE, pl.ds(start, count)]
            column += count


def store_part(outs, layouts, step, tile, value, base=0):
    for out, fields in zip(outs, layouts):
        column = 0
        for kind, _, first, count in fields:
            if kind == "part":
                at = base + step * tile - first

                @pl.when((at >= 0) & (at < count))
                def _(out=out, column=column, at=at):
                    out[:, pl.ds(pl.multiple_of(column + at, 128), tile)] = value

            column += count


def partner_expert(k, tiles):
    d = lax.axis_index("expert")
    return (2 * (lax.shift_right_logical(d, 1) ^ k) + (d & 1)) // tiles


def slot_rows(routing, chips, tiles):
    tok = routing.shape[1] // 2
    r0, r1, g0, g1 = (routing[i : i + 1, :] for i in range(4))
    before = (
        lax.broadcasted_iota(jnp.int32, (tok, tok), 0) < lax.broadcasted_iota(jnp.int32, (tok, tok), 1)
    ).astype(jnp.bfloat16)
    lane = lax.broadcasted_iota(jnp.int32, (1, 2 * tok), 1)
    base = jnp.where(lane >= tok, CAP, 0)
    result = []
    for k in range(chips):
        expert = partner_expert(k, tiles)
        first, second = r0 == expert, r1 == expert
        named = (first | second).astype(jnp.float32)
        flags = jnp.broadcast_to(named, (8, 2 * tok)).astype(jnp.bfloat16)
        position = jnp.concatenate(
            [dot(flags[:, :tok], before), dot(flags[:, tok:], before)], axis=1
        )[0:1]
        row = position.astype(jnp.int32) + base + k * PIECE
        gate = jnp.where(first, g0, g1)
        result.append((jnp.where(named > 0, row, -1), gate))
    return result


def dispatch_kernel(chips, tiles, routing_ref, other_routing_ref, x_ref, other_x_ref, dy_ref, other_dy_ref, *out_refs):
    tok, width = x_ref.shape
    routing = jnp.concatenate([routing_ref[...], other_routing_ref[...]], axis=1)
    slots = chips * PIECE
    row_id = lax.broadcasted_iota(jnp.int32, (slots, 2 * tok), 0)
    chosen = jnp.zeros((slots, 2 * tok), jnp.float32)
    factor = jnp.zeros((slots, 2 * tok), jnp.float32)
    for row, gate in slot_rows(routing, chips, tiles):
        hit = row_id == row
        chosen = jnp.where(hit, 1.0, chosen)
        factor = jnp.where(hit, gate.astype(jnp.float32), factor)
    pick = chosen.astype(jnp.bfloat16)
    scale = jnp.sum(factor, axis=1, keepdims=True) / 1024.0
    step = min(512, width)
    for col in range(0, width, step):
        columns = slice(col, col + step)
        x = dot(pick, jnp.concatenate([x_ref[:, columns], other_x_ref[:, columns]], axis=0))
        dz = scale * dot(pick, jnp.concatenate([dy_ref[:, columns], other_dy_ref[:, columns]], axis=0))
        for k in range(chips):
            rows = slice(k * PIECE, (k + 1) * PIECE)
            out_refs[k][:, columns] = jnp.concatenate([x[rows], dz[rows]], axis=0).astype(jnp.bfloat16)


def dispatch(routing, other_routing, x, other_x, dy, other_dy, chips, tiles):
    tok, width = x.shape
    slots = chips * PIECE
    return pl.pallas_call(
        functools.partial(dispatch_kernel, chips, tiles),
        out_shape=[jax.ShapeDtypeStruct((2 * PIECE, width), jnp.bfloat16)] * chips,
        in_specs=[VMEM] * 6,
        out_specs=[VMEM] * chips,
        compiler_params=params(24),
        cost_estimate=cost(8 * slots * tok * width, 4 * (2 * x.size + slots * width)),
        name="dispatch",
    )(routing, other_routing, *in_hbm(x), other_x, *in_hbm(dy), other_dy)


def combine_kernel(chips, tiles, scaled, routing_ref, other_routing_ref, *refs):
    backs, own_ref, other_ref = refs[:chips], refs[chips], refs[chips + 1]
    tok, width = own_ref.shape
    routing = jnp.concatenate([routing_ref[...], other_routing_ref[...]], axis=1)
    slots = chips * PIECE
    row_id = lax.broadcasted_iota(jnp.int32, (slots, 2 * tok), 0)
    high = jnp.zeros((slots, 2 * tok), jnp.float32)
    low = jnp.zeros((slots, 2 * tok), jnp.float32)
    for row, gate in slot_rows(routing, chips, tiles):
        hit = row_id == row
        if scaled:
            rest = gate & 3
            high = jnp.where(hit, (gate - rest).astype(jnp.float32), high)
            low = jnp.where(hit, rest.astype(jnp.float32), low)
        else:
            high = jnp.where(hit, 1.0, high)
    high = high.astype(jnp.bfloat16)
    low = low.astype(jnp.bfloat16)
    step, lo = min(512, width), 0 if scaled else PIECE
    for col in range(0, width, step):
        rows = jnp.concatenate([back[lo : lo + PIECE, col : col + step] for back in backs], axis=0)
        summed = dot(high, rows, ((0,), (0,)))
        if scaled:
            summed = (summed + dot(low, rows, ((0,), (0,)))) / 1024.0
        own_ref[:, col : col + step] = summed[:tok]
        other_ref[:, col : col + step] = summed[tok:]


def combine(routing, other_routing, backs, tiles, scaled):
    chips = len(backs)
    tok, width = routing.shape[1], backs[0].shape[1]
    return pl.pallas_call(
        functools.partial(combine_kernel, chips, tiles, scaled),
        out_shape=[jax.ShapeDtypeStruct((tok, width), jnp.float32)] * 2,
        in_specs=[VMEM] * (2 + chips),
        out_specs=[VMEM] * 2,
        compiler_params=params(24),
        cost_estimate=cost(4 * chips * PIECE * tok * width, 2 * chips * PIECE * width + 8 * tok * width),
        name="combine_mixed" if scaled else "combine_grad",
    )(routing, other_routing, *backs)


def add_to(total, part, step):
    @pl.when(step == 0)
    def _():
        total[...] = part

    @pl.when(step > 0)
    def _():
        total[...] += part


def experts_kernel(layouts, share, hidden, rows_ref, wg, wu, wd, back_ref, *refs):
    sends, (z_total, dx_total) = refs[: len(layouts)], refs[len(layouts) :]
    step, last = pl.program_id(0), pl.num_programs(0) - 1
    tile = wg.shape[1]

    @pl.when(step == 0)
    def _():
        store_rows(sends, layouts, "x", rows_ref, 0, share)
        store_rows(sends, layouts, "dz", rows_ref, PIECE, share)

    x, dz = rows_ref[:PIECE, :], rows_ref[PIECE:, :]
    a, b = dot(x, wg[...]), dot(x, wu[...])
    dh = dot(dz, wd[...], ((1,), (1,)))
    sig = jax.nn.sigmoid(a)
    act = a * sig
    h = (act * b).astype(jnp.bfloat16)
    d_gate = (dh * b * (sig * (1.0 + a * (1.0 - sig)))).astype(jnp.bfloat16)
    d_up = (dh * act).astype(jnp.bfloat16)
    store_part(sends, layouts, step, tile, h, 0)
    store_part(sends, layouts, step, tile, d_gate, hidden)
    store_part(sends, layouts, step, tile, d_up, 2 * hidden)
    add_to(z_total, dot(h, wd[...]), step)
    add_to(dx_total, dot(d_gate, wg[...], ((1,), (1,))) + dot(d_up, wu[...], ((1,), (1,))), step)

    @pl.when(step == last)
    def _():
        back_ref[...] = jnp.concatenate([z_total[...], dx_total[...]], axis=0).astype(jnp.bfloat16)


def whole(shape):
    return pl.BlockSpec(shape, lambda i: (0, 0))


def in_hbm(*weights):
    return [pltpu.with_memory_space_constraint(w, pltpu.HBM) for w in weights]


def hidden_tile(hidden):
    return 256 if hidden % 256 == 0 else hidden


def experts(rows, weights, groups):
    width, hidden = weights[0].shape
    tile, share = hidden_tile(hidden), width // groups
    layouts = all_layouts(groups, share, 3 * hidden, KINDS)
    sends = [(PIECE, fields_width(fields)) for fields in layouts]
    columns = pl.BlockSpec((width, tile), lambda i: (0, i))
    results = pl.pallas_call(
        functools.partial(experts_kernel, layouts, share, hidden),
        grid=(hidden // tile,),
        out_shape=[jax.ShapeDtypeStruct((2 * PIECE, width), jnp.bfloat16)]
        + [jax.ShapeDtypeStruct(shape, jnp.bfloat16) for shape in sends],
        in_specs=[whole((2 * PIECE, width)), columns, columns, pl.BlockSpec((tile, width), lambda i: (i, 0))],
        out_specs=[whole((2 * PIECE, width))] + [whole(shape) for shape in sends],
        scratch_shapes=[pltpu.VMEM((PIECE, width), jnp.float32)] * 2,
        compiler_params=params(24),
        cost_estimate=cost(12 * PIECE * width * hidden, 6 * width * hidden + 8 * PIECE * width),
        name="experts",
    )(rows, *in_hbm(*weights))
    return results[0], list(results[1:])


def take(refs, fields):
    return jnp.concatenate([refs[i][:, column : column + count] for i, column, _, count in fields], axis=1)


def take_tile(refs, fields, lo, tile):
    for i, column, first, count in fields:
        if first <= lo < first + count:
            return refs[i][:, column + lo - first : column + lo - first + tile]


def weight_kernel(groups, count, *refs):
    gate_ref, up_ref, down_ref = refs[-3:]
    share, hidden = gate_ref.shape
    tile = min(256, hidden)
    fields = received(groups, share, 3 * hidden, KINDS)
    sources = [(refs[at : at + count], found) for at in range(0, len(refs) - 3, count) for found in fields]
    x = jnp.concatenate([take(arrays, found["x"]) for arrays, found in sources], axis=0)
    dz = jnp.concatenate([take(arrays, found["dz"]) for arrays, found in sources], axis=0)

    def part(lo):
        return jnp.concatenate([take_tile(arrays, found["part"], lo, tile) for arrays, found in sources], axis=0)

    for col in range(0, hidden, tile):
        gate_ref[:, col : col + tile] = dot(x, part(hidden + col), ((0,), (0,)))
        up_ref[:, col : col + tile] = dot(x, part(2 * hidden + col), ((0,), (0,)))
        down_ref[col : col + tile, :] = dot(part(col), dz, ((0,), (0,)))


def weight_grads(sets, groups, share, hidden):
    arrays = [array for one in sets for array in one]
    rows = groups * len(sets) * PIECE
    return pl.pallas_call(
        functools.partial(weight_kernel, groups, len(sets[0])),
        out_shape=[jax.ShapeDtypeStruct((share, hidden), jnp.float32)] * 2
        + [jax.ShapeDtypeStruct((hidden, share), jnp.float32)],
        in_specs=[VMEM] * len(arrays),
        out_specs=[VMEM] * 3,
        compiler_params=params(48),
        cost_estimate=cost(6 * rows * share * hidden, 12 * share * hidden + 2 * rows * (2 * share + 3 * hidden)),
        name="weight_grads",
    )(*arrays)


def per_device(tokens, routes, gates, cotangent, w_gate, w_up, w_down):
    devices, groups = lax.axis_size("expert"), lax.axis_size("dp")
    chips, tiles = devices // 2, devices // EXPERTS
    width, hidden = w_gate.shape
    share = width // groups

    def swap(v):
        return lax.ppermute(v, "expert", [(i, i ^ 1) for i in range(devices)])

    def over_z(v, k):
        return lax.ppermute(v, "expert", [(i, i ^ (2 * k)) for i in range(devices)]) if k else v

    def over_dp(v, k):
        return lax.ppermute(v, "dp", [(i, i ^ k) for i in range(groups)]) if k else v

    def after(values, *others):
        return lax.optimization_barrier((values, others))[0]

    messages, relayed = send_layout(groups, share, 3 * hidden, KINDS)

    def first_phase(sends):
        return [sends[0]] + [over_dp(v, k) for v, (k, _) in zip(sends[1:], messages)]

    def second_phase(first, second):
        if relayed:
            for index, k in ((1, 2), (2, 1)):
                both = jnp.concatenate([first[index][:, -relayed:], second[index][:, -relayed:]], axis=0)
                both = over_dp(both, k)
                first.append(both[:PIECE])
                second.append(both[PIECE:])
        return first, second

    routing = jnp.concatenate([routes.T, gates.T], axis=0)
    other_routing = swap(routing)
    out = dispatch(routing, other_routing, tokens, swap(tokens), cotangent, swap(cotangent), chips, tiles)
    weights = (w_gate, w_up, w_down)
    order = [0, 1] + list(range(chips - 1, 1, -1))
    rows = {k: over_z(out[k], k) for k in order}
    back, sets, previous = {}, [], []
    last = order[-1]
    for k in order[:-1]:
        back[k], sends = experts(after(rows[k], *previous), weights, groups)
        if len(sets) == 2:
            sends = after(sends, *sets[0])
        sets.append(first_phase(sends))
        previous = [back[k]]
    held = after([back[k] for k in order[:-1]], back[order[-2]])
    back.update(zip(order[:-1], held))
    got = {k: over_z(back[k], k) for k in order[2:-1]}
    back[last], sends = experts(after(rows[last], *previous, *sets[0], *sets[1]), weights, groups)
    got[last] = over_z(back[last], last)
    got[0], got[1] = back[0], over_z(back[1], 1)
    sends = after(sends, *sets[2], got[1])
    sets.append(first_phase(sends))
    sets[0], sets[1] = after((sets[0], sets[1]), back[last])
    sets[:2] = second_phase(*sets[:2])
    sets[2:4] = second_phase(*sets[2:4])
    grads = weight_grads(sets, groups, share, hidden)
    back = after([got[k] for k in range(chips)], *grads)

    def finish(scaled):
        mine, theirs = combine(routing, other_routing, back, tiles, scaled)
        return (mine + swap(theirs)).astype(jnp.bfloat16)

    mixed, input_grad = finish(True), finish(False)
    return (mixed, input_grad, *grads)


def solution(mesh):
    rows = P(("dp", "expert"), None)
    in_specs = (rows, rows, rows, rows, P(None, "expert"), P(None, "expert"), P("expert", None))
    out_specs = (rows, rows, P("dp", "expert"), P("dp", "expert"), P("expert", "dp"))
    return jax.shard_map(
        per_device, mesh=mesh, in_specs=in_specs, out_specs=out_specs, check_vma=False
    )
```

time: 212 us -> 142 us (0.67)
  the two profiles are of different devices: /device:TPU:16 before, /device:TPU:0 now
where the time goes in v2:
time: 142 us
  Pallas kernels  62.2 us (44%)
  waiting for transfers between devices  39.9 us (28%)
  starting transfers between devices  34.9 us (25%)
  other arithmetic  2.73 us (2%)
    pallas_call x4, Pallas kernels, experts(): pl.pallas_call(functools.partial(experts_kernel, layouts, share, hidden),...  48.6 us
    ppermute x12, waiting for transfers between devices, over_dp(): lax.ppermute(v, 'dp', [(i, i ^ k) for i in range(groups)])  37.2 us
    ppermute x6, starting transfers between devices, over_z(): lax.ppermute(v, 'expert', [(i, i ^ 2 * k) for i in range(devices)])  22 us
    ppermute x12, starting transfers between devices, over_dp(): lax.ppermute(v, 'dp', [(i, i ^ k) for i in range(groups)])  11.3 us
    pallas_call x1, Pallas kernels, weight_grads(): pl.pallas_call(functools.partial(weight_kernel, groups, len(sets[0])), ou...  8.73 us
  transfers between devices with their start and end apart: 23, of which 9 were waited for; matrix products, arithmetic and copies ran while one was open for 1% of the time, Pallas kernels for 42%

profile of v2, /device:TPU:0, one launch (start us, length us, event | category | flops | bytes accessed | tf_op | source)
XLA Modules:
  0.0 141.6 jit_solution(8013481154238909066)
XLA Ops:
  1.2 0.7 pad_add_fusion.routing_ref
  2.4 1.1 collective-permute-done.other_routing_ref
  3.6 2.2 %dispatch.1 = (bf16[144,2048]{1,0:T(8,128)(2,1)S(1)}, bf16[144,2048]{1,0:T(8,128)(2,1)S(1)}, bf16[144,2048]{1,0:T(8,128)(2,1)S(1)}, bf16[144,2048]{1,0:T(8,128)(2,1)S(1)}) custom-call(s32[4,128]{1,0:T(4,128)S(1)} %pad_add_fusion.routing_ref, s32[4,128]{1,0:T(4,128)S(1)} %collective-permute-done.other_routing_ref, bf16[128,2048]{1,0:T(8,128)(2,1)} %x_ref.1, ...), custom_call_target="tpu_custom_call" | custom-call | flops 603979776 | bytes 4456448 | tf_op jit(solution)/shard_map/dispatch/pallas_call | solution.py:151
  5.9 3.0 %collective-permute-start.3 = (bf16[144,2048]{1,0:T(8,128)(2,1)S(1)}, bf16[144,2048]{1,0:T(8,128)(2,1)S(1)}, u32[]{:S(2)}, u32[]{:S(2)}) collective-permute-start(bf16[144,2048]{1,0:T(8,128)(2,1)S(1)} %get-tuple-element.56), channel_id=1, source_target_pairs={{0,2},{1,3},{2,0},{3,1},{4,6},{5,7},{6,4},{7,5},{8,10},{9,11},{10,... | collective-permute-start | bytes 1769480 | tf_op jit(solution)/shard_map/ppermute | solution.py:329
  8.9 2.5 %collective-permute-start.4 = (bf16[144,2048]{1,0:T(8,128)(2,1)S(1)}, bf16[144,2048]{1,0:T(8,128)(2,1)S(1)}, u32[]{:S(2)}, u32[]{:S(2)}) collective-permute-start(bf16[144,2048]{1,0:T(8,128)(2,1)S(1)} %get-tuple-element.59), channel_id=1, source_target_pairs={{0,6},{1,7},{2,4},{3,5},{4,2},{5,3},{6,0},{7,1},{8,14},{9,15},{10,... | collective-permute-start | bytes 1769480 | tf_op jit(solution)/shard_map/ppermute | solution.py:329
  11.4 12.0 %experts.4 = (bf16[144,2048]{1,0:T(8,128)(2,1)S(1)}, bf16[72,4096]{1,0:T(8,128)(2,1)S(1)}, bf16[72,4608]{1,0:T(8,128)(2,1)S(1)}, bf16[72,4608]{1,0:T(8,128)(2,1)S(1)}) custom-call(bf16[144,2048]{1,0:T(8,128)(2,1)S(1)} %get-tuple-element.54.rows_ref, bf16[2048,1024]{1,0:T(8,128)(2,1)} %wg.7, bf16[2048,1024]{1,0:T(8,128)(2,1)} %wu.7, bf16[1024,2048]{1,0:T(8,128)(2,1)} %wd.7), custom_call_target="tpu_custom_call" | custom-call | flops 1811939328 | bytes 13762560 | tf_op jit(solution)/shard_map/experts/pallas_call | solution.py:261
  23.4 1.6 %collective-permute-start.7 = (bf16[72,4608]{1,0:T(8,128)(2,1)S(1)}, bf16[72,4608]{1,0:T(8,128)(2,1)S(1)}, u32[]{:S(2)}, u32[]{:S(2)}) collective-permute-start(bf16[72,4608]{1,0:T(8,128)(2,1)S(1)} %get-tuple-element.66), channel_id=1, source_target_pairs={{0,8},{8,0},{16,24},{24,16},{1,9},{9,1},{17,25},{25,17},{2,10},{10... | collective-permute-start | bytes 1990664 | tf_op jit(solution)/shard_map/ppermute | solution.py:332
  24.9 1.5 %collective-permute-start.8 = (bf16[72,4608]{1,0:T(8,128)(2,1)S(1)}, bf16[72,4608]{1,0:T(8,128)(2,1)S(1)}, u32[]{:S(2)}, u32[]{:S(2)}) collective-permute-start(bf16[72,4608]{1,0:T(8,128)(2,1)S(1)} %get-tuple-element.67), channel_id=1, source_target_pairs={{0,16},{8,24},{16,0},{24,8},{1,17},{9,25},{17,1},{25,9},{2,18},{10... | collective-permute-start | bytes 1990664 | tf_op jit(solution)/shard_map/ppermute | solution.py:332
  26.5 12.0 %experts.5 = (bf16[144,2048]{1,0:T(8,128)(2,1)S(1)}, bf16[72,4096]{1,0:T(8,128)(2,1)S(1)}, bf16[72,4608]{1,0:T(8,128)(2,1)S(1)}, bf16[72,4608]{1,0:T(8,128)(2,1)S(1)}) custom-call(bf16[144,2048]{1,0:T(8,128)(2,1)S(1)} %collective-permute-done.3.rows_ref, bf16[2048,1024]{1,0:T(8,128)(2,1)} %wg.7, bf16[2048,1024]{1,0:T(8,128)(2,1)} %wu.7, bf16[1024,2048]{1,0:T(8,128)(2,1)} %wd.7), custom_call_target="tpu_custom_call" | custom-call | flops 1811939328 | bytes 13762560 | tf_op jit(solution)/shard_map/experts/pallas_call | solution.py:261
  38.5 0.6 collective-permute-start.9
  39.6 1.6 %collective-permute-start.6 = (bf16[144,2048]{1,0:T(8,128)(2,1)S(1)}, bf16[144,2048]{1,0:T(8,128)(2,1)S(1)}, u32[]{:S(2)}, u32[]{:S(2)}) collective-permute-start(bf16[144,2048]{1,0:T(8,128)(2,1)S(1)} %get-tuple-element.64), channel_id=1, source_target_pairs={{0,4},{1,5},{2,6},{3,7},{4,0},{5,1},{6,2},{7,3},{8,12},{9,13},{10,... | collective-permute-start | bytes 1769480 | tf_op jit(solution)/shard_map/ppermute | solution.py:329
  41.2 12.0 %experts.6 = (bf16[144,2048]{1,0:T(8,128)(2,1)S(1)}, bf16[72,4096]{1,0:T(8,128)(2,1)S(1)}, bf16[72,4608]{1,0:T(8,128)(2,1)S(1)}, bf16[72,4608]{1,0:T(8,128)(2,1)S(1)}) custom-call(bf16[144,2048]{1,0:T(8,128)(2,1)S(1)} %collective-permute-done.4.rows_ref, bf16[2048,1024]{1,0:T(8,128)(2,1)} %wg.7, bf16[2048,1024]{1,0:T(8,128)(2,1)} %wu.7, bf16[1024,2048]{1,0:T(8,128)(2,1)} %wd.7), custom_call_target="tpu_custom_call" | custom-call | flops 1811939328 | bytes 13762560 | tf_op jit(solution)/shard_map/experts/pallas_call | solution.py:261
  53.2 13.5 %collective-permute-start.5 = (bf16[144,2048]{1,0:T(8,128)(2,1)S(1)}, bf16[144,2048]{1,0:T(8,128)(2,1)S(1)}, u32[]{:S(2)}, u32[]{:S(2)}) collective-permute-start(bf16[144,2048]{1,0:T(8,128)(2,1)S(1)} %get-tuple-element.63), channel_id=1, source_target_pairs={{0,2},{1,3},{2,0},{3,1},{4,6},{5,7},{6,4},{7,5},{8,10},{9,11},{10,... | collective-permute-start | bytes 1769480 | tf_op jit(solution)/shard_map/ppermute | solution.py:329
  67.2 1.0 collective-permute-start.16
  68.2 12.7 %experts.7 = (bf16[144,2048]{1,0:T(8,128)(2,1)S(1)}, bf16[72,4096]{1,0:T(8,128)(2,1)S(1)}, bf16[72,4608]{1,0:T(8,128)(2,1)S(1)}, bf16[72,4608]{1,0:T(8,128)(2,1)S(1)}) custom-call(bf16[144,2048]{1,0:T(8,128)(2,1)S(1)} %collective-permute-done.6.rows_ref, bf16[2048,1024]{1,0:T(8,128)(2,1)} %wg.7, bf16[2048,1024]{1,0:T(8,128)(2,1)} %wu.7, bf16[1024,2048]{1,0:T(8,128)(2,1)} %wd.7), custom_call_target="tpu_custom_call" | custom-call | flops 1811939328 | bytes 13762560 | tf_op jit(solution)/shard_map/experts/pallas_call | solution.py:261
  81.0 1.7 %collective-permute-start.14 = (bf16[144,2048]{1,0:T(8,128)(2,1)S(1)}, bf16[144,2048]{1,0:T(8,128)(2,1)S(1)}, u32[]{:S(2)}, u32[]{:S(2)}) collective-permute-start(bf16[144,2048]{1,0:T(8,128)(2,1)S(1)} %pad_maximum_fusion.1), channel_id=1, source_target_pairs={{0,8},{8,0},{16,24},{24,16},{1,9},{9,1},{17,25},{25,17},{2,10},{10... | collective-permute-start | bytes 1769480 | tf_op jit(solution)/shard_map/ppermute | solution.py:332
  82.8 1.3 collective-permute-start.12
  84.3 1.3 collective-permute-start.17
  85.7 1.1 collective-permute-start.13
  86.7 10.6 %collective-permute-done.14 = bf16[144,2048]{1,0:T(8,128)(2,1)S(1)} collective-permute-done((bf16[144,2048]{1,0:T(8,128)(2,1)S(1)}, bf16[144,2048]{1,0:T(8,128)(2,1)S(1)}, u32[]{:S(2)}, u32[]{:S(2)}) %collective-permute-start.14) | collective-permute-done | bytes 589856 | tf_op jit(solution)/shard_map/ppermute | solution.py:332
  97.4 1.0 collective-permute-start.19
  98.4 11.6 %collective-permute-done.17.refs_16_ = bf16[72,4608]{1,0:T(8,128)(2,1)S(1)} collective-permute-done((bf16[72,4608]{1,0:T(8,128)(2,1)S(1)}, bf16[72,4608]{1,0:T(8,128)(2,1)S(1)}, u32[]{:S(2)}, u32[]{:S(2)}) %collective-permute-start.17) | collective-permute-done | bytes 663584 | tf_op jit(solution)/shard_map/ppermute | solution.py:332
  110.5 4.3 %collective-permute-done.19.refs_17_ = bf16[72,4608]{1,0:T(8,128)(2,1)S(1)} collective-permute-done((bf16[72,4608]{1,0:T(8,128)(2,1)S(1)}, bf16[72,4608]{1,0:T(8,128)(2,1)S(1)}, u32[]{:S(2)}, u32[]{:S(2)}) %collective-permute-start.19) | collective-permute-done | bytes 663584 | tf_op jit(solution)/shard_map/ppermute | solution.py:332
  115.0 0.6 copy-done.5
  115.6 10.1 %collective-permute-done.18 = bf16[144,2048]{1,0:T(8,128)(2,1)S(1)} collective-permute-done((bf16[144,2048]{1,0:T(8,128)(2,1)S(1)}, bf16[144,2048]{1,0:T(8,128)(2,1)S(1)}, u32[]{:S(2)}, u32[]{:S(2)}) %collective-permute-start.18) | collective-permute-done | bytes 589856 | tf_op jit(solution)/shard_map/ppermute | solution.py:332
  125.7 0.6 collective-permute-done.20
  126.4 8.7 %weight_grads.1 = (f32[512,1024]{1,0:T(8,128)}, f32[512,1024]{1,0:T(8,128)}, f32[1024,512]{1,0:T(8,128)}) custom-call(bf16[72,4096]{1,0:T(8,128)(2,1)S(1)} %get-tuple-element.74.refs_0_, bf16[72,4608]{1,0:T(8,128)(2,1)S(1)} %collective-permute-done.7.refs_1_, bf16[72,4608]{1,0:T(8,128)(2,1)S(1)} %collective-permute-done.8.refs_2_, ...), custom_call_target="tpu_custom_call" | custom-call | flops 3623878656 | bytes 15728640 | tf_op jit(solution)/shard_map/weight_grads/pallas_call | solution.py:307
  135.2 1.0 combine_grad.1
  136.2 1.6 %combine_mixed.1 = (f32[128,2048]{1,0:T(8,128)S(1)}, f32[128,2048]{1,0:T(8,128)S(1)}) custom-call(s32[4,128]{1,0:T(4,128)S(1)} %pad_add_fusion.routing_ref, s32[4,128]{1,0:T(4,128)S(1)} %collective-permute-done.other_routing_ref, bf16[144,2048]{1,0:T(8,128)(2,1)S(1)} %get-tuple-element.95.refs_0_, bf16[144,2048]{1,0:T(8,128)(2,1)S(1)} %collective-permute-done.5.refs_1_, ...), custom_call_target="tpu_custom_call" | custom-call | flops 301989888 | bytes 3276800 | tf_op jit(solution)/shard_map/combine_mixed/pallas_call | solution.py:193
  138.9 0.9 add_convert_fusion
  139.8 0.9 collective-permute-done.21
  140.7 0.9 add_convert_fusion.1
  (55 shorter events, 4.4 us)
Async XLA Ops:
  0.6 2.8 %collective-permute-start.1 = (bf16[128,2048]{1,0:T(8,128)(2,1)}, bf16[128,2048]{1,0:T(8,128)(2,1)S(1)}, u32[]{:S(2)}, u32[]{:S(2)}) collective-permute-start(bf16[128,2048]{1,0:T(8,128)(2,1)} %x_ref.1), channel_id=1, source_target_pairs={{0,1},{1,0},{2,3},{3,2},{4,5},{5,4},{6,7},{7,6},{8,9},{9,8},{10,11... | collective-permute-start | bytes 1572872 | tf_op jit(solution)/shard_map/ppermute | solution.py:326
  1.1 2.5 %collective-permute-start.2 = (bf16[128,2048]{1,0:T(8,128)(2,1)}, bf16[128,2048]{1,0:T(8,128)(2,1)S(1)}, u32[]{:S(2)}, u32[]{:S(2)}) collective-permute-start(bf16[128,2048]{1,0:T(8,128)(2,1)} %dy_ref.1), channel_id=1, source_target_pairs={{0,1},{1,0},{2,3},{3,2},{4,5},{5,4},{6,7},{7,6},{8,9},{9,8},{10,11... | collective-permute-start | bytes 1572872 | tf_op jit(solution)/shard_map/ppermute | solution.py:326
  1.9 1.5 %collective-permute-start = (s32[4,128]{1,0:T(4,128)S(1)}, s32[4,128]{1,0:T(4,128)S(1)}, u32[]{:S(2)}, u32[]{:S(2)}) collective-permute-start(s32[4,128]{1,0:T(4,128)S(1)} %pad_add_fusion.routing_ref), channel_id=1, source_target_pairs={{0,1},{1,0},{2,3},{3,2},{4,5},{5,4},{6,7},{7,6},{8,9},{9,8},{10,11... | collective-permute-start | bytes 6152 | tf_op jit(solution)/shard_map/ppermute | solution.py:326
  5.9 20.6 %collective-permute-start.3 = (bf16[144,2048]{1,0:T(8,128)(2,1)S(1)}, bf16[144,2048]{1,0:T(8,128)(2,1)S(1)}, u32[]{:S(2)}, u32[]{:S(2)}) collective-permute-start(bf16[144,2048]{1,0:T(8,128)(2,1)S(1)} %get-tuple-element.56), channel_id=1, source_target_pairs={{0,2},{1,3},{2,0},{3,1},{4,6},{5,7},{6,4},{7,5},{8,10},{9,11},{10,... | collective-permute-start | bytes 1769480 | tf_op jit(solution)/shard_map/ppermute | solution.py:329
  8.9 30.7 %collective-permute-start.4 = (bf16[144,2048]{1,0:T(8,128)(2,1)S(1)}, bf16[144,2048]{1,0:T(8,128)(2,1)S(1)}, u32[]{:S(2)}, u32[]{:S(2)}) collective-permute-start(bf16[144,2048]{1,0:T(8,128)(2,1)S(1)} %get-tuple-element.59), channel_id=1, source_target_pairs={{0,6},{1,7},{2,4},{3,5},{4,2},{5,3},{6,0},{7,1},{8,14},{9,15},{10,... | collective-permute-start | bytes 1769480 | tf_op jit(solution)/shard_map/ppermute | solution.py:329
  23.4 29.8 %collective-permute-start.7 = (bf16[72,4608]{1,0:T(8,128)(2,1)S(1)}, bf16[72,4608]{1,0:T(8,128)(2,1)S(1)}, u32[]{:S(2)}, u32[]{:S(2)}) collective-permute-start(bf16[72,4608]{1,0:T(8,128)(2,1)S(1)} %get-tuple-element.66), channel_id=1, source_target_pairs={{0,8},{8,0},{16,24},{24,16},{1,9},{9,1},{17,25},{25,17},{2,10},{10... | collective-permute-start | bytes 1990664 | tf_op jit(solution)/shard_map/ppermute | solution.py:332
  24.9 41.7 %collective-permute-start.8 = (bf16[72,4608]{1,0:T(8,128)(2,1)S(1)}, bf16[72,4608]{1,0:T(8,128)(2,1)S(1)}, u32[]{:S(2)}, u32[]{:S(2)}) collective-permute-start(bf16[72,4608]{1,0:T(8,128)(2,1)S(1)} %get-tuple-element.67), channel_id=1, source_target_pairs={{0,16},{8,24},{16,0},{24,8},{1,17},{9,25},{17,1},{25,9},{2,18},{10... | collective-permute-start | bytes 1990664 | tf_op jit(solution)/shard_map/ppermute | solution.py:332
  38.5 29.8 %collective-permute-start.9 = (bf16[72,4608]{1,0:T(8,128)(2,1)S(1)}, bf16[72,4608]{1,0:T(8,128)(2,1)S(1)}, u32[]{:S(2)}, u32[]{:S(2)}) collective-permute-start(bf16[72,4608]{1,0:T(8,128)(2,1)S(1)} %get-tuple-element.69), channel_id=1, source_target_pairs={{0,8},{8,0},{16,24},{24,16},{1,9},{9,1},{17,25},{25,17},{2,10},{10... | collective-permute-start | bytes 1990664 | tf_op jit(solution)/shard_map/ppermute | solution.py:332
  39.1 29.2 %collective-permute-start.10 = (bf16[72,4608]{1,0:T(8,128)(2,1)S(1)}, bf16[72,4608]{1,0:T(8,128)(2,1)S(1)}, u32[]{:S(2)}, u32[]{:S(2)}) collective-permute-start(bf16[72,4608]{1,0:T(8,128)(2,1)S(1)} %get-tuple-element.70), channel_id=1, source_target_pairs={{0,16},{8,24},{16,0},{24,8},{1,17},{9,25},{17,1},{25,9},{2,18},{10... | collective-permute-start | bytes 1990664 | tf_op jit(solution)/shard_map/ppermute | solution.py:332
  39.6 27.6 %collective-permute-start.6 = (bf16[144,2048]{1,0:T(8,128)(2,1)S(1)}, bf16[144,2048]{1,0:T(8,128)(2,1)S(1)}, u32[]{:S(2)}, u32[]{:S(2)}) collective-permute-start(bf16[144,2048]{1,0:T(8,128)(2,1)S(1)} %get-tuple-element.64), channel_id=1, source_target_pairs={{0,4},{1,5},{2,6},{3,7},{4,0},{5,1},{6,2},{7,3},{8,12},{9,13},{10,... | collective-permute-start | bytes 1769480 | tf_op jit(solution)/shard_map/ppermute | solution.py:329
  53.2 31.0 %collective-permute-start.5 = (bf16[144,2048]{1,0:T(8,128)(2,1)S(1)}, bf16[144,2048]{1,0:T(8,128)(2,1)S(1)}, u32[]{:S(2)}, u32[]{:S(2)}) collective-permute-start(bf16[144,2048]{1,0:T(8,128)(2,1)S(1)} %get-tuple-element.63), channel_id=1, source_target_pairs={{0,2},{1,3},{2,0},{3,1},{4,6},{5,7},{6,4},{7,5},{8,10},{9,11},{10,... | collective-permute-start | bytes 1769480 | tf_op jit(solution)/shard_map/ppermute | solution.py:329
  66.7 17.6 %collective-permute-start.15 = (bf16[72,4608]{1,0:T(8,128)(2,1)S(1)}, bf16[72,4608]{1,0:T(8,128)(2,1)S(1)}, u32[]{:S(2)}, u32[]{:S(2)}) collective-permute-start(bf16[72,4608]{1,0:T(8,128)(2,1)S(1)} %get-tuple-element.84), channel_id=1, source_target_pairs={{0,8},{8,0},{16,24},{24,16},{1,9},{9,1},{17,25},{25,17},{2,10},{10... | collective-permute-start | bytes 1990664 | tf_op jit(solution)/shard_map/ppermute | solution.py:332
  67.2 17.1 %collective-permute-start.16 = (bf16[72,4608]{1,0:T(8,128)(2,1)S(1)}, bf16[72,4608]{1,0:T(8,128)(2,1)S(1)}, u32[]{:S(2)}, u32[]{:S(2)}) collective-permute-start(bf16[72,4608]{1,0:T(8,128)(2,1)S(1)} %get-tuple-element.85), channel_id=1, source_target_pairs={{0,16},{8,24},{16,0},{24,8},{1,17},{9,25},{17,1},{25,9},{2,18},{10... | collective-permute-start | bytes 1990664 | tf_op jit(solution)/shard_map/ppermute | solution.py:332
  68.2 15.9 %copy-start.2 = (bf16[72,4608]{1,0:T(8,128)(2,1)}, bf16[72,4608]{1,0:T(8,128)(2,1)S(1)}, u32[]{:S(2)}) copy-start(bf16[72,4608]{1,0:T(8,128)(2,1)S(1)} %collective-permute-done.9.refs_6_) | copy-start | bytes 1990660
  68.2 12.7 %copy-start.3 = (bf16[72,4608]{1,0:T(8,128)(2,1)}, bf16[72,4608]{1,0:T(8,128)(2,1)S(1)}, u32[]{:S(2)}) copy-start(bf16[72,4608]{1,0:T(8,128)(2,1)S(1)} %collective-permute-done.10.refs_7_) | copy-start | bytes 1990660
  81.0 16.3 %collective-permute-start.14 = (bf16[144,2048]{1,0:T(8,128)(2,1)S(1)}, bf16[144,2048]{1,0:T(8,128)(2,1)S(1)}, u32[]{:S(2)}, u32[]{:S(2)}) collective-permute-start(bf16[144,2048]{1,0:T(8,128)(2,1)S(1)} %pad_maximum_fusion.1), channel_id=1, source_target_pairs={{0,8},{8,0},{16,24},{24,16},{1,9},{9,1},{17,25},{25,17},{2,10},{10... | collective-permute-start | bytes 1769480 | tf_op jit(solution)/shard_map/ppermute | solution.py:332
  82.8 52.4 %collective-permute-start.12 = (bf16[144,2048]{1,0:T(8,128)(2,1)S(1)}, bf16[144,2048]{1,0:T(8,128)(2,1)S(1)}, u32[]{:S(2)}, u32[]{:S(2)}) collective-permute-start(bf16[144,2048]{1,0:T(8,128)(2,1)S(1)} %get-tuple-element.73), channel_id=1, source_target_pairs={{0,6},{1,7},{2,4},{3,5},{4,2},{5,3},{6,0},{7,1},{8,14},{9,15},{10,... | collective-permute-start | bytes 1769480 | tf_op jit(solution)/shard_map/ppermute | solution.py:329
  84.2 51.0 %collective-permute-start.11 = (bf16[144,2048]{1,0:T(8,128)(2,1)S(1)}, bf16[144,2048]{1,0:T(8,128)(2,1)S(1)}, u32[]{:S(2)}, u32[]{:S(2)}) collective-permute-start(bf16[144,2048]{1,0:T(8,128)(2,1)S(1)} %get-tuple-element.72), channel_id=1, source_target_pairs={{0,4},{1,5},{2,6},{3,7},{4,0},{5,1},{6,2},{7,3},{8,12},{9,13},{10,... | collective-permute-start | bytes 1769480 | tf_op jit(solution)/shard_map/ppermute | solution.py:329
  84.3 2.5 %copy-start.1 = (bf16[72,4608]{1,0:T(8,128)(2,1)}, bf16[72,4608]{1,0:T(8,128)(2,1)S(1)}, u32[]{:S(2)}) copy-start(bf16[72,4608]{1,0:T(8,128)(2,1)S(1)} %collective-permute-done.15.refs_11_) | copy-start | bytes 1990660
  84.3 2.5 %copy-start = (bf16[72,4608]{1,0:T(8,128)(2,1)}, bf16[72,4608]{1,0:T(8,128)(2,1)S(1)}, u32[]{:S(2)}) copy-start(bf16[72,4608]{1,0:T(8,128)(2,1)S(1)} %collective-permute-done.16.refs_12_) | copy-start | bytes 1990660
  84.3 25.7 %collective-permute-start.17 = (bf16[72,4608]{1,0:T(8,128)(2,1)S(1)}, bf16[72,4608]{1,0:T(8,128)(2,1)S(1)}, u32[]{:S(2)}, u32[]{:S(2)}) collective-permute-start(bf16[72,4608]{1,0:T(8,128)(2,1)S(1)} %get-tuple-element.89), channel_id=1, source_target_pairs={{0,8},{8,0},{16,24},{24,16},{1,9},{9,1},{17,25},{25,17},{2,10},{10... | collective-permute-start | bytes 1990664 | tf_op jit(solution)/shard_map/ppermute | solution.py:332
  85.7 29.3 %collective-permute-start.13 = (bf16[144,2048]{1,0:T(8,128)(2,1)S(1)}, bf16[144,2048]{1,0:T(8,128)(2,1)S(1)}, u32[]{:S(2)}, u32[]{:S(2)}) collective-permute-start(bf16[144,2048]{1,0:T(8,128)(2,1)S(1)} %pad_maximum_fusion), channel_id=1, source_target_pairs={{0,16},{8,24},{16,0},{24,8},{1,17},{9,25},{17,1},{25,9},{2,18},{10... | collective-permute-start | bytes 1769480 | tf_op jit(solution)/shard_map/ppermute | solution.py:332
  97.4 12.7 %slice-start.1 = ((bf16[72,4608]{1,0:T(8,128)(2,1)}), bf16[72,2048]{1,0:T(8,128)(2,1)S(1)}, s32[]{:S(2)}) async-start(bf16[72,4608]{1,0:T(8,128)(2,1)} %copy-done.1), calls=%async_computation.1 | async-start | bytes 589824 | tf_op jit(solution)/shard_map/slice | solution.py:345
  97.4 17.4 %collective-permute-start.19 = (bf16[72,4608]{1,0:T(8,128)(2,1)S(1)}, bf16[72,4608]{1,0:T(8,128)(2,1)S(1)}, u32[]{:S(2)}, u32[]{:S(2)}) collective-permute-start(bf16[72,4608]{1,0:T(8,128)(2,1)S(1)} %get-tuple-element.90), channel_id=1, source_target_pairs={{0,16},{8,24},{16,0},{24,8},{1,17},{9,25},{17,1},{25,9},{2,18},{10... | collective-permute-start | bytes 1990664 | tf_op jit(solution)/shard_map/ppermute | solution.py:332
  98.4 16.3 %slice-start = ((bf16[72,4608]{1,0:T(8,128)(2,1)}), bf16[72,2048]{1,0:T(8,128)(2,1)S(1)}, s32[]{:S(2)}) async-start(bf16[72,4608]{1,0:T(8,128)(2,1)} %copy-done), calls=%async_computation | async-start | bytes 589824 | tf_op jit(solution)/shard_map/slice | solution.py:345
  110.0 4.8 %copy-start.4 = (bf16[72,4608]{1,0:T(8,128)(2,1)}, bf16[72,4608]{1,0:T(8,128)(2,1)S(1)}, u32[]{:S(2)}) copy-start(bf16[72,4608]{1,0:T(8,128)(2,1)S(1)} %collective-permute-done.17.refs_16_) | copy-start | bytes 1990660
  110.1 15.6 %collective-permute-start.18 = (bf16[144,2048]{1,0:T(8,128)(2,1)S(1)}, bf16[144,2048]{1,0:T(8,128)(2,1)S(1)}, u32[]{:S(2)}, u32[]{:S(2)}) collective-permute-start(bf16[144,2048]{1,0:T(8,128)(2,1)S(1)} %pad_maximum_fusion.2), channel_id=1, source_target_pairs={{0,16},{8,24},{16,0},{24,8},{1,17},{9,25},{17,1},{25,9},{2,18},{10... | collective-permute-start | bytes 1769480 | tf_op jit(solution)/shard_map/ppermute | solution.py:332
  114.7 0.8 copy-start.5
  114.8 11.5 %collective-permute-start.20 = (bf16[144,2048]{1,0:T(8,128)(2,1)S(1)}, bf16[144,2048]{1,0:T(8,128)(2,1)S(1)}, u32[]{:S(2)}, u32[]{:S(2)}) collective-permute-start(bf16[144,2048]{1,0:T(8,128)(2,1)S(1)} %pad_maximum_fusion.3), channel_id=1, source_target_pairs={{0,8},{8,0},{16,24},{24,16},{1,9},{9,1},{17,25},{25,17},{2,10},{10... | collective-permute-start | bytes 1769480 | tf_op jit(solution)/shard_map/ppermute | solution.py:332
  136.1 2.7 %collective-permute-start.22 = (f32[128,2048]{1,0:T(8,128)S(1)}, f32[128,2048]{1,0:T(8,128)S(1)}, u32[]{:S(2)}, u32[]{:S(2)}) collective-permute-start(f32[128,2048]{1,0:T(8,128)S(1)} %get-tuple-element.102), channel_id=1, source_target_pairs={{0,1},{1,0},{2,3},{3,2},{4,5},{5,4},{6,7},{7,6},{8,9},{9,8},{10,11... | collective-permute-start | bytes 3145736 | tf_op jit(solution)/shard_map/ppermute | solution.py:326
  137.8 2.8 %collective-permute-start.21 = (f32[128,2048]{1,0:T(8,128)S(1)}, f32[128,2048]{1,0:T(8,128)S(1)}, u32[]{:S(2)}, u32[]{:S(2)}) collective-permute-start(f32[128,2048]{1,0:T(8,128)S(1)} %get-tuple-element.100), channel_id=1, source_target_pairs={{0,1},{1,0},{2,3},{3,2},{4,5},{5,4},{6,7},{7,6},{8,9},{9,8},{10,11... | collective-permute-start | bytes 3145736 | tf_op jit(solution)/shard_map/ppermute | solution.py:326

commit v3 on v2

--- a/solution.py
+++ b/solution.py
@@ -249,7 +249,7 @@
 
 
 def hidden_tile(hidden):
-    return 256 if hidden % 256 == 0 else hidden
+    return 512 if hidden % 512 == 0 else hidden
 
 
 def experts(rows, weights, groups):
@@ -266,8 +266,8 @@
         in_specs=[whole((2 * PIECE, width)), columns, columns, pl.BlockSpec((tile, width), lambda i: (i, 0))],
         out_specs=[whole((2 * PIECE, width))] + [whole(shape) for shape in sends],
         scratch_shapes=[pltpu.VMEM((PIECE, width), jnp.float32)] * 2,
-        compiler_params=params(24),
-        cost_estimate=cost(12 * PIECE * width * hidden, 6 * width * hidden + 8 * PIECE * width),
+        compiler_params=params(28),
+        cost_estimate=cost(12 * PIECE * width * hidden, 6 * width * hidden),
         name="experts",
     )(rows, *in_hbm(*weights))
     return results[0], list(results[1:])
@@ -283,36 +283,58 @@
             return refs[i][:, column + lo - first : column + lo - first + tile]
 
 
-def weight_kernel(groups, count, *refs):
-    gate_ref, up_ref, down_ref = refs[-3:]
-    share, hidden = gate_ref.shape
+def weight_kernel(plan, partial, final, *refs):
+    count = len(refs) - (7 if final else 3)
+    arrays, outs = refs[:count], refs[count : count + 3]
+    results, sems = (refs[count + 3 : count + 6], refs[count + 6]) if final else (outs, None)
+    share, hidden = results[0].shape
     tile = min(256, hidden)
-    fields = received(groups, share, 3 * hidden, KINDS)
-    sources = [(refs[at : at + count], found) for at in range(0, len(refs) - 3, count) for found in fields]
-    x = jnp.concatenate([take(arrays, found["x"]) for arrays, found in sources], axis=0)
-    dz = jnp.concatenate([take(arrays, found["dz"]) for arrays, found in sources], axis=0)
+    x = jnp.concatenate([take(arrays, found["x"]) for found in plan], axis=0)
+    dz = jnp.concatenate([take(arrays, found["dz"]) for found in plan], axis=0)
+    copies = []
 
     def part(lo):
-        return jnp.concatenate([take_tile(arrays, found["part"], lo, tile) for arrays, found in sources], axis=0)
+        return jnp.concatenate([take_tile(arrays, found["part"], lo, tile) for found in plan], axis=0)
+
+    def put(which, rows, columns, left, right):
+        value = dot(left, right, ((0,), (0,)))
+        if partial:
+            value = value + arrays[which][rows, columns]
+        results[which][rows, columns] = value
+        if final:
+            to = outs[which].at[rows, columns]
+            copies.append(pltpu.make_async_copy(results[which].at[rows, columns], to, sems.at[len(copies)]))
+            copies[-1].start()
 
     for col in range(0, hidden, tile):
-        gate_ref[:, col : col + tile] = dot(x, part(hidden + col), ((0,), (0,)))
-        up_ref[:, col : col + tile] = dot(x, part(2 * hidden + col), ((0,), (0,)))
-        down_ref[col : col + tile, :] = dot(part(col), dz, ((0,), (0,)))
-
-
-def weight_grads(sets, groups, share, hidden):
-    arrays = [array for one in sets for array in one]
-    rows = groups * len(sets) * PIECE
+        part_of, whole_of = pl.ds(col, tile), pl.ds(0, share)
+        put(0, whole_of, part_of, x, part(hidden + col))
+        put(1, whole_of, part_of, x, part(2 * hidden + col))
+        put(2, part_of, whole_of, part(col), dz)
+    for copy in copies:
+        copy.wait()
+
+
+def weight_grads(sources, partial, final, share, hidden):
+    arrays, plan = list(partial), []
+    for have, found in sources:
+        used = sorted({field[0] for fields in found.values() for field in fields})
+        at = {index: len(arrays) + i for i, index in enumerate(used)}
+        arrays += [have[index] for index in used]
+        plan.append({kind: [(at[f[0]], *f[1:]) for f in fields] for kind, fields in found.items()})
+    rows = len(sources) * PIECE
+    shapes = [(share, hidden), (share, hidden), (hidden, share)]
+    scratch = [pltpu.VMEM(shape, jnp.float32) for shape in shapes]
+    scratch += [pltpu.SemaphoreType.DMA((3 * hidden // min(256, hidden),))]
     return pl.pallas_call(
-        functools.partial(weight_kernel, groups, len(sets[0])),
-        out_shape=[jax.ShapeDtypeStruct((share, hidden), jnp.float32)] * 2
-        + [jax.ShapeDtypeStruct((hidden, share), jnp.float32)],
+        functools.partial(weight_kernel, plan, bool(partial), final),
+        out_shape=[jax.ShapeDtypeStruct(shape, jnp.float32) for shape in shapes],
         in_specs=[VMEM] * len(arrays),
-        out_specs=[VMEM] * 3,
+        out_specs=[pl.BlockSpec(memory_space=pl.ANY) if final else VMEM] * 3,
+        scratch_shapes=scratch if final else [],
         compiler_params=params(48),
         cost_estimate=cost(6 * rows * share * hidden, 12 * share * hidden + 2 * rows * (2 * share + 3 * hidden)),
-        name="weight_grads",
+        name="weight_grads" if final else "weight_grads_early",
     )(*arrays)
 
 
@@ -355,25 +377,29 @@
     order = [0, 1] + list(range(chips - 1, 1, -1))
     rows = {k: over_z(out[k], k) for k in order}
     back, sets, previous = {}, [], []
-    last = order[-1]
+    last, early = order[-1], order[-2]
     for k in order[:-1]:
         back[k], sends = experts(after(rows[k], *previous), weights, groups)
         if len(sets) == 2:
             sends = after(sends, *sets[0])
         sets.append(first_phase(sends))
         previous = [back[k]]
-    held = after([back[k] for k in order[:-1]], back[order[-2]])
-    back.update(zip(order[:-1], held))
-    got = {k: over_z(back[k], k) for k in order[2:-1]}
+    back[1] = after(back[1], back[early])
+    got = {0: back[0]}
+    got[1] = over_z(back[1], 1)
+    got.update({k: over_z(back[k], k) for k in order[1:-1] if k != 1})
     back[last], sends = experts(after(rows[last], *previous, *sets[0], *sets[1]), weights, groups)
+    back[last] = after(back[last], got[1])
     got[last] = over_z(back[last], last)
-    got[0], got[1] = back[0], over_z(back[1], 1)
-    sends = after(sends, *sets[2], got[1])
+    sets[:2] = second_phase(*sets[:2])
+    sends = after(sends, *sets[2])
     sets.append(first_phase(sends))
-    sets[0], sets[1] = after((sets[0], sets[1]), back[last])
-    sets[:2] = second_phase(*sets[:2])
     sets[2:4] = second_phase(*sets[2:4])
-    grads = weight_grads(sets, groups, share, hidden)
+    fields = received(groups, share, 3 * hidden, KINDS)
+    sources = [(one, found) for one in sets for found in fields]
+    cut = (len(sets) - 2) * len(fields) + (len(fields) - 1) * 1
+    early_grads = weight_grads(sources[:cut], [], False, share, hidden)
+    grads = weight_grads(sources[cut:], early_grads, True, share, hidden)
     back = after([got[k] for k in range(chips)], *grads)
 
     def finish(scaled):

time: 142 us -> 130 us (0.915)
  waiting for transfers between devices: 39.9 us -> 22.6 us
  starting transfers between devices: 34.9 us -> 44.7 us
  Pallas kernels: 62.2 us -> 58.1 us
    ppermute x12, waiting for transfers between devices: 37.2 us -> 19.9 us  [over_dp(): lax.ppermute(v, 'dp', [(i, i ^ k) for i in range(groups)])]
    pallas_call x4, Pallas kernels: 48.6 us -> 40.7 us  [experts(): pl.pallas_call(functools.partial(experts_kernel, layouts, share, hidden),...]
    ppermute x12, starting transfers between devices: 11.3 us -> 17.8 us  [over_dp(): lax.ppermute(v, 'dp', [(i, i ^ k) for i in range(groups)])]
    pallas_call x1 -> x2, Pallas kernels: 8.73 us -> 12.6 us  [weight_grads(): pl.pallas_call(functools.partial(weight_kernel, plan, bool(partial), fina...]
    ppermute x6, starting transfers between devices: 22 us -> 25.3 us  [over_z(): lax.ppermute(v, 'expert', [(i, i ^ 2 * k) for i in range(devices)])]
  transfers between devices with their start and end apart: 23 -> 23, of which waited for: 9 -> 10; matrix products, arithmetic and copies ran while one was open for 1% -> 2% of each run, Pallas kernels for 42% -> 42%
where the time goes in v3:
time: 130 us; the launch traced here: 129 us
  Pallas kernels  58.1 us (45%)
  starting transfers between devices  44.7 us (34%)
  waiting for transfers between devices  22.6 us (17%)
  other arithmetic  2.72 us (2%)
    pallas_call x4, Pallas kernels, experts(): pl.pallas_call(functools.partial(experts_kernel, layouts, share, hidden),...  40.7 us
    ppermute x6, starting transfers between devices, over_z(): lax.ppermute(v, 'expert', [(i, i ^ 2 * k) for i in range(devices)])  25.3 us
    ppermute x12, waiting for transfers between devices, over_dp(): lax.ppermute(v, 'dp', [(i, i ^ k) for i in range(groups)])  19.9 us
    ppermute x12, starting transfers between devices, over_dp(): lax.ppermute(v, 'dp', [(i, i ^ k) for i in range(groups)])  17.8 us
    pallas_call x2, Pallas kernels, weight_grads(): pl.pallas_call(functools.partial(weight_kernel, plan, bool(partial), fina...  12.6 us
    ppermute x5, waiting for transfers between devices, swap(): return lax.ppermute(v, 'expert', [(i, i ^ 1) for i in range(devices)])  2.66 us
  transfers between devices with their start and end apart: 23, of which 10 were waited for; matrix products, arithmetic and copies ran while one was open for 2% of the time, Pallas kernels for 42%

profile of v3, /device:TPU:0, one launch (start us, length us, event | category | flops | bytes accessed | tf_op | source)
XLA Modules:
  0.0 129.4 jit_solution(18201763376857358209)
XLA Ops:
  1.2 0.7 pad_add_fusion.routing_ref
  2.4 1.1 collective-permute-done.other_routing_ref
  3.6 2.2 %dispatch.1 = (bf16[144,2048]{1,0:T(8,128)(2,1)S(1)}, bf16[144,2048]{1,0:T(8,128)(2,1)S(1)}, bf16[144,2048]{1,0:T(8,128)(2,1)S(1)}, bf16[144,2048]{1,0:T(8,128)(2,1)S(1)}) custom-call(s32[4,128]{1,0:T(4,128)S(1)} %pad_add_fusion.routing_ref, s32[4,128]{1,0:T(4,128)S(1)} %collective-permute-done.other_routing_ref, bf16[128,2048]{1,0:T(8,128)(2,1)} %x_ref.1, ...), custom_call_target="tpu_custom_call" | custom-call | flops 603979776 | bytes 4456448 | tf_op jit(solution)/shard_map/dispatch/pallas_call | solution.py:151
  5.9 3.0 %collective-permute-start.3 = (bf16[144,2048]{1,0:T(8,128)(2,1)S(1)}, bf16[144,2048]{1,0:T(8,128)(2,1)S(1)}, u32[]{:S(2)}, u32[]{:S(2)}) collective-permute-start(bf16[144,2048]{1,0:T(8,128)(2,1)S(1)} %get-tuple-element.52), channel_id=1, source_target_pairs={{0,2},{1,3},{2,0},{3,1},{4,6},{5,7},{6,4},{7,5},{8,10},{9,11},{10,... | collective-permute-start | bytes 1769480 | tf_op jit(solution)/shard_map/ppermute | solution.py:351
  8.9 2.5 %collective-permute-start.4 = (bf16[144,2048]{1,0:T(8,128)(2,1)S(1)}, bf16[144,2048]{1,0:T(8,128)(2,1)S(1)}, u32[]{:S(2)}, u32[]{:S(2)}) collective-permute-start(bf16[144,2048]{1,0:T(8,128)(2,1)S(1)} %get-tuple-element.55), channel_id=1, source_target_pairs={{0,6},{1,7},{2,4},{3,5},{4,2},{5,3},{6,0},{7,1},{8,14},{9,15},{10,... | collective-permute-start | bytes 1769480 | tf_op jit(solution)/shard_map/ppermute | solution.py:351
  11.4 10.1 %experts.4 = (bf16[144,2048]{1,0:T(8,128)(2,1)S(1)}, bf16[72,4096]{1,0:T(8,128)(2,1)S(1)}, bf16[72,4608]{1,0:T(8,128)(2,1)S(1)}, bf16[72,4608]{1,0:T(8,128)(2,1)S(1)}) custom-call(bf16[144,2048]{1,0:T(8,128)(2,1)S(1)} %get-tuple-element.50.rows_ref, bf16[2048,1024]{1,0:T(8,128)(2,1)} %wg.7, bf16[2048,1024]{1,0:T(8,128)(2,1)} %wu.7, bf16[1024,2048]{1,0:T(8,128)(2,1)} %wd.7), custom_call_target="tpu_custom_call" | custom-call | flops 1811939328 | bytes 12582912 | tf_op jit(solution)/shard_map/experts/pallas_call | solution.py:261
  21.5 1.6 %collective-permute-start.7 = (bf16[72,4608]{1,0:T(8,128)(2,1)S(1)}, bf16[72,4608]{1,0:T(8,128)(2,1)S(1)}, u32[]{:S(2)}, u32[]{:S(2)}) collective-permute-start(bf16[72,4608]{1,0:T(8,128)(2,1)S(1)} %get-tuple-element.61), channel_id=1, source_target_pairs={{0,8},{8,0},{16,24},{24,16},{1,9},{9,1},{17,25},{25,17},{2,10},{10... | collective-permute-start | bytes 1990664 | tf_op jit(solution)/shard_map/ppermute | solution.py:354
  23.1 1.5 %collective-permute-start.8 = (bf16[72,4608]{1,0:T(8,128)(2,1)S(1)}, bf16[72,4608]{1,0:T(8,128)(2,1)S(1)}, u32[]{:S(2)}, u32[]{:S(2)}) collective-permute-start(bf16[72,4608]{1,0:T(8,128)(2,1)S(1)} %get-tuple-element.62), channel_id=1, source_target_pairs={{0,16},{8,24},{16,0},{24,8},{1,17},{9,25},{17,1},{25,9},{2,18},{10... | collective-permute-start | bytes 1990664 | tf_op jit(solution)/shard_map/ppermute | solution.py:354
  24.6 10.1 %experts.5 = (bf16[144,2048]{1,0:T(8,128)(2,1)S(1)}, bf16[72,4096]{1,0:T(8,128)(2,1)S(1)}, bf16[72,4608]{1,0:T(8,128)(2,1)S(1)}, bf16[72,4608]{1,0:T(8,128)(2,1)S(1)}) custom-call(bf16[144,2048]{1,0:T(8,128)(2,1)S(1)} %collective-permute-done.3.rows_ref, bf16[2048,1024]{1,0:T(8,128)(2,1)} %wg.7, bf16[2048,1024]{1,0:T(8,128)(2,1)} %wu.7, bf16[1024,2048]{1,0:T(8,128)(2,1)} %wd.7), custom_call_target="tpu_custom_call" | custom-call | flops 1811939328 | bytes 12582912 | tf_op jit(solution)/shard_map/experts/pallas_call | solution.py:261
  35.3 2.5 %collective-permute-start.6 = (bf16[144,2048]{1,0:T(8,128)(2,1)S(1)}, bf16[144,2048]{1,0:T(8,128)(2,1)S(1)}, u32[]{:S(2)}, u32[]{:S(2)}) collective-permute-start(bf16[144,2048]{1,0:T(8,128)(2,1)S(1)} %get-tuple-element.59), channel_id=1, source_target_pairs={{0,4},{1,5},{2,6},{3,7},{4,0},{5,1},{6,2},{7,3},{8,12},{9,13},{10,... | collective-permute-start | bytes 1769480 | tf_op jit(solution)/shard_map/ppermute | solution.py:351
  37.8 1.5 %collective-permute-start.10 = (bf16[72,4608]{1,0:T(8,128)(2,1)S(1)}, bf16[72,4608]{1,0:T(8,128)(2,1)S(1)}, u32[]{:S(2)}, u32[]{:S(2)}) collective-permute-start(bf16[72,4608]{1,0:T(8,128)(2,1)S(1)} %get-tuple-element.65), channel_id=1, source_target_pairs={{0,16},{8,24},{16,0},{24,8},{1,17},{9,25},{17,1},{25,9},{2,18},{10... | collective-permute-start | bytes 1990664 | tf_op jit(solution)/shard_map/ppermute | solution.py:354
  39.3 10.1 %experts.6 = (bf16[144,2048]{1,0:T(8,128)(2,1)S(1)}, bf16[72,4096]{1,0:T(8,128)(2,1)S(1)}, bf16[72,4608]{1,0:T(8,128)(2,1)S(1)}, bf16[72,4608]{1,0:T(8,128)(2,1)S(1)}) custom-call(bf16[144,2048]{1,0:T(8,128)(2,1)S(1)} %collective-permute-done.4.rows_ref, bf16[2048,1024]{1,0:T(8,128)(2,1)} %wg.7, bf16[2048,1024]{1,0:T(8,128)(2,1)} %wu.7, bf16[1024,2048]{1,0:T(8,128)(2,1)} %wd.7), custom_call_target="tpu_custom_call" | custom-call | flops 1811939328 | bytes 12582912 | tf_op jit(solution)/shard_map/experts/pallas_call | solution.py:261
  49.4 1.4 %collective-permute-start.15 = (bf16[72,4608]{1,0:T(8,128)(2,1)S(1)}, bf16[72,4608]{1,0:T(8,128)(2,1)S(1)}, u32[]{:S(2)}, u32[]{:S(2)}) collective-permute-start(bf16[72,4608]{1,0:T(8,128)(2,1)S(1)} %get-tuple-element.73), channel_id=1, source_target_pairs={{0,8},{8,0},{16,24},{24,16},{1,9},{9,1},{17,25},{25,17},{2,10},{10... | collective-permute-start | bytes 1990664 | tf_op jit(solution)/shard_map/ppermute | solution.py:354
  51.2 2.3 %collective-permute-done.9.refs_6_ = bf16[72,4608]{1,0:T(8,128)(2,1)S(1)} collective-permute-done((bf16[72,4608]{1,0:T(8,128)(2,1)S(1)}, bf16[72,4608]{1,0:T(8,128)(2,1)S(1)}, u32[]{:S(2)}, u32[]{:S(2)}) %collective-permute-start.9) | collective-permute-done | bytes 663584 | tf_op jit(solution)/shard_map/ppermute | solution.py:354
  53.5 10.8 %collective-permute-start.5 = (bf16[144,2048]{1,0:T(8,128)(2,1)S(1)}, bf16[144,2048]{1,0:T(8,128)(2,1)S(1)}, u32[]{:S(2)}, u32[]{:S(2)}) collective-permute-start(bf16[144,2048]{1,0:T(8,128)(2,1)S(1)} %get-tuple-element.58), channel_id=1, source_target_pairs={{0,2},{1,3},{2,0},{3,1},{4,6},{5,7},{6,4},{7,5},{8,10},{9,11},{10,... | collective-permute-start | bytes 1769480 | tf_op jit(solution)/shard_map/ppermute | solution.py:351
  64.4 1.6 %collective-permute-start.13 = (bf16[144,2048]{1,0:T(8,128)(2,1)S(1)}, bf16[144,2048]{1,0:T(8,128)(2,1)S(1)}, u32[]{:S(2)}, u32[]{:S(2)}) collective-permute-start(bf16[144,2048]{1,0:T(8,128)(2,1)S(1)} %pad_maximum_fusion), channel_id=1, source_target_pairs={{0,16},{8,24},{16,0},{24,8},{1,17},{9,25},{17,1},{25,9},{2,18},{10... | collective-permute-start | bytes 1769480 | tf_op jit(solution)/shard_map/ppermute | solution.py:354
  66.0 3.4 %collective-permute-start.12 = (bf16[144,2048]{1,0:T(8,128)(2,1)S(1)}, bf16[144,2048]{1,0:T(8,128)(2,1)S(1)}, u32[]{:S(2)}, u32[]{:S(2)}) collective-permute-start(bf16[144,2048]{1,0:T(8,128)(2,1)S(1)} %get-tuple-element.57), channel_id=1, source_target_pairs={{0,6},{1,7},{2,4},{3,5},{4,2},{5,3},{6,0},{7,1},{8,14},{9,15},{10,... | collective-permute-start | bytes 1769480 | tf_op jit(solution)/shard_map/ppermute | solution.py:351
  69.4 10.3 %experts.7 = (bf16[144,2048]{1,0:T(8,128)(2,1)S(1)}, bf16[72,4096]{1,0:T(8,128)(2,1)S(1)}, bf16[72,4608]{1,0:T(8,128)(2,1)S(1)}, bf16[72,4608]{1,0:T(8,128)(2,1)S(1)}) custom-call(bf16[144,2048]{1,0:T(8,128)(2,1)S(1)} %collective-permute-done.6.rows_ref, bf16[2048,1024]{1,0:T(8,128)(2,1)} %wg.7, bf16[2048,1024]{1,0:T(8,128)(2,1)} %wu.7, bf16[1024,2048]{1,0:T(8,128)(2,1)} %wd.7), custom_call_target="tpu_custom_call" | custom-call | flops 1811939328 | bytes 12582912 | tf_op jit(solution)/shard_map/experts/pallas_call | solution.py:261
  80.0 2.0 %collective-permute-start.14 = (bf16[144,2048]{1,0:T(8,128)(2,1)S(1)}, bf16[144,2048]{1,0:T(8,128)(2,1)S(1)}, u32[]{:S(2)}, u32[]{:S(2)}) collective-permute-start(bf16[144,2048]{1,0:T(8,128)(2,1)S(1)} %pad_maximum_fusion.1), channel_id=1, source_target_pairs={{0,8},{8,0},{16,24},{24,16},{1,9},{9,1},{17,25},{25,17},{2,10},{10... | collective-permute-start | bytes 1769480 | tf_op jit(solution)/shard_map/ppermute | solution.py:354
  82.0 3.2 %collective-permute-start.11 = (bf16[144,2048]{1,0:T(8,128)(2,1)S(1)}, bf16[144,2048]{1,0:T(8,128)(2,1)S(1)}, u32[]{:S(2)}, u32[]{:S(2)}) collective-permute-start(bf16[144,2048]{1,0:T(8,128)(2,1)S(1)} %get-tuple-element.68), channel_id=1, source_target_pairs={{0,4},{1,5},{2,6},{3,7},{4,0},{5,1},{6,2},{7,3},{8,12},{9,13},{10,... | collective-permute-start | bytes 1769480 | tf_op jit(solution)/shard_map/ppermute | solution.py:351
  85.2 5.4 %collective-permute-start.19 = (bf16[72,4608]{1,0:T(8,128)(2,1)S(1)}, bf16[72,4608]{1,0:T(8,128)(2,1)S(1)}, u32[]{:S(2)}, u32[]{:S(2)}) collective-permute-start(bf16[72,4608]{1,0:T(8,128)(2,1)S(1)} %get-tuple-element.82), channel_id=1, source_target_pairs={{0,16},{8,24},{16,0},{24,8},{1,17},{9,25},{17,1},{25,9},{2,18},{10... | collective-permute-start | bytes 1990664 | tf_op jit(solution)/shard_map/ppermute | solution.py:354
  90.7 7.0 %collective-permute-done.17.refs_6_ = bf16[72,4608]{1,0:T(8,128)(2,1)S(1)} collective-permute-done((bf16[72,4608]{1,0:T(8,128)(2,1)S(1)}, bf16[72,4608]{1,0:T(8,128)(2,1)S(1)}, u32[]{:S(2)}, u32[]{:S(2)}) %collective-permute-start.17) | collective-permute-done | bytes 663584 | tf_op jit(solution)/shard_map/ppermute | solution.py:354
  98.4 7.3 %collective-permute-done.14 = bf16[144,2048]{1,0:T(8,128)(2,1)S(1)} collective-permute-done((bf16[144,2048]{1,0:T(8,128)(2,1)S(1)}, bf16[144,2048]{1,0:T(8,128)(2,1)S(1)}, u32[]{:S(2)}, u32[]{:S(2)}) %collective-permute-start.14) | collective-permute-done | bytes 589856 | tf_op jit(solution)/shard_map/ppermute | solution.py:354
  106.5 1.1 collective-permute-start.20
  107.7 7.2 %weight_grads_early.1 = (f32[512,1024]{1,0:T(8,128)}, f32[512,1024]{1,0:T(8,128)}, f32[1024,512]{1,0:T(8,128)}) custom-call(bf16[72,4096]{1,0:T(8,128)(2,1)S(1)} %get-tuple-element.60.refs_0_, bf16[72,4608]{1,0:T(8,128)(2,1)S(1)} %collective-permute-done.7.refs_1_, bf16[72,4608]{1,0:T(8,128)(2,1)S(1)} %copy-done.2, ...), custom_call_target="tpu_custom_call" | custom-call | flops 2491416576 | bytes 12779520 | tf_op jit(solution)/shard_map/weight_grads_early/pallas_call | solution.py:329
  115.2 2.2 %collective-permute-done.20 = bf16[144,2048]{1,0:T(8,128)(2,1)S(1)} collective-permute-done((bf16[144,2048]{1,0:T(8,128)(2,1)S(1)}, bf16[144,2048]{1,0:T(8,128)(2,1)S(1)}, u32[]{:S(2)}, u32[]{:S(2)}) %collective-permute-start.20) | collective-permute-done | bytes 589856 | tf_op jit(solution)/shard_map/ppermute | solution.py:354
  117.5 5.4 %weight_grads.1 = (f32[512,1024]{1,0:T(8,128)}, f32[512,1024]{1,0:T(8,128)}, f32[1024,512]{1,0:T(8,128)}) custom-call(f32[512,1024]{1,0:T(8,128)S(1)} %copy-done, f32[512,1024]{1,0:T(8,128)} %get-tuple-element.76.refs_1_, f32[1024,512]{1,0:T(8,128)} %get-tuple-element.77.refs_2_, bf16[72,2048]{1,0:T(8,128)(2,1)S(1)} %get-tuple-element.98.refs_3_, ...), custom_call_target="tpu_custom_call" | custom-call | flops 1132462080 | bytes 9240576 | tf_op jit(solution)/shard_map/weight_grads/pallas_call | solution.py:329
  123.0 1.0 combine_grad.1
  124.0 1.6 %combine_mixed.1 = (f32[128,2048]{1,0:T(8,128)S(1)}, f32[128,2048]{1,0:T(8,128)S(1)}) custom-call(s32[4,128]{1,0:T(4,128)S(1)} %pad_add_fusion.routing_ref, s32[4,128]{1,0:T(4,128)S(1)} %collective-permute-done.other_routing_ref, bf16[144,2048]{1,0:T(8,128)(2,1)S(1)} %get-tuple-element.87.refs_0_, bf16[144,2048]{1,0:T(8,128)(2,1)S(1)} %collective-permute-done.5.refs_1_, ...), custom_call_target="tpu_custom_call" | custom-call | flops 301989888 | bytes 3276800 | tf_op jit(solution)/shard_map/combine_mixed/pallas_call | solution.py:193
  126.7 0.9 add_convert_fusion
  127.6 0.9 collective-permute-done.21
  128.5 0.9 add_convert_fusion.1
  (55 shorter events, 5.5 us)
Async XLA Ops:
  0.6 2.8 %collective-permute-start.1 = (bf16[128,2048]{1,0:T(8,128)(2,1)}, bf16[128,2048]{1,0:T(8,128)(2,1)S(1)}, u32[]{:S(2)}, u32[]{:S(2)}) collective-permute-start(bf16[128,2048]{1,0:T(8,128)(2,1)} %x_ref.1), channel_id=1, source_target_pairs={{0,1},{1,0},{2,3},{3,2},{4,5},{5,4},{6,7},{7,6},{8,9},{9,8},{10,11... | collective-permute-start | bytes 1572872 | tf_op jit(solution)/shard_map/ppermute | solution.py:348
  1.2 2.5 %collective-permute-start.2 = (bf16[128,2048]{1,0:T(8,128)(2,1)}, bf16[128,2048]{1,0:T(8,128)(2,1)S(1)}, u32[]{:S(2)}, u32[]{:S(2)}) collective-permute-start(bf16[128,2048]{1,0:T(8,128)(2,1)} %dy_ref.1), channel_id=1, source_target_pairs={{0,1},{1,0},{2,3},{3,2},{4,5},{5,4},{6,7},{7,6},{8,9},{9,8},{10,11... | collective-permute-start | bytes 1572872 | tf_op jit(solution)/shard_map/ppermute | solution.py:348
  1.9 1.5 %collective-permute-start = (s32[4,128]{1,0:T(4,128)S(1)}, s32[4,128]{1,0:T(4,128)S(1)}, u32[]{:S(2)}, u32[]{:S(2)}) collective-permute-start(s32[4,128]{1,0:T(4,128)S(1)} %pad_add_fusion.routing_ref), channel_id=1, source_target_pairs={{0,1},{1,0},{2,3},{3,2},{4,5},{5,4},{6,7},{7,6},{8,9},{9,8},{10,11... | collective-permute-start | bytes 6152 | tf_op jit(solution)/shard_map/ppermute | solution.py:348
  5.9 18.7 %collective-permute-start.3 = (bf16[144,2048]{1,0:T(8,128)(2,1)S(1)}, bf16[144,2048]{1,0:T(8,128)(2,1)S(1)}, u32[]{:S(2)}, u32[]{:S(2)}) collective-permute-start(bf16[144,2048]{1,0:T(8,128)(2,1)S(1)} %get-tuple-element.52), channel_id=1, source_target_pairs={{0,2},{1,3},{2,0},{3,1},{4,6},{5,7},{6,4},{7,5},{8,10},{9,11},{10,... | collective-permute-start | bytes 1769480 | tf_op jit(solution)/shard_map/ppermute | solution.py:351
  8.9 28.9 %collective-permute-start.4 = (bf16[144,2048]{1,0:T(8,128)(2,1)S(1)}, bf16[144,2048]{1,0:T(8,128)(2,1)S(1)}, u32[]{:S(2)}, u32[]{:S(2)}) collective-permute-start(bf16[144,2048]{1,0:T(8,128)(2,1)S(1)} %get-tuple-element.55), channel_id=1, source_target_pairs={{0,6},{1,7},{2,4},{3,5},{4,2},{5,3},{6,0},{7,1},{8,14},{9,15},{10,... | collective-permute-start | bytes 1769480 | tf_op jit(solution)/shard_map/ppermute | solution.py:351
  21.5 27.9 %collective-permute-start.7 = (bf16[72,4608]{1,0:T(8,128)(2,1)S(1)}, bf16[72,4608]{1,0:T(8,128)(2,1)S(1)}, u32[]{:S(2)}, u32[]{:S(2)}) collective-permute-start(bf16[72,4608]{1,0:T(8,128)(2,1)S(1)} %get-tuple-element.61), channel_id=1, source_target_pairs={{0,8},{8,0},{16,24},{24,16},{1,9},{9,1},{17,25},{25,17},{2,10},{10... | collective-permute-start | bytes 1990664 | tf_op jit(solution)/shard_map/ppermute | solution.py:354
  23.1 26.4 %collective-permute-start.8 = (bf16[72,4608]{1,0:T(8,128)(2,1)S(1)}, bf16[72,4608]{1,0:T(8,128)(2,1)S(1)}, u32[]{:S(2)}, u32[]{:S(2)}) collective-permute-start(bf16[72,4608]{1,0:T(8,128)(2,1)S(1)} %get-tuple-element.62), channel_id=1, source_target_pairs={{0,16},{8,24},{16,0},{24,8},{1,17},{9,25},{17,1},{25,9},{2,18},{10... | collective-permute-start | bytes 1990664 | tf_op jit(solution)/shard_map/ppermute | solution.py:354
  34.7 18.8 %collective-permute-start.9 = (bf16[72,4608]{1,0:T(8,128)(2,1)S(1)}, bf16[72,4608]{1,0:T(8,128)(2,1)S(1)}, u32[]{:S(2)}, u32[]{:S(2)}) collective-permute-start(bf16[72,4608]{1,0:T(8,128)(2,1)S(1)} %get-tuple-element.64), channel_id=1, source_target_pairs={{0,8},{8,0},{16,24},{24,16},{1,9},{9,1},{17,25},{25,17},{2,10},{10... | collective-permute-start | bytes 1990664 | tf_op jit(solution)/shard_map/ppermute | solution.py:354
  35.3 29.1 %collective-permute-start.6 = (bf16[144,2048]{1,0:T(8,128)(2,1)S(1)}, bf16[144,2048]{1,0:T(8,128)(2,1)S(1)}, u32[]{:S(2)}, u32[]{:S(2)}) collective-permute-start(bf16[144,2048]{1,0:T(8,128)(2,1)S(1)} %get-tuple-element.59), channel_id=1, source_target_pairs={{0,4},{1,5},{2,6},{3,7},{4,0},{5,1},{6,2},{7,3},{8,12},{9,13},{10,... | collective-permute-start | bytes 1769480 | tf_op jit(solution)/shard_map/ppermute | solution.py:351
  37.8 28.2 %collective-permute-start.10 = (bf16[72,4608]{1,0:T(8,128)(2,1)S(1)}, bf16[72,4608]{1,0:T(8,128)(2,1)S(1)}, u32[]{:S(2)}, u32[]{:S(2)}) collective-permute-start(bf16[72,4608]{1,0:T(8,128)(2,1)S(1)} %get-tuple-element.65), channel_id=1, source_target_pairs={{0,16},{8,24},{16,0},{24,8},{1,17},{9,25},{17,1},{25,9},{2,18},{10... | collective-permute-start | bytes 1990664 | tf_op jit(solution)/shard_map/ppermute | solution.py:354
  49.4 16.5 %copy-start.1 = (bf16[72,4608]{1,0:T(8,128)(2,1)}, bf16[72,4608]{1,0:T(8,128)(2,1)S(1)}, u32[]{:S(2)}) copy-start(bf16[72,4608]{1,0:T(8,128)(2,1)S(1)} %collective-permute-done.8.refs_2_) | copy-start | bytes 1990660
  49.4 30.3 %collective-permute-start.15 = (bf16[72,4608]{1,0:T(8,128)(2,1)S(1)}, bf16[72,4608]{1,0:T(8,128)(2,1)S(1)}, u32[]{:S(2)}, u32[]{:S(2)}) collective-permute-start(bf16[72,4608]{1,0:T(8,128)(2,1)S(1)} %get-tuple-element.73), channel_id=1, source_target_pairs={{0,8},{8,0},{16,24},{24,16},{1,9},{9,1},{17,25},{25,17},{2,10},{10... | collective-permute-start | bytes 1990664 | tf_op jit(solution)/shard_map/ppermute | solution.py:354
  50.9 28.9 %collective-permute-start.16 = (bf16[72,4608]{1,0:T(8,128)(2,1)S(1)}, bf16[72,4608]{1,0:T(8,128)(2,1)S(1)}, u32[]{:S(2)}, u32[]{:S(2)}) collective-permute-start(bf16[72,4608]{1,0:T(8,128)(2,1)S(1)} %get-tuple-element.74), channel_id=1, source_target_pairs={{0,16},{8,24},{16,0},{24,8},{1,17},{9,25},{17,1},{25,9},{2,18},{10... | collective-permute-start | bytes 1990664 | tf_op jit(solution)/shard_map/ppermute | solution.py:354
  53.5 28.5 %collective-permute-start.5 = (bf16[144,2048]{1,0:T(8,128)(2,1)S(1)}, bf16[144,2048]{1,0:T(8,128)(2,1)S(1)}, u32[]{:S(2)}, u32[]{:S(2)}) collective-permute-start(bf16[144,2048]{1,0:T(8,128)(2,1)S(1)} %get-tuple-element.58), channel_id=1, source_target_pairs={{0,2},{1,3},{2,0},{3,1},{4,6},{5,7},{6,4},{7,5},{8,10},{9,11},{10,... | collective-permute-start | bytes 1769480 | tf_op jit(solution)/shard_map/ppermute | solution.py:351
  64.4 20.8 %collective-permute-start.13 = (bf16[144,2048]{1,0:T(8,128)(2,1)S(1)}, bf16[144,2048]{1,0:T(8,128)(2,1)S(1)}, u32[]{:S(2)}, u32[]{:S(2)}) collective-permute-start(bf16[144,2048]{1,0:T(8,128)(2,1)S(1)} %pad_maximum_fusion), channel_id=1, source_target_pairs={{0,16},{8,24},{16,0},{24,8},{1,17},{9,25},{17,1},{25,9},{2,18},{10... | collective-permute-start | bytes 1769480 | tf_op jit(solution)/shard_map/ppermute | solution.py:354
  66.0 57.0 %collective-permute-start.12 = (bf16[144,2048]{1,0:T(8,128)(2,1)S(1)}, bf16[144,2048]{1,0:T(8,128)(2,1)S(1)}, u32[]{:S(2)}, u32[]{:S(2)}) collective-permute-start(bf16[144,2048]{1,0:T(8,128)(2,1)S(1)} %get-tuple-element.57), channel_id=1, source_target_pairs={{0,6},{1,7},{2,4},{3,5},{4,2},{5,3},{6,0},{7,1},{8,14},{9,15},{10,... | collective-permute-start | bytes 1769480 | tf_op jit(solution)/shard_map/ppermute | solution.py:351
  69.4 10.6 %slice-start = ((bf16[72,4608]{1,0:T(8,128)(2,1)}), bf16[72,2048]{1,0:T(8,128)(2,1)S(1)}, s32[]{:S(2)}) async-start(bf16[72,4608]{1,0:T(8,128)(2,1)} %copy-done.1), calls=%async_computation | async-start | bytes 589824 | tf_op jit(solution)/shard_map/slice | solution.py:367
  79.8 5.5 %copy-start.4 = (bf16[72,4608]{1,0:T(8,128)(2,1)}, bf16[72,4608]{1,0:T(8,128)(2,1)S(1)}, u32[]{:S(2)}) copy-start(bf16[72,4608]{1,0:T(8,128)(2,1)S(1)} %collective-permute-done.15.refs_11_) | copy-start | bytes 1990660
  79.8 5.4 %copy-start.3 = (bf16[72,4608]{1,0:T(8,128)(2,1)}, bf16[72,4608]{1,0:T(8,128)(2,1)S(1)}, u32[]{:S(2)}) copy-start(bf16[72,4608]{1,0:T(8,128)(2,1)S(1)} %collective-permute-done.16.refs_12_) | copy-start | bytes 1990660
  79.8 17.9 %collective-permute-start.17 = (bf16[72,4608]{1,0:T(8,128)(2,1)S(1)}, bf16[72,4608]{1,0:T(8,128)(2,1)S(1)}, u32[]{:S(2)}, u32[]{:S(2)}) collective-permute-start(bf16[72,4608]{1,0:T(8,128)(2,1)S(1)} %get-tuple-element.81), channel_id=1, source_target_pairs={{0,8},{8,0},{16,24},{24,16},{1,9},{9,1},{17,25},{25,17},{2,10},{10... | collective-permute-start | bytes 1990664 | tf_op jit(solution)/shard_map/ppermute | solution.py:354
  80.0 25.7 %collective-permute-start.14 = (bf16[144,2048]{1,0:T(8,128)(2,1)S(1)}, bf16[144,2048]{1,0:T(8,128)(2,1)S(1)}, u32[]{:S(2)}, u32[]{:S(2)}) collective-permute-start(bf16[144,2048]{1,0:T(8,128)(2,1)S(1)} %pad_maximum_fusion.1), channel_id=1, source_target_pairs={{0,8},{8,0},{16,24},{24,16},{1,9},{9,1},{17,25},{25,17},{2,10},{10... | collective-permute-start | bytes 1769480 | tf_op jit(solution)/shard_map/ppermute | solution.py:354
  82.0 40.9 %collective-permute-start.11 = (bf16[144,2048]{1,0:T(8,128)(2,1)S(1)}, bf16[144,2048]{1,0:T(8,128)(2,1)S(1)}, u32[]{:S(2)}, u32[]{:S(2)}) collective-permute-start(bf16[144,2048]{1,0:T(8,128)(2,1)S(1)} %get-tuple-element.68), channel_id=1, source_target_pairs={{0,4},{1,5},{2,6},{3,7},{4,0},{5,1},{6,2},{7,3},{8,12},{9,13},{10,... | collective-permute-start | bytes 1769480 | tf_op jit(solution)/shard_map/ppermute | solution.py:351
  85.2 12.5 %slice-start.2 = ((bf16[72,4608]{1,0:T(8,128)(2,1)}), bf16[72,2048]{1,0:T(8,128)(2,1)S(1)}, s32[]{:S(2)}) async-start(bf16[72,4608]{1,0:T(8,128)(2,1)} %copy-done.4), calls=%async_computation.2 | async-start | bytes 589824 | tf_op jit(solution)/shard_map/slice | solution.py:367
  85.2 21.2 %collective-permute-start.19 = (bf16[72,4608]{1,0:T(8,128)(2,1)S(1)}, bf16[72,4608]{1,0:T(8,128)(2,1)S(1)}, u32[]{:S(2)}, u32[]{:S(2)}) collective-permute-start(bf16[72,4608]{1,0:T(8,128)(2,1)S(1)} %get-tuple-element.82), channel_id=1, source_target_pairs={{0,16},{8,24},{16,0},{24,8},{1,17},{9,25},{17,1},{25,9},{2,18},{10... | collective-permute-start | bytes 1990664 | tf_op jit(solution)/shard_map/ppermute | solution.py:354
  97.7 8.7 %slice-start.1 = ((bf16[72,4608]{1,0:T(8,128)(2,1)}), bf16[72,2048]{1,0:T(8,128)(2,1)S(1)}, s32[]{:S(2)}) async-start(bf16[72,4608]{1,0:T(8,128)(2,1)} %copy-done.3), calls=%async_computation.1 | async-start | bytes 589824 | tf_op jit(solution)/shard_map/slice | solution.py:367
  97.8 17.4 %collective-permute-start.18 = (bf16[144,2048]{1,0:T(8,128)(2,1)S(1)}, bf16[144,2048]{1,0:T(8,128)(2,1)S(1)}, u32[]{:S(2)}, u32[]{:S(2)}) collective-permute-start(bf16[144,2048]{1,0:T(8,128)(2,1)S(1)} %pad_maximum_fusion.2), channel_id=1, source_target_pairs={{0,16},{8,24},{16,0},{24,8},{1,17},{9,25},{17,1},{25,9},{2,18},{10... | collective-permute-start | bytes 1769480 | tf_op jit(solution)/shard_map/ppermute | solution.py:354
  105.7 1.9 %copy-start.2 = (bf16[72,4608]{1,0:T(8,128)(2,1)S(1)}, bf16[72,4608]{1,0:T(8,128)(2,1)}, u32[]{:S(2)}) copy-start(bf16[72,4608]{1,0:T(8,128)(2,1)} %copy-done.1) | copy-start | bytes 1990660
  106.5 10.9 %collective-permute-start.20 = (bf16[144,2048]{1,0:T(8,128)(2,1)S(1)}, bf16[144,2048]{1,0:T(8,128)(2,1)S(1)}, u32[]{:S(2)}, u32[]{:S(2)}) collective-permute-start(bf16[144,2048]{1,0:T(8,128)(2,1)S(1)} %pad_maximum_fusion.3), channel_id=1, source_target_pairs={{0,8},{8,0},{16,24},{24,16},{1,9},{9,1},{17,25},{25,17},{2,10},{10... | collective-permute-start | bytes 1769480 | tf_op jit(solution)/shard_map/ppermute | solution.py:354
  114.8 2.6 %copy-start = (f32[512,1024]{1,0:T(8,128)S(1)}, f32[512,1024]{1,0:T(8,128)}, u32[]{:S(2)}) copy-start(f32[512,1024]{1,0:T(8,128)} %get-tuple-element.75.refs_0_) | copy-start | bytes 6291460
  123.9 2.7 %collective-permute-start.22 = (f32[128,2048]{1,0:T(8,128)S(1)}, f32[128,2048]{1,0:T(8,128)S(1)}, u32[]{:S(2)}, u32[]{:S(2)}) collective-permute-start(f32[128,2048]{1,0:T(8,128)S(1)} %get-tuple-element.94), channel_id=1, source_target_pairs={{0,1},{1,0},{2,3},{3,2},{4,5},{5,4},{6,7},{7,6},{8,9},{9,8},{10,11... | collective-permute-start | bytes 3145736 | tf_op jit(solution)/shard_map/ppermute | solution.py:348
  125.6 2.8 %collective-permute-start.21 = (f32[128,2048]{1,0:T(8,128)S(1)}, f32[128,2048]{1,0:T(8,128)S(1)}, u32[]{:S(2)}, u32[]{:S(2)}) collective-permute-start(f32[128,2048]{1,0:T(8,128)S(1)} %get-tuple-element.92), channel_id=1, source_target_pairs={{0,1},{1,0},{2,3},{3,2},{4,5},{5,4},{6,7},{7,6},{8,9},{9,8},{10,11... | collective-permute-start | bytes 3145736 | tf_op jit(solution)/shard_map/ppermute | solution.py:348

commit v4 on v3

--- a/solution.py
+++ b/solution.py
@@ -184,7 +184,7 @@
         if scaled:
             summed = (summed + dot(low, rows, ((0,), (0,)))) / 1024.0
         own_ref[:, col : col + step] = summed[:tok]
-        other_ref[:, col : col + step] = summed[tok:]
+        other_ref[:, col : col + step] = summed[tok:].astype(jnp.bfloat16)
 
 
 def combine(routing, other_routing, backs, tiles, scaled):
@@ -192,7 +192,7 @@
     tok, width = routing.shape[1], backs[0].shape[1]
     return pl.pallas_call(
         functools.partial(combine_kernel, chips, tiles, scaled),
-        out_shape=[jax.ShapeDtypeStruct((tok, width), jnp.float32)] * 2,
+        out_shape=[jax.ShapeDtypeStruct((tok, width), kind) for kind in (jnp.float32, jnp.bfloat16)],
         in_specs=[VMEM] * (2 + chips),
         out_specs=[VMEM] * 2,
         compiler_params=params(24),

time: 130 us -> 129 us (level)
  transfers between devices with their start and end apart: 23 -> 23, of which waited for: 10 -> 9; matrix products, arithmetic and copies ran while one was open for 2% -> 2% of each run, Pallas kernels for 42% -> 43%
where the time goes in v4:
time: 129 us
  Pallas kernels  58.1 us (45%)
  starting transfers between devices  44.7 us (35%)
  waiting for transfers between devices  21.8 us (17%)
  other arithmetic  2.7 us (2%)
    pallas_call x4, Pallas kernels, experts(): pl.pallas_call(functools.partial(experts_kernel, layouts, share, hidden),...  40.7 us
    ppermute x6, starting transfers between devices, over_z(): lax.ppermute(v, 'expert', [(i, i ^ 2 * k) for i in range(devices)])  25.3 us
    ppermute x12, waiting for transfers between devices, over_dp(): lax.ppermute(v, 'dp', [(i, i ^ k) for i in range(groups)])  19.9 us
    ppermute x12, starting transfers between devices, over_dp(): lax.ppermute(v, 'dp', [(i, i ^ k) for i in range(groups)])  17.8 us
    pallas_call x2, Pallas kernels, weight_grads(): pl.pallas_call(functools.partial(weight_kernel, plan, bool(partial), fina...  12.6 us
  transfers between devices with their start and end apart: 23, of which 9 were waited for; matrix products, arithmetic and copies ran while one was open for 2% of the time, Pallas kernels for 43%

profile of v4, /device:TPU:0, one launch (start us, length us, event | category | flops | bytes accessed | tf_op | source)
XLA Modules:
  0.0 128.6 jit_solution(15017130639846696848)
XLA Ops:
  1.2 0.7 pad_add_fusion.routing_ref
  2.4 1.1 collective-permute-done.other_routing_ref
  3.6 2.2 %dispatch.1 = (bf16[144,2048]{1,0:T(8,128)(2,1)S(1)}, bf16[144,2048]{1,0:T(8,128)(2,1)S(1)}, bf16[144,2048]{1,0:T(8,128)(2,1)S(1)}, bf16[144,2048]{1,0:T(8,128)(2,1)S(1)}) custom-call(s32[4,128]{1,0:T(4,128)S(1)} %pad_add_fusion.routing_ref, s32[4,128]{1,0:T(4,128)S(1)} %collective-permute-done.other_routing_ref, bf16[128,2048]{1,0:T(8,128)(2,1)} %x_ref.1, ...), custom_call_target="tpu_custom_call" | custom-call | flops 603979776 | bytes 4456448 | tf_op jit(solution)/shard_map/dispatch/pallas_call | solution.py:151
  5.9 3.0 %collective-permute-start.3 = (bf16[144,2048]{1,0:T(8,128)(2,1)S(1)}, bf16[144,2048]{1,0:T(8,128)(2,1)S(1)}, u32[]{:S(2)}, u32[]{:S(2)}) collective-permute-start(bf16[144,2048]{1,0:T(8,128)(2,1)S(1)} %get-tuple-element.52), channel_id=1, source_target_pairs={{0,2},{1,3},{2,0},{3,1},{4,6},{5,7},{6,4},{7,5},{8,10},{9,11},{10,... | collective-permute-start | bytes 1769480 | tf_op jit(solution)/shard_map/ppermute | solution.py:351
  8.9 2.5 %collective-permute-start.4 = (bf16[144,2048]{1,0:T(8,128)(2,1)S(1)}, bf16[144,2048]{1,0:T(8,128)(2,1)S(1)}, u32[]{:S(2)}, u32[]{:S(2)}) collective-permute-start(bf16[144,2048]{1,0:T(8,128)(2,1)S(1)} %get-tuple-element.55), channel_id=1, source_target_pairs={{0,6},{1,7},{2,4},{3,5},{4,2},{5,3},{6,0},{7,1},{8,14},{9,15},{10,... | collective-permute-start | bytes 1769480 | tf_op jit(solution)/shard_map/ppermute | solution.py:351
  11.4 10.1 %experts.4 = (bf16[144,2048]{1,0:T(8,128)(2,1)S(1)}, bf16[72,4096]{1,0:T(8,128)(2,1)S(1)}, bf16[72,4608]{1,0:T(8,128)(2,1)S(1)}, bf16[72,4608]{1,0:T(8,128)(2,1)S(1)}) custom-call(bf16[144,2048]{1,0:T(8,128)(2,1)S(1)} %get-tuple-element.50.rows_ref, bf16[2048,1024]{1,0:T(8,128)(2,1)} %wg.7, bf16[2048,1024]{1,0:T(8,128)(2,1)} %wu.7, bf16[1024,2048]{1,0:T(8,128)(2,1)} %wd.7), custom_call_target="tpu_custom_call" | custom-call | flops 1811939328 | bytes 12582912 | tf_op jit(solution)/shard_map/experts/pallas_call | solution.py:261
  21.5 1.6 %collective-permute-start.7 = (bf16[72,4608]{1,0:T(8,128)(2,1)S(1)}, bf16[72,4608]{1,0:T(8,128)(2,1)S(1)}, u32[]{:S(2)}, u32[]{:S(2)}) collective-permute-start(bf16[72,4608]{1,0:T(8,128)(2,1)S(1)} %get-tuple-element.61), channel_id=1, source_target_pairs={{0,8},{8,0},{16,24},{24,16},{1,9},{9,1},{17,25},{25,17},{2,10},{10... | collective-permute-start | bytes 1990664 | tf_op jit(solution)/shard_map/ppermute | solution.py:354
  23.1 1.5 %collective-permute-start.8 = (bf16[72,4608]{1,0:T(8,128)(2,1)S(1)}, bf16[72,4608]{1,0:T(8,128)(2,1)S(1)}, u32[]{:S(2)}, u32[]{:S(2)}) collective-permute-start(bf16[72,4608]{1,0:T(8,128)(2,1)S(1)} %get-tuple-element.62), channel_id=1, source_target_pairs={{0,16},{8,24},{16,0},{24,8},{1,17},{9,25},{17,1},{25,9},{2,18},{10... | collective-permute-start | bytes 1990664 | tf_op jit(solution)/shard_map/ppermute | solution.py:354
  24.6 10.1 %experts.5 = (bf16[144,2048]{1,0:T(8,128)(2,1)S(1)}, bf16[72,4096]{1,0:T(8,128)(2,1)S(1)}, bf16[72,4608]{1,0:T(8,128)(2,1)S(1)}, bf16[72,4608]{1,0:T(8,128)(2,1)S(1)}) custom-call(bf16[144,2048]{1,0:T(8,128)(2,1)S(1)} %collective-permute-done.3.rows_ref, bf16[2048,1024]{1,0:T(8,128)(2,1)} %wg.7, bf16[2048,1024]{1,0:T(8,128)(2,1)} %wu.7, bf16[1024,2048]{1,0:T(8,128)(2,1)} %wd.7), custom_call_target="tpu_custom_call" | custom-call | flops 1811939328 | bytes 12582912 | tf_op jit(solution)/shard_map/experts/pallas_call | solution.py:261
  35.3 2.5 %collective-permute-start.6 = (bf16[144,2048]{1,0:T(8,128)(2,1)S(1)}, bf16[144,2048]{1,0:T(8,128)(2,1)S(1)}, u32[]{:S(2)}, u32[]{:S(2)}) collective-permute-start(bf16[144,2048]{1,0:T(8,128)(2,1)S(1)} %get-tuple-element.59), channel_id=1, source_target_pairs={{0,4},{1,5},{2,6},{3,7},{4,0},{5,1},{6,2},{7,3},{8,12},{9,13},{10,... | collective-permute-start | bytes 1769480 | tf_op jit(solution)/shard_map/ppermute | solution.py:351
  37.8 1.5 %collective-permute-start.10 = (bf16[72,4608]{1,0:T(8,128)(2,1)S(1)}, bf16[72,4608]{1,0:T(8,128)(2,1)S(1)}, u32[]{:S(2)}, u32[]{:S(2)}) collective-permute-start(bf16[72,4608]{1,0:T(8,128)(2,1)S(1)} %get-tuple-element.65), channel_id=1, source_target_pairs={{0,16},{8,24},{16,0},{24,8},{1,17},{9,25},{17,1},{25,9},{2,18},{10... | collective-permute-start | bytes 1990664 | tf_op jit(solution)/shard_map/ppermute | solution.py:354
  39.3 10.1 %experts.6 = (bf16[144,2048]{1,0:T(8,128)(2,1)S(1)}, bf16[72,4096]{1,0:T(8,128)(2,1)S(1)}, bf16[72,4608]{1,0:T(8,128)(2,1)S(1)}, bf16[72,4608]{1,0:T(8,128)(2,1)S(1)}) custom-call(bf16[144,2048]{1,0:T(8,128)(2,1)S(1)} %collective-permute-done.4.rows_ref, bf16[2048,1024]{1,0:T(8,128)(2,1)} %wg.7, bf16[2048,1024]{1,0:T(8,128)(2,1)} %wu.7, bf16[1024,2048]{1,0:T(8,128)(2,1)} %wd.7), custom_call_target="tpu_custom_call" | custom-call | flops 1811939328 | bytes 12582912 | tf_op jit(solution)/shard_map/experts/pallas_call | solution.py:261
  49.4 1.4 %collective-permute-start.15 = (bf16[72,4608]{1,0:T(8,128)(2,1)S(1)}, bf16[72,4608]{1,0:T(8,128)(2,1)S(1)}, u32[]{:S(2)}, u32[]{:S(2)}) collective-permute-start(bf16[72,4608]{1,0:T(8,128)(2,1)S(1)} %get-tuple-element.73), channel_id=1, source_target_pairs={{0,8},{8,0},{16,24},{24,16},{1,9},{9,1},{17,25},{25,17},{2,10},{10... | collective-permute-start | bytes 1990664 | tf_op jit(solution)/shard_map/ppermute | solution.py:354
  51.2 2.3 %collective-permute-done.9.refs_6_ = bf16[72,4608]{1,0:T(8,128)(2,1)S(1)} collective-permute-done((bf16[72,4608]{1,0:T(8,128)(2,1)S(1)}, bf16[72,4608]{1,0:T(8,128)(2,1)S(1)}, u32[]{:S(2)}, u32[]{:S(2)}) %collective-permute-start.9) | collective-permute-done | bytes 663584 | tf_op jit(solution)/shard_map/ppermute | solution.py:354
  53.5 10.8 %collective-permute-start.5 = (bf16[144,2048]{1,0:T(8,128)(2,1)S(1)}, bf16[144,2048]{1,0:T(8,128)(2,1)S(1)}, u32[]{:S(2)}, u32[]{:S(2)}) collective-permute-start(bf16[144,2048]{1,0:T(8,128)(2,1)S(1)} %get-tuple-element.58), channel_id=1, source_target_pairs={{0,2},{1,3},{2,0},{3,1},{4,6},{5,7},{6,4},{7,5},{8,10},{9,11},{10,... | collective-permute-start | bytes 1769480 | tf_op jit(solution)/shard_map/ppermute | solution.py:351
  64.4 1.6 %collective-permute-start.13 = (bf16[144,2048]{1,0:T(8,128)(2,1)S(1)}, bf16[144,2048]{1,0:T(8,128)(2,1)S(1)}, u32[]{:S(2)}, u32[]{:S(2)}) collective-permute-start(bf16[144,2048]{1,0:T(8,128)(2,1)S(1)} %pad_maximum_fusion), channel_id=1, source_target_pairs={{0,16},{8,24},{16,0},{24,8},{1,17},{9,25},{17,1},{25,9},{2,18},{10... | collective-permute-start | bytes 1769480 | tf_op jit(solution)/shard_map/ppermute | solution.py:354
  66.0 3.4 %collective-permute-start.12 = (bf16[144,2048]{1,0:T(8,128)(2,1)S(1)}, bf16[144,2048]{1,0:T(8,128)(2,1)S(1)}, u32[]{:S(2)}, u32[]{:S(2)}) collective-permute-start(bf16[144,2048]{1,0:T(8,128)(2,1)S(1)} %get-tuple-element.57), channel_id=1, source_target_pairs={{0,6},{1,7},{2,4},{3,5},{4,2},{5,3},{6,0},{7,1},{8,14},{9,15},{10,... | collective-permute-start | bytes 1769480 | tf_op jit(solution)/shard_map/ppermute | solution.py:351
  69.4 10.3 %experts.7 = (bf16[144,2048]{1,0:T(8,128)(2,1)S(1)}, bf16[72,4096]{1,0:T(8,128)(2,1)S(1)}, bf16[72,4608]{1,0:T(8,128)(2,1)S(1)}, bf16[72,4608]{1,0:T(8,128)(2,1)S(1)}) custom-call(bf16[144,2048]{1,0:T(8,128)(2,1)S(1)} %collective-permute-done.6.rows_ref, bf16[2048,1024]{1,0:T(8,128)(2,1)} %wg.7, bf16[2048,1024]{1,0:T(8,128)(2,1)} %wu.7, bf16[1024,2048]{1,0:T(8,128)(2,1)} %wd.7), custom_call_target="tpu_custom_call" | custom-call | flops 1811939328 | bytes 12582912 | tf_op jit(solution)/shard_map/experts/pallas_call | solution.py:261
  80.0 2.0 %collective-permute-start.14 = (bf16[144,2048]{1,0:T(8,128)(2,1)S(1)}, bf16[144,2048]{1,0:T(8,128)(2,1)S(1)}, u32[]{:S(2)}, u32[]{:S(2)}) collective-permute-start(bf16[144,2048]{1,0:T(8,128)(2,1)S(1)} %pad_maximum_fusion.1), channel_id=1, source_target_pairs={{0,8},{8,0},{16,24},{24,16},{1,9},{9,1},{17,25},{25,17},{2,10},{10... | collective-permute-start | bytes 1769480 | tf_op jit(solution)/shard_map/ppermute | solution.py:354
  82.0 3.2 %collective-permute-start.11 = (bf16[144,2048]{1,0:T(8,128)(2,1)S(1)}, bf16[144,2048]{1,0:T(8,128)(2,1)S(1)}, u32[]{:S(2)}, u32[]{:S(2)}) collective-permute-start(bf16[144,2048]{1,0:T(8,128)(2,1)S(1)} %get-tuple-element.68), channel_id=1, source_target_pairs={{0,4},{1,5},{2,6},{3,7},{4,0},{5,1},{6,2},{7,3},{8,12},{9,13},{10,... | collective-permute-start | bytes 1769480 | tf_op jit(solution)/shard_map/ppermute | solution.py:351
  85.2 5.4 %collective-permute-start.19 = (bf16[72,4608]{1,0:T(8,128)(2,1)S(1)}, bf16[72,4608]{1,0:T(8,128)(2,1)S(1)}, u32[]{:S(2)}, u32[]{:S(2)}) collective-permute-start(bf16[72,4608]{1,0:T(8,128)(2,1)S(1)} %get-tuple-element.82), channel_id=1, source_target_pairs={{0,16},{8,24},{16,0},{24,8},{1,17},{9,25},{17,1},{25,9},{2,18},{10... | collective-permute-start | bytes 1990664 | tf_op jit(solution)/shard_map/ppermute | solution.py:354
  90.7 7.0 %collective-permute-done.17.refs_6_ = bf16[72,4608]{1,0:T(8,128)(2,1)S(1)} collective-permute-done((bf16[72,4608]{1,0:T(8,128)(2,1)S(1)}, bf16[72,4608]{1,0:T(8,128)(2,1)S(1)}, u32[]{:S(2)}, u32[]{:S(2)}) %collective-permute-start.17) | collective-permute-done | bytes 663584 | tf_op jit(solution)/shard_map/ppermute | solution.py:354
  98.4 7.3 %collective-permute-done.14 = bf16[144,2048]{1,0:T(8,128)(2,1)S(1)} collective-permute-done((bf16[144,2048]{1,0:T(8,128)(2,1)S(1)}, bf16[144,2048]{1,0:T(8,128)(2,1)S(1)}, u32[]{:S(2)}, u32[]{:S(2)}) %collective-permute-start.14) | collective-permute-done | bytes 589856 | tf_op jit(solution)/shard_map/ppermute | solution.py:354
  105.8 0.7 collective-permute-done.19.refs_7_
  106.5 1.1 collective-permute-start.20
  107.7 7.2 %weight_grads_early.1 = (f32[512,1024]{1,0:T(8,128)}, f32[512,1024]{1,0:T(8,128)}, f32[1024,512]{1,0:T(8,128)}) custom-call(bf16[72,4096]{1,0:T(8,128)(2,1)S(1)} %get-tuple-element.60.refs_0_, bf16[72,4608]{1,0:T(8,128)(2,1)S(1)} %collective-permute-done.7.refs_1_, bf16[72,4608]{1,0:T(8,128)(2,1)S(1)} %copy-done.2, ...), custom_call_target="tpu_custom_call" | custom-call | flops 2491416576 | bytes 12779520 | tf_op jit(solution)/shard_map/weight_grads_early/pallas_call | solution.py:329
  115.2 2.2 %collective-permute-done.20 = bf16[144,2048]{1,0:T(8,128)(2,1)S(1)} collective-permute-done((bf16[144,2048]{1,0:T(8,128)(2,1)S(1)}, bf16[144,2048]{1,0:T(8,128)(2,1)S(1)}, u32[]{:S(2)}, u32[]{:S(2)}) %collective-permute-start.20) | collective-permute-done | bytes 589856 | tf_op jit(solution)/shard_map/ppermute | solution.py:354
  117.5 5.4 %weight_grads.1 = (f32[512,1024]{1,0:T(8,128)}, f32[512,1024]{1,0:T(8,128)}, f32[1024,512]{1,0:T(8,128)}) custom-call(f32[512,1024]{1,0:T(8,128)S(1)} %copy-done, f32[512,1024]{1,0:T(8,128)} %get-tuple-element.76.refs_1_, f32[1024,512]{1,0:T(8,128)} %get-tuple-element.77.refs_2_, bf16[72,2048]{1,0:T(8,128)(2,1)S(1)} %get-tuple-element.98.refs_3_, ...), custom_call_target="tpu_custom_call" | custom-call | flops 1132462080 | bytes 9240576 | tf_op jit(solution)/shard_map/weight_grads/pallas_call | solution.py:329
  123.0 1.0 combine_grad.1
  124.0 1.6 %combine_mixed.1 = (f32[128,2048]{1,0:T(8,128)S(1)}, bf16[128,2048]{1,0:T(8,128)(2,1)S(1)}) custom-call(s32[4,128]{1,0:T(4,128)S(1)} %pad_add_fusion.routing_ref, s32[4,128]{1,0:T(4,128)S(1)} %collective-permute-done.other_routing_ref, bf16[144,2048]{1,0:T(8,128)(2,1)S(1)} %get-tuple-element.87.refs_0_, ...), custom_call_target="tpu_custom_call" | custom-call | flops 301989888 | bytes 3276800 | tf_op jit(solution)/shard_map/combine_mixed/pallas_call | solution.py:193
  126.2 0.9 add_convert_fusion
  127.7 0.9 add_convert_fusion.1
  (55 shorter events, 5.0 us)
Async XLA Ops:
  0.6 2.8 %collective-permute-start.1 = (bf16[128,2048]{1,0:T(8,128)(2,1)}, bf16[128,2048]{1,0:T(8,128)(2,1)S(1)}, u32[]{:S(2)}, u32[]{:S(2)}) collective-permute-start(bf16[128,2048]{1,0:T(8,128)(2,1)} %x_ref.1), channel_id=1, source_target_pairs={{0,1},{1,0},{2,3},{3,2},{4,5},{5,4},{6,7},{7,6},{8,9},{9,8},{10,11... | collective-permute-start | bytes 1572872 | tf_op jit(solution)/shard_map/ppermute | solution.py:348
  1.2 2.5 %collective-permute-start.2 = (bf16[128,2048]{1,0:T(8,128)(2,1)}, bf16[128,2048]{1,0:T(8,128)(2,1)S(1)}, u32[]{:S(2)}, u32[]{:S(2)}) collective-permute-start(bf16[128,2048]{1,0:T(8,128)(2,1)} %dy_ref.1), channel_id=1, source_target_pairs={{0,1},{1,0},{2,3},{3,2},{4,5},{5,4},{6,7},{7,6},{8,9},{9,8},{10,11... | collective-permute-start | bytes 1572872 | tf_op jit(solution)/shard_map/ppermute | solution.py:348
  1.9 1.5 %collective-permute-start = (s32[4,128]{1,0:T(4,128)S(1)}, s32[4,128]{1,0:T(4,128)S(1)}, u32[]{:S(2)}, u32[]{:S(2)}) collective-permute-start(s32[4,128]{1,0:T(4,128)S(1)} %pad_add_fusion.routing_ref), channel_id=1, source_target_pairs={{0,1},{1,0},{2,3},{3,2},{4,5},{5,4},{6,7},{7,6},{8,9},{9,8},{10,11... | collective-permute-start | bytes 6152 | tf_op jit(solution)/shard_map/ppermute | solution.py:348
  5.9 18.7 %collective-permute-start.3 = (bf16[144,2048]{1,0:T(8,128)(2,1)S(1)}, bf16[144,2048]{1,0:T(8,128)(2,1)S(1)}, u32[]{:S(2)}, u32[]{:S(2)}) collective-permute-start(bf16[144,2048]{1,0:T(8,128)(2,1)S(1)} %get-tuple-element.52), channel_id=1, source_target_pairs={{0,2},{1,3},{2,0},{3,1},{4,6},{5,7},{6,4},{7,5},{8,10},{9,11},{10,... | collective-permute-start | bytes 1769480 | tf_op jit(solution)/shard_map/ppermute | solution.py:351
  8.9 28.9 %collective-permute-start.4 = (bf16[144,2048]{1,0:T(8,128)(2,1)S(1)}, bf16[144,2048]{1,0:T(8,128)(2,1)S(1)}, u32[]{:S(2)}, u32[]{:S(2)}) collective-permute-start(bf16[144,2048]{1,0:T(8,128)(2,1)S(1)} %get-tuple-element.55), channel_id=1, source_target_pairs={{0,6},{1,7},{2,4},{3,5},{4,2},{5,3},{6,0},{7,1},{8,14},{9,15},{10,... | collective-permute-start | bytes 1769480 | tf_op jit(solution)/shard_map/ppermute | solution.py:351
  21.5 27.9 %collective-permute-start.7 = (bf16[72,4608]{1,0:T(8,128)(2,1)S(1)}, bf16[72,4608]{1,0:T(8,128)(2,1)S(1)}, u32[]{:S(2)}, u32[]{:S(2)}) collective-permute-start(bf16[72,4608]{1,0:T(8,128)(2,1)S(1)} %get-tuple-element.61), channel_id=1, source_target_pairs={{0,8},{8,0},{16,24},{24,16},{1,9},{9,1},{17,25},{25,17},{2,10},{10... | collective-permute-start | bytes 1990664 | tf_op jit(solution)/shard_map/ppermute | solution.py:354
  23.1 26.4 %collective-permute-start.8 = (bf16[72,4608]{1,0:T(8,128)(2,1)S(1)}, bf16[72,4608]{1,0:T(8,128)(2,1)S(1)}, u32[]{:S(2)}, u32[]{:S(2)}) collective-permute-start(bf16[72,4608]{1,0:T(8,128)(2,1)S(1)} %get-tuple-element.62), channel_id=1, source_target_pairs={{0,16},{8,24},{16,0},{24,8},{1,17},{9,25},{17,1},{25,9},{2,18},{10... | collective-permute-start | bytes 1990664 | tf_op jit(solution)/shard_map/ppermute | solution.py:354
  34.7 18.8 %collective-permute-start.9 = (bf16[72,4608]{1,0:T(8,128)(2,1)S(1)}, bf16[72,4608]{1,0:T(8,128)(2,1)S(1)}, u32[]{:S(2)}, u32[]{:S(2)}) collective-permute-start(bf16[72,4608]{1,0:T(8,128)(2,1)S(1)} %get-tuple-element.64), channel_id=1, source_target_pairs={{0,8},{8,0},{16,24},{24,16},{1,9},{9,1},{17,25},{25,17},{2,10},{10... | collective-permute-start | bytes 1990664 | tf_op jit(solution)/shard_map/ppermute | solution.py:354
  35.3 29.1 %collective-permute-start.6 = (bf16[144,2048]{1,0:T(8,128)(2,1)S(1)}, bf16[144,2048]{1,0:T(8,128)(2,1)S(1)}, u32[]{:S(2)}, u32[]{:S(2)}) collective-permute-start(bf16[144,2048]{1,0:T(8,128)(2,1)S(1)} %get-tuple-element.59), channel_id=1, source_target_pairs={{0,4},{1,5},{2,6},{3,7},{4,0},{5,1},{6,2},{7,3},{8,12},{9,13},{10,... | collective-permute-start | bytes 1769480 | tf_op jit(solution)/shard_map/ppermute | solution.py:351
  37.8 28.2 %collective-permute-start.10 = (bf16[72,4608]{1,0:T(8,128)(2,1)S(1)}, bf16[72,4608]{1,0:T(8,128)(2,1)S(1)}, u32[]{:S(2)}, u32[]{:S(2)}) collective-permute-start(bf16[72,4608]{1,0:T(8,128)(2,1)S(1)} %get-tuple-element.65), channel_id=1, source_target_pairs={{0,16},{8,24},{16,0},{24,8},{1,17},{9,25},{17,1},{25,9},{2,18},{10... | collective-permute-start | bytes 1990664 | tf_op jit(solution)/shard_map/ppermute | solution.py:354
  49.4 16.5 %copy-start.1 = (bf16[72,4608]{1,0:T(8,128)(2,1)}, bf16[72,4608]{1,0:T(8,128)(2,1)S(1)}, u32[]{:S(2)}) copy-start(bf16[72,4608]{1,0:T(8,128)(2,1)S(1)} %collective-permute-done.8.refs_2_) | copy-start | bytes 1990660
  49.4 30.3 %collective-permute-start.15 = (bf16[72,4608]{1,0:T(8,128)(2,1)S(1)}, bf16[72,4608]{1,0:T(8,128)(2,1)S(1)}, u32[]{:S(2)}, u32[]{:S(2)}) collective-permute-start(bf16[72,4608]{1,0:T(8,128)(2,1)S(1)} %get-tuple-element.73), channel_id=1, source_target_pairs={{0,8},{8,0},{16,24},{24,16},{1,9},{9,1},{17,25},{25,17},{2,10},{10... | collective-permute-start | bytes 1990664 | tf_op jit(solution)/shard_map/ppermute | solution.py:354
  50.9 28.9 %collective-permute-start.16 = (bf16[72,4608]{1,0:T(8,128)(2,1)S(1)}, bf16[72,4608]{1,0:T(8,128)(2,1)S(1)}, u32[]{:S(2)}, u32[]{:S(2)}) collective-permute-start(bf16[72,4608]{1,0:T(8,128)(2,1)S(1)} %get-tuple-element.74), channel_id=1, source_target_pairs={{0,16},{8,24},{16,0},{24,8},{1,17},{9,25},{17,1},{25,9},{2,18},{10... | collective-permute-start | bytes 1990664 | tf_op jit(solution)/shard_map/ppermute | solution.py:354
  53.5 28.5 %collective-permute-start.5 = (bf16[144,2048]{1,0:T(8,128)(2,1)S(1)}, bf16[144,2048]{1,0:T(8,128)(2,1)S(1)}, u32[]{:S(2)}, u32[]{:S(2)}) collective-permute-start(bf16[144,2048]{1,0:T(8,128)(2,1)S(1)} %get-tuple-element.58), channel_id=1, source_target_pairs={{0,2},{1,3},{2,0},{3,1},{4,6},{5,7},{6,4},{7,5},{8,10},{9,11},{10,... | collective-permute-start | bytes 1769480 | tf_op jit(solution)/shard_map/ppermute | solution.py:351
  64.4 20.8 %collective-permute-start.13 = (bf16[144,2048]{1,0:T(8,128)(2,1)S(1)}, bf16[144,2048]{1,0:T(8,128)(2,1)S(1)}, u32[]{:S(2)}, u32[]{:S(2)}) collective-permute-start(bf16[144,2048]{1,0:T(8,128)(2,1)S(1)} %pad_maximum_fusion), channel_id=1, source_target_pairs={{0,16},{8,24},{16,0},{24,8},{1,17},{9,25},{17,1},{25,9},{2,18},{10... | collective-permute-start | bytes 1769480 | tf_op jit(solution)/shard_map/ppermute | solution.py:354
  66.0 57.0 %collective-permute-start.12 = (bf16[144,2048]{1,0:T(8,128)(2,1)S(1)}, bf16[144,2048]{1,0:T(8,128)(2,1)S(1)}, u32[]{:S(2)}, u32[]{:S(2)}) collective-permute-start(bf16[144,2048]{1,0:T(8,128)(2,1)S(1)} %get-tuple-element.57), channel_id=1, source_target_pairs={{0,6},{1,7},{2,4},{3,5},{4,2},{5,3},{6,0},{7,1},{8,14},{9,15},{10,... | collective-permute-start | bytes 1769480 | tf_op jit(solution)/shard_map/ppermute | solution.py:351
  69.4 10.6 %slice-start = ((bf16[72,4608]{1,0:T(8,128)(2,1)}), bf16[72,2048]{1,0:T(8,128)(2,1)S(1)}, s32[]{:S(2)}) async-start(bf16[72,4608]{1,0:T(8,128)(2,1)} %copy-done.1), calls=%async_computation | async-start | bytes 589824 | tf_op jit(solution)/shard_map/slice | solution.py:367
  79.8 5.5 %copy-start.4 = (bf16[72,4608]{1,0:T(8,128)(2,1)}, bf16[72,4608]{1,0:T(8,128)(2,1)S(1)}, u32[]{:S(2)}) copy-start(bf16[72,4608]{1,0:T(8,128)(2,1)S(1)} %collective-permute-done.15.refs_11_) | copy-start | bytes 1990660
  79.8 5.4 %copy-start.3 = (bf16[72,4608]{1,0:T(8,128)(2,1)}, bf16[72,4608]{1,0:T(8,128)(2,1)S(1)}, u32[]{:S(2)}) copy-start(bf16[72,4608]{1,0:T(8,128)(2,1)S(1)} %collective-permute-done.16.refs_12_) | copy-start | bytes 1990660
  79.8 17.9 %collective-permute-start.17 = (bf16[72,4608]{1,0:T(8,128)(2,1)S(1)}, bf16[72,4608]{1,0:T(8,128)(2,1)S(1)}, u32[]{:S(2)}, u32[]{:S(2)}) collective-permute-start(bf16[72,4608]{1,0:T(8,128)(2,1)S(1)} %get-tuple-element.81), channel_id=1, source_target_pairs={{0,8},{8,0},{16,24},{24,16},{1,9},{9,1},{17,25},{25,17},{2,10},{10... | collective-permute-start | bytes 1990664 | tf_op jit(solution)/shard_map/ppermute | solution.py:354
  80.0 25.7 %collective-permute-start.14 = (bf16[144,2048]{1,0:T(8,128)(2,1)S(1)}, bf16[144,2048]{1,0:T(8,128)(2,1)S(1)}, u32[]{:S(2)}, u32[]{:S(2)}) collective-permute-start(bf16[144,2048]{1,0:T(8,128)(2,1)S(1)} %pad_maximum_fusion.1), channel_id=1, source_target_pairs={{0,8},{8,0},{16,24},{24,16},{1,9},{9,1},{17,25},{25,17},{2,10},{10... | collective-permute-start | bytes 1769480 | tf_op jit(solution)/shard_map/ppermute | solution.py:354
  82.0 40.9 %collective-permute-start.11 = (bf16[144,2048]{1,0:T(8,128)(2,1)S(1)}, bf16[144,2048]{1,0:T(8,128)(2,1)S(1)}, u32[]{:S(2)}, u32[]{:S(2)}) collective-permute-start(bf16[144,2048]{1,0:T(8,128)(2,1)S(1)} %get-tuple-element.68), channel_id=1, source_target_pairs={{0,4},{1,5},{2,6},{3,7},{4,0},{5,1},{6,2},{7,3},{8,12},{9,13},{10,... | collective-permute-start | bytes 1769480 | tf_op jit(solution)/shard_map/ppermute | solution.py:351
  85.2 12.5 %slice-start.2 = ((bf16[72,4608]{1,0:T(8,128)(2,1)}), bf16[72,2048]{1,0:T(8,128)(2,1)S(1)}, s32[]{:S(2)}) async-start(bf16[72,4608]{1,0:T(8,128)(2,1)} %copy-done.4), calls=%async_computation.2 | async-start | bytes 589824 | tf_op jit(solution)/shard_map/slice | solution.py:367
  85.2 21.2 %collective-permute-start.19 = (bf16[72,4608]{1,0:T(8,128)(2,1)S(1)}, bf16[72,4608]{1,0:T(8,128)(2,1)S(1)}, u32[]{:S(2)}, u32[]{:S(2)}) collective-permute-start(bf16[72,4608]{1,0:T(8,128)(2,1)S(1)} %get-tuple-element.82), channel_id=1, source_target_pairs={{0,16},{8,24},{16,0},{24,8},{1,17},{9,25},{17,1},{25,9},{2,18},{10... | collective-permute-start | bytes 1990664 | tf_op jit(solution)/shard_map/ppermute | solution.py:354
  97.7 8.7 %slice-start.1 = ((bf16[72,4608]{1,0:T(8,128)(2,1)}), bf16[72,2048]{1,0:T(8,128)(2,1)S(1)}, s32[]{:S(2)}) async-start(bf16[72,4608]{1,0:T(8,128)(2,1)} %copy-done.3), calls=%async_computation.1 | async-start | bytes 589824 | tf_op jit(solution)/shard_map/slice | solution.py:367
  97.8 17.4 %collective-permute-start.18 = (bf16[144,2048]{1,0:T(8,128)(2,1)S(1)}, bf16[144,2048]{1,0:T(8,128)(2,1)S(1)}, u32[]{:S(2)}, u32[]{:S(2)}) collective-permute-start(bf16[144,2048]{1,0:T(8,128)(2,1)S(1)} %pad_maximum_fusion.2), channel_id=1, source_target_pairs={{0,16},{8,24},{16,0},{24,8},{1,17},{9,25},{17,1},{25,9},{2,18},{10... | collective-permute-start | bytes 1769480 | tf_op jit(solution)/shard_map/ppermute | solution.py:354
  105.7 1.9 %copy-start.2 = (bf16[72,4608]{1,0:T(8,128)(2,1)S(1)}, bf16[72,4608]{1,0:T(8,128)(2,1)}, u32[]{:S(2)}) copy-start(bf16[72,4608]{1,0:T(8,128)(2,1)} %copy-done.1) | copy-start | bytes 1990660
  106.5 10.9 %collective-permute-start.20 = (bf16[144,2048]{1,0:T(8,128)(2,1)S(1)}, bf16[144,2048]{1,0:T(8,128)(2,1)S(1)}, u32[]{:S(2)}, u32[]{:S(2)}) collective-permute-start(bf16[144,2048]{1,0:T(8,128)(2,1)S(1)} %pad_maximum_fusion.3), channel_id=1, source_target_pairs={{0,8},{8,0},{16,24},{24,16},{1,9},{9,1},{17,25},{25,17},{2,10},{10... | collective-permute-start | bytes 1769480 | tf_op jit(solution)/shard_map/ppermute | solution.py:354
  114.8 2.6 %copy-start = (f32[512,1024]{1,0:T(8,128)S(1)}, f32[512,1024]{1,0:T(8,128)}, u32[]{:S(2)}) copy-start(f32[512,1024]{1,0:T(8,128)} %get-tuple-element.75.refs_0_) | copy-start | bytes 6291460
  123.9 2.3 %collective-permute-start.22 = (bf16[128,2048]{1,0:T(8,128)(2,1)S(1)}, bf16[128,2048]{1,0:T(8,128)(2,1)S(1)}, u32[]{:S(2)}, u32[]{:S(2)}) collective-permute-start(bf16[128,2048]{1,0:T(8,128)(2,1)S(1)} %get-tuple-element.94), channel_id=1, source_target_pairs={{0,1},{1,0},{2,3},{3,2},{4,5},{5,4},{6,7},{7,6},{8,9},{9,8},{10,11... | collective-permute-start | bytes 1572872 | tf_op jit(solution)/shard_map/ppermute | solution.py:348
  125.6 2.1 %collective-permute-start.21 = (bf16[128,2048]{1,0:T(8,128)(2,1)S(1)}, bf16[128,2048]{1,0:T(8,128)(2,1)S(1)}, u32[]{:S(2)}, u32[]{:S(2)}) collective-permute-start(bf16[128,2048]{1,0:T(8,128)(2,1)S(1)} %get-tuple-element.92), channel_id=1, source_target_pairs={{0,1},{1,0},{2,3},{3,2},{4,5},{5,4},{6,7},{7,6},{8,9},{9,8},{10,11... | collective-permute-start | bytes 1572872 | tf_op jit(solution)/shard_map/ppermute | solution.py:348

commit v5 on v4

--- a/solution.py
+++ b/solution.py
@@ -388,7 +388,7 @@
     got = {0: back[0]}
     got[1] = over_z(back[1], 1)
     got.update({k: over_z(back[k], k) for k in order[1:-1] if k != 1})
-    back[last], sends = experts(after(rows[last], *previous, *sets[0], *sets[1]), weights, groups)
+    back[last], sends = experts(after(rows[last], *previous), weights, groups)
     back[last] = after(back[last], got[1])
     got[last] = over_z(back[last], last)
     sets[:2] = second_phase(*sets[:2])

time: 129 us -> 131 us (1.016)
  waiting for transfers between devices: 21.8 us -> 31.4 us
  starting transfers between devices: 44.7 us -> 37.3 us
    ppermute x12, waiting for transfers between devices: 19.9 us -> 27.4 us  [over_dp(): lax.ppermute(v, 'dp', [(i, i ^ k) for i in range(groups)])]
    ppermute x12, starting transfers between devices: 17.8 us -> 13.6 us  [over_dp(): lax.ppermute(v, 'dp', [(i, i ^ k) for i in range(groups)])]
    ppermute x6, starting transfers between devices: 25.3 us -> 22.1 us  [over_z(): lax.ppermute(v, 'expert', [(i, i ^ 2 * k) for i in range(devices)])]
    ppermute x6, waiting for transfers between devices: 0.02 us -> 2.13 us  [over_z(): lax.ppermute(v, 'expert', [(i, i ^ 2 * k) for i in range(devices)])]
  transfers between devices with their start and end apart: 23 -> 23, of which waited for: 9 -> 8; matrix products, arithmetic and copies ran while one was open for 2% -> 2% of each run, Pallas kernels for 43% -> 42%
where the time goes in v5:
time: 131 us
  Pallas kernels  58.1 us (44%)
  starting transfers between devices  37.3 us (28%)
  waiting for transfers between devices  31.4 us (24%)
  other arithmetic  2.7 us (2%)
    pallas_call x4, Pallas kernels, experts(): pl.pallas_call(functools.partial(experts_kernel, layouts, share, hidden),...  40.7 us
    ppermute x12, waiting for transfers between devices, over_dp(): lax.ppermute(v, 'dp', [(i, i ^ k) for i in range(groups)])  27.4 us
    ppermute x6, starting transfers between devices, over_z(): lax.ppermute(v, 'expert', [(i, i ^ 2 * k) for i in range(devices)])  22.1 us
    ppermute x12, starting transfers between devices, over_dp(): lax.ppermute(v, 'dp', [(i, i ^ k) for i in range(groups)])  13.6 us
    pallas_call x2, Pallas kernels, weight_grads(): pl.pallas_call(functools.partial(weight_kernel, plan, bool(partial), fina...  12.6 us
  transfers between devices with their start and end apart: 23, of which 8 were waited for; matrix products, arithmetic and copies ran while one was open for 2% of the time, Pallas kernels for 42%

profile of v5, /device:TPU:0, one launch (start us, length us, event | category | flops | bytes accessed | tf_op | source)
XLA Modules:
  0.0 130.8 jit_solution(1266132208065934777)
XLA Ops:
  1.2 0.7 pad_add_fusion.routing_ref
  2.4 1.1 collective-permute-done.other_routing_ref
  3.6 2.2 %dispatch.1 = (bf16[144,2048]{1,0:T(8,128)(2,1)S(1)}, bf16[144,2048]{1,0:T(8,128)(2,1)S(1)}, bf16[144,2048]{1,0:T(8,128)(2,1)S(1)}, bf16[144,2048]{1,0:T(8,128)(2,1)S(1)}) custom-call(s32[4,128]{1,0:T(4,128)S(1)} %pad_add_fusion.routing_ref, s32[4,128]{1,0:T(4,128)S(1)} %collective-permute-done.other_routing_ref, bf16[128,2048]{1,0:T(8,128)(2,1)} %x_ref.1, ...), custom_call_target="tpu_custom_call" | custom-call | flops 603979776 | bytes 4456448 | tf_op jit(solution)/shard_map/dispatch/pallas_call | solution.py:151
  5.9 3.0 %collective-permute-start.3 = (bf16[144,2048]{1,0:T(8,128)(2,1)S(1)}, bf16[144,2048]{1,0:T(8,128)(2,1)S(1)}, u32[]{:S(2)}, u32[]{:S(2)}) collective-permute-start(bf16[144,2048]{1,0:T(8,128)(2,1)S(1)} %get-tuple-element.52), channel_id=1, source_target_pairs={{0,2},{1,3},{2,0},{3,1},{4,6},{5,7},{6,4},{7,5},{8,10},{9,11},{10,... | collective-permute-start | bytes 1769480 | tf_op jit(solution)/shard_map/ppermute | solution.py:351
  8.9 2.5 %collective-permute-start.4 = (bf16[144,2048]{1,0:T(8,128)(2,1)S(1)}, bf16[144,2048]{1,0:T(8,128)(2,1)S(1)}, u32[]{:S(2)}, u32[]{:S(2)}) collective-permute-start(bf16[144,2048]{1,0:T(8,128)(2,1)S(1)} %get-tuple-element.55), channel_id=1, source_target_pairs={{0,6},{1,7},{2,4},{3,5},{4,2},{5,3},{6,0},{7,1},{8,14},{9,15},{10,... | collective-permute-start | bytes 1769480 | tf_op jit(solution)/shard_map/ppermute | solution.py:351
  11.4 10.1 %experts.4 = (bf16[144,2048]{1,0:T(8,128)(2,1)S(1)}, bf16[72,4096]{1,0:T(8,128)(2,1)S(1)}, bf16[72,4608]{1,0:T(8,128)(2,1)S(1)}, bf16[72,4608]{1,0:T(8,128)(2,1)S(1)}) custom-call(bf16[144,2048]{1,0:T(8,128)(2,1)S(1)} %get-tuple-element.50.rows_ref, bf16[2048,1024]{1,0:T(8,128)(2,1)} %wg.7, bf16[2048,1024]{1,0:T(8,128)(2,1)} %wu.7, bf16[1024,2048]{1,0:T(8,128)(2,1)} %wd.7), custom_call_target="tpu_custom_call" | custom-call | flops 1811939328 | bytes 12582912 | tf_op jit(solution)/shard_map/experts/pallas_call | solution.py:261
  21.5 1.6 %collective-permute-start.9 = (bf16[72,4608]{1,0:T(8,128)(2,1)S(1)}, bf16[72,4608]{1,0:T(8,128)(2,1)S(1)}, u32[]{:S(2)}, u32[]{:S(2)}) collective-permute-start(bf16[72,4608]{1,0:T(8,128)(2,1)S(1)} %get-tuple-element.64), channel_id=1, source_target_pairs={{0,8},{8,0},{16,24},{24,16},{1,9},{9,1},{17,25},{25,17},{2,10},{10... | collective-permute-start | bytes 1990664 | tf_op jit(solution)/shard_map/ppermute | solution.py:354
  23.1 1.5 %collective-permute-start.10 = (bf16[72,4608]{1,0:T(8,128)(2,1)S(1)}, bf16[72,4608]{1,0:T(8,128)(2,1)S(1)}, u32[]{:S(2)}, u32[]{:S(2)}) collective-permute-start(bf16[72,4608]{1,0:T(8,128)(2,1)S(1)} %get-tuple-element.65), channel_id=1, source_target_pairs={{0,16},{8,24},{16,0},{24,8},{1,17},{9,25},{17,1},{25,9},{2,18},{10... | collective-permute-start | bytes 1990664 | tf_op jit(solution)/shard_map/ppermute | solution.py:354
  24.6 10.1 %experts.5 = (bf16[144,2048]{1,0:T(8,128)(2,1)S(1)}, bf16[72,4096]{1,0:T(8,128)(2,1)S(1)}, bf16[72,4608]{1,0:T(8,128)(2,1)S(1)}, bf16[72,4608]{1,0:T(8,128)(2,1)S(1)}) custom-call(bf16[144,2048]{1,0:T(8,128)(2,1)S(1)} %collective-permute-done.3.rows_ref, bf16[2048,1024]{1,0:T(8,128)(2,1)} %wg.7, bf16[2048,1024]{1,0:T(8,128)(2,1)} %wu.7, bf16[1024,2048]{1,0:T(8,128)(2,1)} %wd.7), custom_call_target="tpu_custom_call" | custom-call | flops 1811939328 | bytes 12582912 | tf_op jit(solution)/shard_map/experts/pallas_call | solution.py:261
  34.7 0.6 collective-permute-start.11
  35.3 2.5 %collective-permute-start.6 = (bf16[144,2048]{1,0:T(8,128)(2,1)S(1)}, bf16[144,2048]{1,0:T(8,128)(2,1)S(1)}, u32[]{:S(2)}, u32[]{:S(2)}) collective-permute-start(bf16[144,2048]{1,0:T(8,128)(2,1)S(1)} %get-tuple-element.59), channel_id=1, source_target_pairs={{0,4},{1,5},{2,6},{3,7},{4,0},{5,1},{6,2},{7,3},{8,12},{9,13},{10,... | collective-permute-start | bytes 1769480 | tf_op jit(solution)/shard_map/ppermute | solution.py:351
  37.8 1.5 %collective-permute-start.13 = (bf16[72,4608]{1,0:T(8,128)(2,1)S(1)}, bf16[72,4608]{1,0:T(8,128)(2,1)S(1)}, u32[]{:S(2)}, u32[]{:S(2)}) collective-permute-start(bf16[72,4608]{1,0:T(8,128)(2,1)S(1)} %get-tuple-element.67), channel_id=1, source_target_pairs={{0,16},{8,24},{16,0},{24,8},{1,17},{9,25},{17,1},{25,9},{2,18},{10... | collective-permute-start | bytes 1990664 | tf_op jit(solution)/shard_map/ppermute | solution.py:354
  39.3 10.1 %experts.6 = (bf16[144,2048]{1,0:T(8,128)(2,1)S(1)}, bf16[72,4096]{1,0:T(8,128)(2,1)S(1)}, bf16[72,4608]{1,0:T(8,128)(2,1)S(1)}, bf16[72,4608]{1,0:T(8,128)(2,1)S(1)}) custom-call(bf16[144,2048]{1,0:T(8,128)(2,1)S(1)} %collective-permute-done.4.rows_ref, bf16[2048,1024]{1,0:T(8,128)(2,1)} %wg.7, bf16[2048,1024]{1,0:T(8,128)(2,1)} %wu.7, bf16[1024,2048]{1,0:T(8,128)(2,1)} %wd.7), custom_call_target="tpu_custom_call" | custom-call | flops 1811939328 | bytes 12582912 | tf_op jit(solution)/shard_map/experts/pallas_call | solution.py:261
  49.4 1.4 %collective-permute-start.15 = (bf16[72,4608]{1,0:T(8,128)(2,1)S(1)}, bf16[72,4608]{1,0:T(8,128)(2,1)S(1)}, u32[]{:S(2)}, u32[]{:S(2)}) collective-permute-start(bf16[72,4608]{1,0:T(8,128)(2,1)S(1)} %get-tuple-element.73), channel_id=1, source_target_pairs={{0,8},{8,0},{16,24},{24,16},{1,9},{9,1},{17,25},{25,17},{2,10},{10... | collective-permute-start | bytes 1990664 | tf_op jit(solution)/shard_map/ppermute | solution.py:354
  51.2 2.3 %collective-permute-done.11.refs_6_ = bf16[72,4608]{1,0:T(8,128)(2,1)S(1)} collective-permute-done((bf16[72,4608]{1,0:T(8,128)(2,1)S(1)}, bf16[72,4608]{1,0:T(8,128)(2,1)S(1)}, u32[]{:S(2)}, u32[]{:S(2)}) %collective-permute-start.11) | collective-permute-done | bytes 663584 | tf_op jit(solution)/shard_map/ppermute | solution.py:354
  53.5 10.7 %collective-permute-start.5 = (bf16[144,2048]{1,0:T(8,128)(2,1)S(1)}, bf16[144,2048]{1,0:T(8,128)(2,1)S(1)}, u32[]{:S(2)}, u32[]{:S(2)}) collective-permute-start(bf16[144,2048]{1,0:T(8,128)(2,1)S(1)} %get-tuple-element.58), channel_id=1, source_target_pairs={{0,2},{1,3},{2,0},{3,1},{4,6},{5,7},{6,4},{7,5},{8,10},{9,11},{10,... | collective-permute-start | bytes 1769480 | tf_op jit(solution)/shard_map/ppermute | solution.py:351
  64.3 1.6 %collective-permute-start.12 = (bf16[144,2048]{1,0:T(8,128)(2,1)S(1)}, bf16[144,2048]{1,0:T(8,128)(2,1)S(1)}, u32[]{:S(2)}, u32[]{:S(2)}) collective-permute-start(bf16[144,2048]{1,0:T(8,128)(2,1)S(1)} %pad_maximum_fusion), channel_id=1, source_target_pairs={{0,16},{8,24},{16,0},{24,8},{1,17},{9,25},{17,1},{25,9},{2,18},{10... | collective-permute-start | bytes 1769480 | tf_op jit(solution)/shard_map/ppermute | solution.py:354
  65.9 10.3 %experts.7 = (bf16[144,2048]{1,0:T(8,128)(2,1)S(1)}, bf16[72,4096]{1,0:T(8,128)(2,1)S(1)}, bf16[72,4608]{1,0:T(8,128)(2,1)S(1)}, bf16[72,4608]{1,0:T(8,128)(2,1)S(1)}) custom-call(bf16[144,2048]{1,0:T(8,128)(2,1)S(1)} %collective-permute-done.6.rows_ref, bf16[2048,1024]{1,0:T(8,128)(2,1)} %wg.7, bf16[2048,1024]{1,0:T(8,128)(2,1)} %wu.7, bf16[1024,2048]{1,0:T(8,128)(2,1)} %wd.7), custom_call_target="tpu_custom_call" | custom-call | flops 1811939328 | bytes 12582912 | tf_op jit(solution)/shard_map/experts/pallas_call | solution.py:261
  76.2 3.5 %collective-permute-start.8 = (bf16[144,2048]{1,0:T(8,128)(2,1)S(1)}, bf16[144,2048]{1,0:T(8,128)(2,1)S(1)}, u32[]{:S(2)}, u32[]{:S(2)}) collective-permute-start(bf16[144,2048]{1,0:T(8,128)(2,1)S(1)} %get-tuple-element.57), channel_id=1, source_target_pairs={{0,6},{1,7},{2,4},{3,5},{4,2},{5,3},{6,0},{7,1},{8,14},{9,15},{10,... | collective-permute-start | bytes 1769480 | tf_op jit(solution)/shard_map/ppermute | solution.py:351
  80.0 2.0 %collective-permute-start.14 = (bf16[144,2048]{1,0:T(8,128)(2,1)S(1)}, bf16[144,2048]{1,0:T(8,128)(2,1)S(1)}, u32[]{:S(2)}, u32[]{:S(2)}) collective-permute-start(bf16[144,2048]{1,0:T(8,128)(2,1)S(1)} %pad_maximum_fusion.1), channel_id=1, source_target_pairs={{0,8},{8,0},{16,24},{24,16},{1,9},{9,1},{17,25},{25,17},{2,10},{10... | collective-permute-start | bytes 1769480 | tf_op jit(solution)/shard_map/ppermute | solution.py:354
  82.6 15.1 %collective-permute-done.17.refs_6_ = bf16[72,4608]{1,0:T(8,128)(2,1)S(1)} collective-permute-done((bf16[72,4608]{1,0:T(8,128)(2,1)S(1)}, bf16[72,4608]{1,0:T(8,128)(2,1)S(1)}, u32[]{:S(2)}, u32[]{:S(2)}) %collective-permute-start.17) | collective-permute-done | bytes 663584 | tf_op jit(solution)/shard_map/ppermute | solution.py:354
  98.3 7.3 %collective-permute-done.14 = bf16[144,2048]{1,0:T(8,128)(2,1)S(1)} collective-permute-done((bf16[144,2048]{1,0:T(8,128)(2,1)S(1)}, bf16[144,2048]{1,0:T(8,128)(2,1)S(1)}, u32[]{:S(2)}, u32[]{:S(2)}) %collective-permute-start.14) | collective-permute-done | bytes 589856 | tf_op jit(solution)/shard_map/ppermute | solution.py:354
  105.8 1.8 %collective-permute-start.20 = (bf16[144,2048]{1,0:T(8,128)(2,1)S(1)}, bf16[144,2048]{1,0:T(8,128)(2,1)S(1)}, u32[]{:S(2)}, u32[]{:S(2)}) collective-permute-start(bf16[144,2048]{1,0:T(8,128)(2,1)S(1)} %pad_maximum_fusion.3), channel_id=1, source_target_pairs={{0,8},{8,0},{16,24},{24,16},{1,9},{9,1},{17,25},{25,17},{2,10},{10... | collective-permute-start | bytes 1769480 | tf_op jit(solution)/shard_map/ppermute | solution.py:354
  107.6 7.2 %weight_grads_early.1 = (f32[512,1024]{1,0:T(8,128)}, f32[512,1024]{1,0:T(8,128)}, f32[1024,512]{1,0:T(8,128)}) custom-call(bf16[72,4096]{1,0:T(8,128)(2,1)S(1)} %get-tuple-element.63.refs_0_, bf16[72,4608]{1,0:T(8,128)(2,1)S(1)} %collective-permute-done.9.refs_1_, bf16[72,4608]{1,0:T(8,128)(2,1)S(1)} %collective-permute-done.10.refs_2_, ...), custom_call_target="tpu_custom_call" | custom-call | flops 2491416576 | bytes 12779520 | tf_op jit(solution)/shard_map/weight_grads_early/pallas_call | solution.py:329
  114.9 2.6 %collective-permute-done.20 = bf16[144,2048]{1,0:T(8,128)(2,1)S(1)} collective-permute-done((bf16[144,2048]{1,0:T(8,128)(2,1)S(1)}, bf16[144,2048]{1,0:T(8,128)(2,1)S(1)}, u32[]{:S(2)}, u32[]{:S(2)}) %collective-permute-start.20) | collective-permute-done | bytes 589856 | tf_op jit(solution)/shard_map/ppermute | solution.py:354
  117.5 5.4 %weight_grads.1 = (f32[512,1024]{1,0:T(8,128)}, f32[512,1024]{1,0:T(8,128)}, f32[1024,512]{1,0:T(8,128)}) custom-call(f32[512,1024]{1,0:T(8,128)S(1)} %copy-done, f32[512,1024]{1,0:T(8,128)} %get-tuple-element.76.refs_1_, f32[1024,512]{1,0:T(8,128)} %get-tuple-element.77.refs_2_, bf16[72,2048]{1,0:T(8,128)(2,1)S(1)} %get-tuple-element.98.refs_3_, ...), custom_call_target="tpu_custom_call" | custom-call | flops 1132462080 | bytes 9240576 | tf_op jit(solution)/shard_map/weight_grads/pallas_call | solution.py:329
  123.0 2.1 %collective-permute-done.7.refs_2_ = bf16[144,2048]{1,0:T(8,128)(2,1)S(1)} collective-permute-done((bf16[144,2048]{1,0:T(8,128)(2,1)S(1)}, bf16[144,2048]{1,0:T(8,128)(2,1)S(1)}, u32[]{:S(2)}, u32[]{:S(2)}) %collective-permute-start.7) | collective-permute-done | bytes 589856 | tf_op jit(solution)/shard_map/ppermute | solution.py:351
  125.1 1.0 combine_grad.1
  126.2 1.6 %combine_mixed.1 = (f32[128,2048]{1,0:T(8,128)S(1)}, bf16[128,2048]{1,0:T(8,128)(2,1)S(1)}) custom-call(s32[4,128]{1,0:T(4,128)S(1)} %pad_add_fusion.routing_ref, s32[4,128]{1,0:T(4,128)S(1)} %collective-permute-done.other_routing_ref, bf16[144,2048]{1,0:T(8,128)(2,1)S(1)} %get-tuple-element.87.refs_0_, ...), custom_call_target="tpu_custom_call" | custom-call | flops 301989888 | bytes 3276800 | tf_op jit(solution)/shard_map/combine_mixed/pallas_call | solution.py:193
  128.3 0.9 add_convert_fusion
  129.2 0.6 collective-permute-done.21
  129.9 0.9 add_convert_fusion.1
  (50 shorter events, 4.0 us)
Async XLA Ops:
  0.6 2.8 %collective-permute-start.1 = (bf16[128,2048]{1,0:T(8,128)(2,1)}, bf16[128,2048]{1,0:T(8,128)(2,1)S(1)}, u32[]{:S(2)}, u32[]{:S(2)}) collective-permute-start(bf16[128,2048]{1,0:T(8,128)(2,1)} %x_ref.1), channel_id=1, source_target_pairs={{0,1},{1,0},{2,3},{3,2},{4,5},{5,4},{6,7},{7,6},{8,9},{9,8},{10,11... | collective-permute-start | bytes 1572872 | tf_op jit(solution)/shard_map/ppermute | solution.py:348
  1.2 2.5 %collective-permute-start.2 = (bf16[128,2048]{1,0:T(8,128)(2,1)}, bf16[128,2048]{1,0:T(8,128)(2,1)S(1)}, u32[]{:S(2)}, u32[]{:S(2)}) collective-permute-start(bf16[128,2048]{1,0:T(8,128)(2,1)} %dy_ref.1), channel_id=1, source_target_pairs={{0,1},{1,0},{2,3},{3,2},{4,5},{5,4},{6,7},{7,6},{8,9},{9,8},{10,11... | collective-permute-start | bytes 1572872 | tf_op jit(solution)/shard_map/ppermute | solution.py:348
  1.9 1.5 %collective-permute-start = (s32[4,128]{1,0:T(4,128)S(1)}, s32[4,128]{1,0:T(4,128)S(1)}, u32[]{:S(2)}, u32[]{:S(2)}) collective-permute-start(s32[4,128]{1,0:T(4,128)S(1)} %pad_add_fusion.routing_ref), channel_id=1, source_target_pairs={{0,1},{1,0},{2,3},{3,2},{4,5},{5,4},{6,7},{7,6},{8,9},{9,8},{10,11... | collective-permute-start | bytes 6152 | tf_op jit(solution)/shard_map/ppermute | solution.py:348
  5.9 18.7 %collective-permute-start.3 = (bf16[144,2048]{1,0:T(8,128)(2,1)S(1)}, bf16[144,2048]{1,0:T(8,128)(2,1)S(1)}, u32[]{:S(2)}, u32[]{:S(2)}) collective-permute-start(bf16[144,2048]{1,0:T(8,128)(2,1)S(1)} %get-tuple-element.52), channel_id=1, source_target_pairs={{0,2},{1,3},{2,0},{3,1},{4,6},{5,7},{6,4},{7,5},{8,10},{9,11},{10,... | collective-permute-start | bytes 1769480 | tf_op jit(solution)/shard_map/ppermute | solution.py:351
  8.9 28.9 %collective-permute-start.4 = (bf16[144,2048]{1,0:T(8,128)(2,1)S(1)}, bf16[144,2048]{1,0:T(8,128)(2,1)S(1)}, u32[]{:S(2)}, u32[]{:S(2)}) collective-permute-start(bf16[144,2048]{1,0:T(8,128)(2,1)S(1)} %get-tuple-element.55), channel_id=1, source_target_pairs={{0,6},{1,7},{2,4},{3,5},{4,2},{5,3},{6,0},{7,1},{8,14},{9,15},{10,... | collective-permute-start | bytes 1769480 | tf_op jit(solution)/shard_map/ppermute | solution.py:351
  21.5 27.9 %collective-permute-start.9 = (bf16[72,4608]{1,0:T(8,128)(2,1)S(1)}, bf16[72,4608]{1,0:T(8,128)(2,1)S(1)}, u32[]{:S(2)}, u32[]{:S(2)}) collective-permute-start(bf16[72,4608]{1,0:T(8,128)(2,1)S(1)} %get-tuple-element.64), channel_id=1, source_target_pairs={{0,8},{8,0},{16,24},{24,16},{1,9},{9,1},{17,25},{25,17},{2,10},{10... | collective-permute-start | bytes 1990664 | tf_op jit(solution)/shard_map/ppermute | solution.py:354
  23.1 26.4 %collective-permute-start.10 = (bf16[72,4608]{1,0:T(8,128)(2,1)S(1)}, bf16[72,4608]{1,0:T(8,128)(2,1)S(1)}, u32[]{:S(2)}, u32[]{:S(2)}) collective-permute-start(bf16[72,4608]{1,0:T(8,128)(2,1)S(1)} %get-tuple-element.65), channel_id=1, source_target_pairs={{0,16},{8,24},{16,0},{24,8},{1,17},{9,25},{17,1},{25,9},{2,18},{10... | collective-permute-start | bytes 1990664 | tf_op jit(solution)/shard_map/ppermute | solution.py:354
  34.7 18.8 %collective-permute-start.11 = (bf16[72,4608]{1,0:T(8,128)(2,1)S(1)}, bf16[72,4608]{1,0:T(8,128)(2,1)S(1)}, u32[]{:S(2)}, u32[]{:S(2)}) collective-permute-start(bf16[72,4608]{1,0:T(8,128)(2,1)S(1)} %get-tuple-element.66), channel_id=1, source_target_pairs={{0,8},{8,0},{16,24},{24,16},{1,9},{9,1},{17,25},{25,17},{2,10},{10... | collective-permute-start | bytes 1990664 | tf_op jit(solution)/shard_map/ppermute | solution.py:354
  35.3 29.0 %collective-permute-start.6 = (bf16[144,2048]{1,0:T(8,128)(2,1)S(1)}, bf16[144,2048]{1,0:T(8,128)(2,1)S(1)}, u32[]{:S(2)}, u32[]{:S(2)}) collective-permute-start(bf16[144,2048]{1,0:T(8,128)(2,1)S(1)} %get-tuple-element.59), channel_id=1, source_target_pairs={{0,4},{1,5},{2,6},{3,7},{4,0},{5,1},{6,2},{7,3},{8,12},{9,13},{10,... | collective-permute-start | bytes 1769480 | tf_op jit(solution)/shard_map/ppermute | solution.py:351
  37.8 41.9 %collective-permute-start.13 = (bf16[72,4608]{1,0:T(8,128)(2,1)S(1)}, bf16[72,4608]{1,0:T(8,128)(2,1)S(1)}, u32[]{:S(2)}, u32[]{:S(2)}) collective-permute-start(bf16[72,4608]{1,0:T(8,128)(2,1)S(1)} %get-tuple-element.67), channel_id=1, source_target_pairs={{0,16},{8,24},{16,0},{24,8},{1,17},{9,25},{17,1},{25,9},{2,18},{10... | collective-permute-start | bytes 1990664 | tf_op jit(solution)/shard_map/ppermute | solution.py:354
  49.4 30.3 %collective-permute-start.15 = (bf16[72,4608]{1,0:T(8,128)(2,1)S(1)}, bf16[72,4608]{1,0:T(8,128)(2,1)S(1)}, u32[]{:S(2)}, u32[]{:S(2)}) collective-permute-start(bf16[72,4608]{1,0:T(8,128)(2,1)S(1)} %get-tuple-element.73), channel_id=1, source_target_pairs={{0,8},{8,0},{16,24},{24,16},{1,9},{9,1},{17,25},{25,17},{2,10},{10... | collective-permute-start | bytes 1990664 | tf_op jit(solution)/shard_map/ppermute | solution.py:354
  50.9 28.9 %collective-permute-start.16 = (bf16[72,4608]{1,0:T(8,128)(2,1)S(1)}, bf16[72,4608]{1,0:T(8,128)(2,1)S(1)}, u32[]{:S(2)}, u32[]{:S(2)}) collective-permute-start(bf16[72,4608]{1,0:T(8,128)(2,1)S(1)} %get-tuple-element.74), channel_id=1, source_target_pairs={{0,16},{8,24},{16,0},{24,8},{1,17},{9,25},{17,1},{25,9},{2,18},{10... | collective-permute-start | bytes 1990664 | tf_op jit(solution)/shard_map/ppermute | solution.py:354
  53.5 22.7 %collective-permute-start.5 = (bf16[144,2048]{1,0:T(8,128)(2,1)S(1)}, bf16[144,2048]{1,0:T(8,128)(2,1)S(1)}, u32[]{:S(2)}, u32[]{:S(2)}) collective-permute-start(bf16[144,2048]{1,0:T(8,128)(2,1)S(1)} %get-tuple-element.58), channel_id=1, source_target_pairs={{0,2},{1,3},{2,0},{3,1},{4,6},{5,7},{6,4},{7,5},{8,10},{9,11},{10,... | collective-permute-start | bytes 1769480 | tf_op jit(solution)/shard_map/ppermute | solution.py:351
  64.3 17.7 %collective-permute-start.12 = (bf16[144,2048]{1,0:T(8,128)(2,1)S(1)}, bf16[144,2048]{1,0:T(8,128)(2,1)S(1)}, u32[]{:S(2)}, u32[]{:S(2)}) collective-permute-start(bf16[144,2048]{1,0:T(8,128)(2,1)S(1)} %pad_maximum_fusion), channel_id=1, source_target_pairs={{0,16},{8,24},{16,0},{24,8},{1,17},{9,25},{17,1},{25,9},{2,18},{10... | collective-permute-start | bytes 1769480 | tf_op jit(solution)/shard_map/ppermute | solution.py:354
  76.2 46.7 %collective-permute-start.8 = (bf16[144,2048]{1,0:T(8,128)(2,1)S(1)}, bf16[144,2048]{1,0:T(8,128)(2,1)S(1)}, u32[]{:S(2)}, u32[]{:S(2)}) collective-permute-start(bf16[144,2048]{1,0:T(8,128)(2,1)S(1)} %get-tuple-element.57), channel_id=1, source_target_pairs={{0,6},{1,7},{2,4},{3,5},{4,2},{5,3},{6,0},{7,1},{8,14},{9,15},{10,... | collective-permute-start | bytes 1769480 | tf_op jit(solution)/shard_map/ppermute | solution.py:351
  79.7 45.4 %collective-permute-start.7 = (bf16[144,2048]{1,0:T(8,128)(2,1)S(1)}, bf16[144,2048]{1,0:T(8,128)(2,1)S(1)}, u32[]{:S(2)}, u32[]{:S(2)}) collective-permute-start(bf16[144,2048]{1,0:T(8,128)(2,1)S(1)} %get-tuple-element.62), channel_id=1, source_target_pairs={{0,4},{1,5},{2,6},{3,7},{4,0},{5,1},{6,2},{7,3},{8,12},{9,13},{10,... | collective-permute-start | bytes 1769480 | tf_op jit(solution)/shard_map/ppermute | solution.py:351
  79.7 2.2 %copy-start.2 = (bf16[72,4608]{1,0:T(8,128)(2,1)}, bf16[72,4608]{1,0:T(8,128)(2,1)S(1)}, u32[]{:S(2)}) copy-start(bf16[72,4608]{1,0:T(8,128)(2,1)S(1)} %collective-permute-done.15.refs_11_) | copy-start | bytes 1990660
  79.8 2.2 %copy-start.1 = (bf16[72,4608]{1,0:T(8,128)(2,1)}, bf16[72,4608]{1,0:T(8,128)(2,1)S(1)}, u32[]{:S(2)}) copy-start(bf16[72,4608]{1,0:T(8,128)(2,1)S(1)} %collective-permute-done.16.refs_12_) | copy-start | bytes 1990660
  79.8 17.9 %collective-permute-start.17 = (bf16[72,4608]{1,0:T(8,128)(2,1)S(1)}, bf16[72,4608]{1,0:T(8,128)(2,1)S(1)}, u32[]{:S(2)}, u32[]{:S(2)}) collective-permute-start(bf16[72,4608]{1,0:T(8,128)(2,1)S(1)} %get-tuple-element.81), channel_id=1, source_target_pairs={{0,8},{8,0},{16,24},{24,16},{1,9},{9,1},{17,25},{25,17},{2,10},{10... | collective-permute-start | bytes 1990664 | tf_op jit(solution)/shard_map/ppermute | solution.py:354
  80.0 25.7 %collective-permute-start.14 = (bf16[144,2048]{1,0:T(8,128)(2,1)S(1)}, bf16[144,2048]{1,0:T(8,128)(2,1)S(1)}, u32[]{:S(2)}, u32[]{:S(2)}) collective-permute-start(bf16[144,2048]{1,0:T(8,128)(2,1)S(1)} %pad_maximum_fusion.1), channel_id=1, source_target_pairs={{0,8},{8,0},{16,24},{24,16},{1,9},{9,1},{17,25},{25,17},{2,10},{10... | collective-permute-start | bytes 1769480 | tf_op jit(solution)/shard_map/ppermute | solution.py:354
  82.0 15.7 %slice-start.1 = ((bf16[72,4608]{1,0:T(8,128)(2,1)}), bf16[72,2048]{1,0:T(8,128)(2,1)S(1)}, s32[]{:S(2)}) async-start(bf16[72,4608]{1,0:T(8,128)(2,1)} %copy-done.2), calls=%async_computation.1 | async-start | bytes 589824 | tf_op jit(solution)/shard_map/slice | solution.py:367
  82.0 23.7 %collective-permute-start.19 = (bf16[72,4608]{1,0:T(8,128)(2,1)S(1)}, bf16[72,4608]{1,0:T(8,128)(2,1)S(1)}, u32[]{:S(2)}, u32[]{:S(2)}) collective-permute-start(bf16[72,4608]{1,0:T(8,128)(2,1)S(1)} %get-tuple-element.82), channel_id=1, source_target_pairs={{0,16},{8,24},{16,0},{24,8},{1,17},{9,25},{17,1},{25,9},{2,18},{10... | collective-permute-start | bytes 1990664 | tf_op jit(solution)/shard_map/ppermute | solution.py:354
  97.7 8.0 %slice-start = ((bf16[72,4608]{1,0:T(8,128)(2,1)}), bf16[72,2048]{1,0:T(8,128)(2,1)S(1)}, s32[]{:S(2)}) async-start(bf16[72,4608]{1,0:T(8,128)(2,1)} %copy-done.1), calls=%async_computation | async-start | bytes 589824 | tf_op jit(solution)/shard_map/slice | solution.py:367
  97.8 17.0 %collective-permute-start.18 = (bf16[144,2048]{1,0:T(8,128)(2,1)S(1)}, bf16[144,2048]{1,0:T(8,128)(2,1)S(1)}, u32[]{:S(2)}, u32[]{:S(2)}) collective-permute-start(bf16[144,2048]{1,0:T(8,128)(2,1)S(1)} %pad_maximum_fusion.2), channel_id=1, source_target_pairs={{0,16},{8,24},{16,0},{24,8},{1,17},{9,25},{17,1},{25,9},{2,18},{10... | collective-permute-start | bytes 1769480 | tf_op jit(solution)/shard_map/ppermute | solution.py:354
  105.8 11.6 %collective-permute-start.20 = (bf16[144,2048]{1,0:T(8,128)(2,1)S(1)}, bf16[144,2048]{1,0:T(8,128)(2,1)S(1)}, u32[]{:S(2)}, u32[]{:S(2)}) collective-permute-start(bf16[144,2048]{1,0:T(8,128)(2,1)S(1)} %pad_maximum_fusion.3), channel_id=1, source_target_pairs={{0,8},{8,0},{16,24},{24,16},{1,9},{9,1},{17,25},{25,17},{2,10},{10... | collective-permute-start | bytes 1769480 | tf_op jit(solution)/shard_map/ppermute | solution.py:354
  114.8 2.7 %copy-start = (f32[512,1024]{1,0:T(8,128)S(1)}, f32[512,1024]{1,0:T(8,128)}, u32[]{:S(2)}) copy-start(f32[512,1024]{1,0:T(8,128)} %get-tuple-element.75.refs_0_) | copy-start | bytes 6291460
  126.1 2.3 %collective-permute-start.22 = (bf16[128,2048]{1,0:T(8,128)(2,1)S(1)}, bf16[128,2048]{1,0:T(8,128)(2,1)S(1)}, u32[]{:S(2)}, u32[]{:S(2)}) collective-permute-start(bf16[128,2048]{1,0:T(8,128)(2,1)S(1)} %get-tuple-element.94), channel_id=1, source_target_pairs={{0,1},{1,0},{2,3},{3,2},{4,5},{5,4},{6,7},{7,6},{8,9},{9,8},{10,11... | collective-permute-start | bytes 1572872 | tf_op jit(solution)/shard_map/ppermute | solution.py:348
  127.8 2.1 %collective-permute-start.21 = (bf16[128,2048]{1,0:T(8,128)(2,1)S(1)}, bf16[128,2048]{1,0:T(8,128)(2,1)S(1)}, u32[]{:S(2)}, u32[]{:S(2)}) collective-permute-start(bf16[128,2048]{1,0:T(8,128)(2,1)S(1)} %get-tuple-element.92), channel_id=1, source_target_pairs={{0,1},{1,0},{2,3},{3,2},{4,5},{5,4},{6,7},{7,6},{8,9},{9,8},{10,11... | collective-permute-start | bytes 1572872 | tf_op jit(solution)/shard_map/ppermute | solution.py:348
